TPU v7x, 32 devices: a whole 2x2x4 slice. The times are simulated.
32 devices in a mesh: seq: 8 (over z, y), mp: 4 (over x, core).
Axes of the slice: x: 2, y: 2, z: 4, core: 2. Of those that a mesh axis runs over, the one named last changes fastest.
Arguments:
- queries: bfloat16 [16384, 4096], P('seq', 'mp'), may hold values from -1000 to 1000, as said below
- encoded: bfloat16 [256, 32, 896], P('seq'), may hold values from -6 to 6
- w_kv: bfloat16 [896, 2, 4096], P(None, None, 'mp'), may hold values from -0.1875 to 0.1875
- retrieved: int32 [256, 2], P('seq'), may hold values from 0 to 255, as said below
Outputs:
- attended: bfloat16 [16384, 4096], P('seq', 'mp')
Inputs may be any that keep to these rules, and one draw needn't show every extreme that they name: Decoder queries; their rows have unequal scales. `retrieved`: tile i is stored on index i // 32 of seq; of the 64 ids of one index of seq, exactly 8 name tiles stored on each index of seq; a tile may be named by many groups.
All inputs are finite; a program needn't handle non-finite values.
Results may differ from a plain program's by a relative error of at most 0.012.
Values may be sent and summed in bfloat16 or wider, within the bound.
No kernel may reach another device: no remote copies, remote signals or barrier semaphores. Data moves between devices by JAX's collectives and lax.ppermute only.
A program may use at most 128 MiB of HBM per device.

v0:
```python
import jax
import jax.numpy as jnp
from jax import lax
from jax.sharding import PartitionSpec as P

GROUP = 64
HEAD_DIM = 128


def project_rows(tiles, weights):
    count, rows, width = tiles.shape
    flat = jnp.dot(tiles.reshape(count * rows, width), weights, preferred_element_type=jnp.float32)
    return flat.astype(jnp.bfloat16).reshape(count, rows, weights.shape[1])


def ref_ranks(owners):
    length = owners.shape[-1]
    position = jnp.arange(length)
    earlier = position[None, :] < position[:, None]
    same_owner = owners[..., :, None] == owners[..., None, :]
    return jnp.sum(same_owner & earlier, axis=-1)


def body(queries, encoded, w_kv, retrieved):
    seq_count = lax.axis_size("seq")
    group_count = retrieved.shape[0]
    ref_count = 2 * group_count
    tile_count = encoded.shape[0]
    capacity = (ref_count + seq_count - 1) // seq_count
    slot_count = seq_count * capacity
    tile_ids = retrieved.reshape(ref_count)
    owners = tile_ids // tile_count
    slot_ids = owners * capacity + ref_ranks(owners)
    wanted = jnp.arange(slot_count, dtype=jnp.int32)[:, None] == slot_ids[None, :]
    request = jnp.sum(jnp.where(wanted, (tile_ids % tile_count)[None, :], 0), axis=1)
    asked = lax.all_to_all(request, "seq", split_axis=0, concat_axis=0, tiled=True)
    outgoing = jnp.take(encoded, asked, axis=0)
    weights = w_kv.reshape(w_kv.shape[0], -1)
    key_value = project_rows(
        jnp.take(
            lax.all_to_all(outgoing, "seq", split_axis=0, concat_axis=0, tiled=True),
            slot_ids,
            axis=0,
        ),
        weights,
    )
    local_width = queries.shape[1]
    heads_here = local_width // HEAD_DIM
    paired = key_value.reshape(group_count, 2 * key_value.shape[1], 2, heads_here, HEAD_DIM)
    key_rows = paired[:, :, 0]
    value_rows = paired[:, :, 1]
    query_heads = queries.reshape(group_count, GROUP, heads_here, HEAD_DIM)
    scores = jnp.einsum(
        "cthe,cshe->chts", query_heads, key_rows, preferred_element_type=jnp.float32
    ) * HEAD_DIM ** (-0.5)
    top = jnp.max(scores, axis=-1, keepdims=True)
    expd = jnp.exp(scores - top)
    probs = (expd / jnp.sum(expd, axis=-1, keepdims=True)).astype(jnp.bfloat16)
    mixed = jnp.einsum("chts,cshe->cthe", probs, value_rows, preferred_element_type=jnp.float32)
    return mixed.astype(jnp.bfloat16).reshape(group_count * GROUP, local_width)


def solution(mesh):
    in_specs = (P("seq", "mp"), P("seq", None, None), P(None, None, "mp"), P("seq", None))
    out_specs = P("seq", "mp")
    return jax.shard_map(body, mesh=mesh, in_specs=in_specs, out_specs=out_specs, check_vma=False)
```

profile of v0, /device:TPU:0, one launch (start us, length us, event | category | flops | bytes accessed | tf_op | source)
XLA Modules:
  0.0 167.9 jit_solution(2379053309135739307)
XLA Ops:
  0.0 0.0 copy-start
  0.0 0.9 copy.26
  0.9 0.1 reshape.252
  1.0 0.2 convert_reduce_fusion
  1.2 0.1 select_reduce_fusion
  1.3 0.1 all_to_all.13
  1.4 13.5 %all_to_all.20 = s32[8,8,1]{1,2,0:T(1,128)S(1)} all-to-all(s32[8,8,1]{1,2,0:T(1,128)S(1)} %bitcast.57), channel_id=1, replica_groups=mesh['seq'=8,'mp'=4] {'seq'}, dimensions={0} | all-to-all | bytes 512 | tf_op jit(solution)/shard_map/all_to_all | solution.py:36
  15.0 0.1 all_to_all.16
  15.1 0.5 broadcast.280
  15.6 0.7 reduce.5
  16.2 0.1 all_to_all.15
  16.3 2.8 %gather_fusion = bf16[64,32,896]{2,1,0:T(8,128)(2,1)} fusion(bf16[32,32,896]{2,1,0:T(8,128)(2,1)S(1)} %copy-done, s32[1024]{0:T(1024)S(1)} %pad_clamp_fusion.1), kind=kCustom, calls=%fused_computation | custom fusion | bytes 7340288 | tf_op jit(solution)/shard_map/jit(_take)/gather | solution.py:37
  19.1 4.3 %broadcast_select_fusion = bf16[64,32,896]{2,1,0:T(8,128)(2,1)} fusion(bf16[64,32,896]{2,1,0:T(8,128)(2,1)} %gather_fusion, pred[64]{0:T(512)(128)(4,1)S(1)} %compare_and_fusion), kind=kLoop, calls=%fused_computation.19 | loop fusion | flops 1835008 | bytes 7340096 | tf_op jit(solution)/shard_map/jit(_take)/select_n | solution.py:37
  23.4 4.5 %all-to-all-start.1 = ((bf16[64,32,896]{2,1,0:T(8,128)(2,1)}), bf16[64,32,896]{2,1,0:T(8,128)(2,1)}, u32[]{:S(2)}, u32[]{:S(2)}) async-start(bf16[64,32,896]{2,1,0:T(8,128)(2,1)} %broadcast_select_fusion), calls=%async_computation.1 | async-start | bytes 7340032 | tf_op jit(solution)/shard_map/all_to_all | solution.py:41
  27.9 0.1 reshape.253
  28.0 0.0 copy-start.3
  28.1 5.3 %copy.37 = bf16[112,8,2,1024]{3,1,2,0:T(8,128)(2,1)} copy(bf16[112,8,2,1024]{3,2,1,0:T(2,128)(2,1)} %bitcast.53) | data formatting | bytes 7340032
  33.3 3.0 %copy.39 = bf16[256,8,8,128]{3,2,1,0:T(8,128)(2,1)} copy(bf16[256,8,8,128]{3,1,2,0:T(8,128)(2,1)S(1)} %bitcast.52) | data formatting | bytes 8388608
  36.4 72.3 %all-to-all-done.1 = bf16[64,32,896]{2,1,0:T(8,128)(2,1)} async-done(((bf16[64,32,896]{2,1,0:T(8,128)(2,1)}), bf16[64,32,896]{2,1,0:T(8,128)(2,1)}, u32[]{:S(2)}, u32[]{:S(2)}) %all-to-all-start.1) | async-done | bytes 3670048 | tf_op jit(solution)/shard_map/all_to_all | solution.py:41
  108.7 4.8 %gather_fusion.1 = bf16[64,32,896]{2,1,0:T(8,128)(2,1)} fusion(bf16[64,32,896]{2,1,0:T(8,128)(2,1)} %all-to-all-done.1, s32[1024]{0:T(1024)S(1)} %pad_clamp_fusion), kind=kCustom, calls=%fused_computation.1 | custom fusion | bytes 7340288 | tf_op jit(solution)/shard_map/jit(_take)/gather | solution.py:40
  113.6 2.6 %broadcast_select_fusion.1 = bf16[64,32,896]{2,1,0:T(8,128)(2,1)S(1)} fusion(bf16[64,32,896]{2,1,0:T(8,128)(2,1)} %gather_fusion.1, pred[64]{0:T(512)(128)(4,1)S(1)} %get-tuple-element.5), kind=kLoop, calls=%fused_computation.20 | loop fusion | flops 1835008 | bytes 7340096 | tf_op jit(solution)/shard_map/jit(_take)/select_n | solution.py:40
  116.2 0.5 copy-done.4
  116.7 10.9 %convert_bitcast_fusion = bf16[256,8,16,128]{3,1,2,0:T(8,128)(2,1)} fusion(bf16[2048,896]{1,0:T(8,128)(2,1)S(1)} %bitcast.55, bf16[896,2048]{1,0:T(8,128)(2,1)S(1)} %bitcast.54), kind=kOutput, calls=%fused_computation.8 | convolution fusion | flops 7520387072 | bytes 15728640 | tf_op jit(solution)/shard_map/dot_general | solution.py:12
  127.6 9.7 %copy.38 = bf16[256,8,16,128]{3,2,1,0:T(8,128)(2,1)} copy(bf16[256,8,16,128]{3,1,2,0:T(8,128)(2,1)} %convert_bitcast_fusion) | data formatting | bytes 16777216
  137.3 5.3 %fusion.15 = (bf16[32,64,1,8,128]{4,3,2,1,0:T(8,128)(2,1)}, bf16[32,64,1,8,128]{4,3,2,1,0:T(8,128)(2,1)S(1)}) fusion(bf16[32,64,2,8,128]{4,3,2,1,0:T(8,128)(2,1)} %bitcast.49), kind=kLoop, calls=%fused_computation.48 | loop fusion | bytes 16777216 | tf_op jit(solution)/shard_map/slice | solution.py:51
  142.6 0.9 copy-done.2
  143.5 2.3 %fusion.7 = f32[32,8,64,64]{3,2,1,0:T(8,128)S(1)} fusion(bf16[32,64,1,8,128]{4,3,2,1,0:T(8,128)(2,1)S(1)} %get-tuple-element.8, bf16[32,64,8,128]{3,2,1,0:T(8,128)(2,1)S(1)} %bitcast.51), kind=kOutput, calls=%fused_computation.13 | convolution fusion | flops 268435456 | bytes 12582912 | tf_op jit(solution)/shard_map/cthe,cshe->chts/dot_general | solution.py:53
  145.8 4.5 %fusion.16 = (f32[32,8,64]{2,1,0:T(8,128)S(1)}, f32[32,8,64,64]{2,3,1,0:T(8,128)}) fusion(f32[32,8,64,64]{3,2,1,0:T(8,128)S(1)} %fusion.7), kind=kOutput, calls=%fused_computation.49 | output fusion | flops 4194367 | bytes 8454144 | tf_op jit(solution)/shard_map/sub | solution.py:57
  150.3 6.3 %convert_bitcast_fusion.1 = bf16[32,64,8,128]{3,1,2,0:T(8,128)(2,1)S(1)} fusion(f32[32,8,64,64]{2,3,1,0:T(8,128)} %get-tuple-element.12, f32[32,8,64]{2,1,0:T(8,128)S(1)} %get-tuple-element.11, bf16[32,64,1,8,128]{4,3,2,1,0:T(8,128)(2,1)} %get-tuple-element.7), kind=kOutput, calls=%fused_computation.16 | convolution fusion | flops 272629760 | bytes 12648448 | tf_op jit(solution)/shard_map/chts,cshe->cthe/dot_general | solution.py:59
  156.6 8.1 %copy.33 = bf16[32,64,8,128]{3,2,1,0:T(8,128)(2,1)S(1)} copy(bf16[32,64,8,128]{3,1,2,0:T(8,128)(2,1)S(1)} %convert_bitcast_fusion.1) | data formatting | bytes 8388608 | tf_op jit(solution)/shard_map/convert_element_type | solution.py:60
  164.8 0.0 copy-start.1
  164.8 3.1 %copy.50 = bf16[256,8,8,128]{3,1,2,0:T(8,128)(2,1)} copy(bf16[256,8,8,128]{3,2,1,0:T(8,128)(2,1)S(1)} %bitcast.50) | data formatting | bytes 8388608
  (12 shorter events, 0.1 us)
Async XLA Ops:
  0.0 16.3 %copy-start = (bf16[32,32,896]{2,1,0:T(8,128)(2,1)S(1)}, bf16[32,32,896]{2,1,0:T(8,128)(2,1)}, u32[]{:S(2)}) copy-start(bf16[32,32,896]{2,1,0:T(8,128)(2,1)} %param.5) | copy-start | bytes 5505028
  23.4 85.3 %all-to-all-start.1 = ((bf16[64,32,896]{2,1,0:T(8,128)(2,1)}), bf16[64,32,896]{2,1,0:T(8,128)(2,1)}, u32[]{:S(2)}, u32[]{:S(2)}) async-start(bf16[64,32,896]{2,1,0:T(8,128)(2,1)} %broadcast_select_fusion), calls=%async_computation.1 | async-start | bytes 7340032 | tf_op jit(solution)/shard_map/all_to_all | solution.py:41
  28.0 5.3 %copy-start.3 = (bf16[2048,1024]{1,0:T(8,128)(2,1)S(1)}, bf16[2048,1024]{1,0:T(8,128)(2,1)}, u32[]{:S(2)}) copy-start(bf16[2048,1024]{1,0:T(8,128)(2,1)} %param.4) | copy-start | bytes 12582916
  113.5 3.1 %copy-start.4 = (bf16[112,8,2,1024]{3,1,2,0:T(8,128)(2,1)S(1)}, bf16[112,8,2,1024]{3,1,2,0:T(8,128)(2,1)}, u32[]{:S(2)}) copy-start(bf16[112,8,2,1024]{3,1,2,0:T(8,128)(2,1)} %copy.37) | copy-start | bytes 11010052
  137.3 6.2 %copy-start.2 = (bf16[256,8,8,128]{3,2,1,0:T(8,128)(2,1)S(1)}, bf16[256,8,8,128]{3,2,1,0:T(8,128)(2,1)}, u32[]{:S(2)}) copy-start(bf16[256,8,8,128]{3,2,1,0:T(8,128)(2,1)} %copy.39) | copy-start | bytes 12582916
  164.8 3.2 %copy-start.1 = (bf16[32,32,896]{2,1,0:T(8,128)(2,1)S(1)}, bf16[32,32,896]{2,1,0:T(8,128)(2,1)}, u32[]{:S(2)}) copy-start(bf16[32,32,896]{2,1,0:T(8,128)(2,1)} %param.5) | copy-start | bytes 5505028
where the time goes:
time: 168 us
  waiting for transfers between devices  72.3 us (43%)
  local copies, waits for them, and re-layouts  45.5 us (27%)
  matrix products  19.5 us (12%)
  blocking collectives  13.5 us (8%)
  other arithmetic  12.4 us (7%)
  starting transfers between devices  4.5 us (3%)
    all_to_all x1, waiting for transfers between devices, body(): lax.all_to_all(outgoing, 'seq', split_axis=0, concat_axis=0, tiled=True)  72.3 us
    unnamed x15, local copies, waits for them, and re-layouts  23.5 us
    all_to_all x1, blocking collectives, body(): lax.all_to_all(request, 'seq', split_axis=0, concat_axis=0, tiled=True)  13.5 us
    dot_general x1, matrix products, project_rows(): jnp.dot(tiles.reshape(count * rows, width), weights, preferred_element_ty...  10.9 us
    convert_element_type x1, local copies, waits for them, and re-layouts, body(): return mixed.astype(jnp.bfloat16).reshape(group_count * GROUP, local_width)  8.14 us
    dot_general x1, matrix products, body(): jnp.einsum('chts,cshe->cthe', probs, value_rows, preferred_element_type=j...  6.32 us
    slice x1, local copies, waits for them, and re-layouts, body(): value_rows = paired[:, :, 1]  5.3 us
    gather x1, local copies, waits for them, and re-layouts, body(): jnp.take(lax.all_to_all(outgoing, 'seq', split_axis=0, concat_axis=0, til...  4.82 us
  transfers between devices with their start and end apart: 1, of which 1 were waited for; matrix products, arithmetic and copies ran while one was open for 5% of the time, Pallas kernels for 0%

commit v1 on v0

v1 whole, which is shorter than its diff:
```python
import functools

import jax
import jax.numpy as jnp
from jax import lax
from jax.experimental import pallas as pl
from jax.experimental.pallas import tpu as pltpu
from jax.sharding import PartitionSpec as P

GROUP = 64
HEAD_DIM = 128
MIB = 1024 * 1024


def hits_of(ids_ref, table_ref, owner, tile_count, ref_count):
    def step(i, count):
        tile_id = ids_ref[lax.rem(i, 2), lax.div(i, 2)]
        table_ref[count] = lax.rem(tile_id, tile_count)
        return count + (lax.div(tile_id, tile_count) == owner).astype(jnp.int32)

    lax.fori_loop(0, ref_count, step, jnp.int32(0), unroll=8)


def pick_kernel(rows, split, capacity, ids_ref, stored_ref, out_ref, table_ref, sem):
    seq_at, mp_at = lax.axis_index("seq"), lax.axis_index("mp")
    tile_count = stored_ref.shape[0]
    hits_of(ids_ref, table_ref, seq_at, tile_count, 2 * ids_ref.shape[1])
    first = pl.multiple_of((mp_at // 2) * rows, rows) if split else 0
    copies = []
    for j in range(capacity):
        source = stored_ref.at[table_ref[j], pl.ds(first, rows), :]
        copies.append(pltpu.make_async_copy(source, out_ref.at[j], sem.at[j]))
        copies[-1].start()
    for copy in copies:
        copy.wait()


def pick(ids, stored, rows, capacity):
    split = rows < stored.shape[1]
    return pl.pallas_call(
        functools.partial(pick_kernel, rows, split, capacity),
        out_shape=jax.ShapeDtypeStruct((capacity, rows, stored.shape[2]), stored.dtype),
        in_specs=[pl.BlockSpec(memory_space=pltpu.SMEM), pl.BlockSpec(memory_space=pl.ANY)],
        out_specs=pl.BlockSpec(memory_space=pl.ANY),
        scratch_shapes=[pltpu.SMEM((2 * ids.shape[1] + 1,), jnp.int32), pltpu.SemaphoreType.DMA((capacity,))],
        name="pick",
    )(ids, stored)


def slots_kernel(tile_count, seq_count, capacity, ids_ref, slots_ref, rank_ref):
    seq_at, core = lax.axis_index("seq"), lax.rem(lax.axis_index("mp"), 2)
    for owner in range(seq_count):
        rank_ref[owner] = 0

    def step(i, carry):
        owner = lax.div(ids_ref[lax.rem(i, 2), lax.div(i, 2)], tile_count)
        rank = rank_ref[owner]
        rank_ref[owner] = rank + 1
        apart = owner ^ seq_at
        part, side = lax.div(apart, 2), lax.rem(apart, 2)
        side = jnp.where(part == 0, side, side ^ core)
        slots_ref[i] = (part * 2 + side) * capacity + rank
        return carry

    lax.fori_loop(0, 2 * ids_ref.shape[1], step, 0)


def slots_of(ids, tile_count, seq_count, capacity):
    return pl.pallas_call(
        functools.partial(slots_kernel, tile_count, seq_count, capacity),
        out_shape=jax.ShapeDtypeStruct((2 * ids.shape[1],), jnp.int32),
        in_specs=[pl.BlockSpec(memory_space=pltpu.SMEM)],
        out_specs=pl.BlockSpec(memory_space=pltpu.SMEM),
        scratch_shapes=[pltpu.SMEM((seq_count,), jnp.int32)],
        name="slots",
    )(ids)


def project_kernel(count, *refs):
    pieces, weights_ref, out_ref = refs[:count], refs[count], refs[-1]
    if count == 2:
        for side, piece in enumerate(pieces):
            tiles, rows, width = piece.shape
            flat = jnp.dot(piece[...].reshape(tiles * rows, width), weights_ref[...], preferred_element_type=jnp.float32)
            out_ref[pl.ds(side * tiles, tiles)] = flat.astype(jnp.bfloat16).reshape(tiles, rows, -1)
    else:
        for at, piece in enumerate(pieces):
            side, half = at // 2, at % 2
            tiles, rows, width = piece.shape
            flat = jnp.dot(piece[...].reshape(tiles * rows, width), weights_ref[...], preferred_element_type=jnp.float32)
            out_ref[pl.ds(side * tiles, tiles), pl.ds(half * rows, rows)] = flat.astype(jnp.bfloat16).reshape(tiles, rows, -1)


def project(pieces, weights, held, part, shape):
    count = len(pieces)
    width, columns = weights.shape
    step = min(columns, 512)
    tiles = 2 * pieces[0].shape[0]
    rows = shape[1]
    operands = [*pieces, weights]
    in_specs = [pl.BlockSpec(p.shape, lambda n: (0, 0, 0)) for p in pieces]
    in_specs.append(pl.BlockSpec((width, step), lambda n: (0, n)))
    aliases = {}
    if held is not None:
        operands.append(held)
        in_specs.append(pl.BlockSpec(memory_space=pl.ANY))
        aliases = {count + 1: 0}
    flops = 2 * tiles * rows * width * columns
    return pl.pallas_call(
        functools.partial(project_kernel, count),
        grid=(columns // step,),
        out_shape=jax.ShapeDtypeStruct(shape, jnp.bfloat16),
        in_specs=in_specs,
        out_specs=pl.BlockSpec((tiles, rows, step), lambda n: (part, 0, n)),
        input_output_aliases=aliases,
        compiler_params=pltpu.CompilerParams(vmem_limit_bytes=32 * MIB),
        cost_estimate=pl.CostEstimate(flops=flops, bytes_accessed=8 * MIB, transcendentals=0),
        name="project",
    )(*operands)


def attend_kernel(heads, slots_ref, queries_ref, first_ref, second_ref, out_ref):
    width = heads * HEAD_DIM
    scale = HEAD_DIM ** (-0.5)
    for h in range(heads):
        key_at, value_at = pl.ds(h * HEAD_DIM, HEAD_DIM), pl.ds(width + h * HEAD_DIM, HEAD_DIM)
        keys = jnp.concatenate([first_ref[0, :, key_at], second_ref[0, :, key_at]], axis=0)
        values = jnp.concatenate([first_ref[0, :, value_at], second_ref[0, :, value_at]], axis=0)
        scores = lax.dot_general(
            queries_ref[:, key_at], keys, (((1,), (1,)), ((), ())), preferred_element_type=jnp.float32
        )
        top = jnp.max(scores, axis=-1, keepdims=True)
        expd = jnp.exp((scores - top) * scale)
        probs = (expd / jnp.sum(expd, axis=-1, keepdims=True)).astype(jnp.bfloat16)
        mixed = jnp.dot(probs, values, preferred_element_type=jnp.float32)
        out_ref[:, key_at] = mixed.astype(jnp.bfloat16)


def attend(queries, held, slots, heads):
    groups = queries.shape[0] // GROUP
    tile = (1, held.shape[1], held.shape[2])
    block = (GROUP, queries.shape[1])
    return pl.pallas_call(
        functools.partial(attend_kernel, heads),
        out_shape=jax.ShapeDtypeStruct(queries.shape, jnp.bfloat16),
        grid_spec=pltpu.PrefetchScalarGridSpec(
            num_scalar_prefetch=1,
            grid=(groups,),
            in_specs=[
                pl.BlockSpec(block, lambda c, s: (c, 0)),
                pl.BlockSpec(tile, lambda c, s: (s[2 * c], 0, 0)),
                pl.BlockSpec(tile, lambda c, s: (s[2 * c + 1], 0, 0)),
            ],
            out_specs=pl.BlockSpec(block, lambda c, s: (c, 0)),
        ),
        compiler_params=pltpu.CompilerParams(vmem_limit_bytes=32 * MIB),
        cost_estimate=pl.CostEstimate(flops=10**9, bytes_accessed=16 * MIB, transcendentals=10**6),
        name="attend",
    )(slots, queries, held, held)


def ref_ranks(owners):
    length = owners.shape[-1]
    position = jnp.arange(length)
    earlier = position[None, :] < position[:, None]
    same_owner = owners[..., :, None] == owners[..., None, :]
    return jnp.sum(same_owner & earlier, axis=-1)


def plain_body(queries, encoded, w_kv, retrieved):
    seq_count = lax.axis_size("seq")
    ref_count = 2 * retrieved.shape[0]
    tile_count = encoded.shape[0]
    capacity = (ref_count + seq_count - 1) // seq_count
    tile_ids = retrieved.reshape(ref_count)
    owners = tile_ids // tile_count
    slot_ids = owners * capacity + ref_ranks(owners)
    wanted = jnp.arange(seq_count * capacity, dtype=jnp.int32)[:, None] == slot_ids[None, :]
    request = jnp.sum(jnp.where(wanted, (tile_ids % tile_count)[None, :], 0), axis=1)
    asked = lax.all_to_all(request, "seq", split_axis=0, concat_axis=0, tiled=True)
    outgoing = jnp.take(encoded, asked, axis=0, mode="clip")
    tiles = lax.all_to_all(outgoing, "seq", split_axis=0, concat_axis=0, tiled=True)
    weights = w_kv.reshape(w_kv.shape[0], -1)
    flat = jnp.dot(tiles.reshape(-1, tiles.shape[2]), weights, preferred_element_type=jnp.float32)
    held = flat.astype(jnp.bfloat16).reshape(tiles.shape[0], tiles.shape[1], -1)
    return attend(queries, held, slot_ids, queries.shape[1] // HEAD_DIM)


def split_body(queries, encoded, w_kv, retrieved):
    seq_count, mp_count = lax.axis_size("seq"), lax.axis_size("mp")
    ref_count = 2 * retrieved.shape[0]
    tile_count, rows, width = encoded.shape
    capacity = ref_count // seq_count
    parts = seq_count // 2
    both = ("seq", "mp")

    def joint(move):
        return [(s * mp_count + m, move(s, m)) for s in range(seq_count) for m in range(mp_count)]

    def across(value, part):
        if part == 0:
            return lax.ppermute(value, "seq", [(s, s ^ 1) for s in range(seq_count)])
        return lax.ppermute(value, both, joint(lambda s, m: (s ^ (2 * part) ^ (m % 2)) * mp_count + m))

    def over_mp(value, flip):
        return lax.ppermute(value, "mp", [(m, m ^ flip) for m in range(mp_count)])

    ids = retrieved.T
    order = [p for p in range(parts - 1, 0, -1)] + [0]
    order = sorted(range(parts), key=lambda p: (-(p // 2), p))
    weights = w_kv.reshape(width, -1)
    slots = slots_of(ids, tile_count, seq_count, capacity)
    asked = {p: across(ids, p) for p in order}
    sent = {p: across(pick(asked[p], encoded, rows if p == 0 else rows // 2, capacity), p) for p in order}
    shape = (ref_count, rows, weights.shape[1])
    own = pick(ids, encoded, rows, capacity)
    held = None
    for p in [0, 1] + [q for q in order if q > 1]:
        if p == 0:
            pieces = [own, sent[p]]
        else:
            mine = sent[p]
            theirs = over_mp(mine, 2)
            pieces = [mine, theirs, over_mp(mine, 1), over_mp(theirs, 1)]
        held = project(pieces, weights, held, p, shape)
    return attend(queries, held, slots, queries.shape[1] // HEAD_DIM)


def body(queries, encoded, w_kv, retrieved):
    seq_count, mp_count = lax.axis_size("seq"), lax.axis_size("mp")
    ref_count = 2 * retrieved.shape[0]
    few = seq_count in (2, 4, 8) and mp_count == 4
    even = ref_count % seq_count == 0 and encoded.shape[1] % 32 == 0
    if few and even:
        return split_body(queries, encoded, w_kv, retrieved)
    return plain_body(queries, encoded, w_kv, retrieved)


def solution(mesh):
    in_specs = (P("seq", "mp"), P("seq", None, None), P(None, None, "mp"), P("seq", None))
    out_specs = P("seq", "mp")
    return jax.shard_map(body, mesh=mesh, in_specs=in_specs, out_specs=out_specs, check_vma=False)
```

time: 168 us -> 200 us (1.19)
  Pallas kernels: 0 us -> 159 us
  waiting for transfers between devices: 72.3 us -> 12.3 us
  local copies, waits for them, and re-layouts: 45.5 us -> 5.52 us
  matrix products: 19.5 us -> 0 us
  starting transfers between devices: 4.5 us -> 21.2 us
  blocking collectives: 13.5 us -> 0 us
  other arithmetic: 12.4 us -> 0 us
    pallas_call x0 -> x11, Pallas kernels: none -> 159 us  [the longest x1 82.4 us: attend(): pl.pallas_call(functools.partial(attend_kernel, heads), out_shape=jax.Sha...]
    all_to_all x1 -> x0, waiting for transfers between devices: 72.3 us -> none  [body(): lax.all_to_all(outgoing, 'seq', split_axis=0, concat_axis=0, tiled=True)]
    ppermute x0 -> x17, starting transfers between devices: none -> 21.2 us  [the longest x6 13.7 us: across(): lax.ppermute(value, both, joint(lambda s, m: (s ^ 2 * part ^ m % 2) * mp_...]
    dot_general x3 -> x0, matrix products: 19.5 us -> none  [the longest x1 10.9 us: project_rows(): jnp.dot(tiles.reshape(count * rows, width), weights, preferred_element_ty...]
    unnamed x15 -> x17, local copies, waits for them, and re-layouts: 23.5 us -> 5.52 us
    all_to_all x1 -> x0, blocking collectives: 13.5 us -> none  [body(): lax.all_to_all(request, 'seq', split_axis=0, concat_axis=0, tiled=True)]
    ppermute x0 -> x17, waiting for transfers between devices: none -> 12.3 us  [the longest x6 11 us: across(): lax.ppermute(value, both, joint(lambda s, m: (s ^ 2 * part ^ m % 2) * mp_...]
    convert_element_type x1 -> x0, local copies, waits for them, and re-layouts: 8.14 us -> none  [body(): return mixed.astype(jnp.bfloat16).reshape(group_count * GROUP, local_width)]
  transfers between devices with their start and end apart: 1 -> 17, of which waited for: 1 -> 4; matrix products, arithmetic and copies ran while one was open for 5% -> 2% of each run, Pallas kernels for 0% -> 32%
where the time goes in v1:
time: 200 us; the launch traced here: 198 us
  Pallas kernels  159 us (80%)
  starting transfers between devices  21.2 us (11%)
  waiting for transfers between devices  12.3 us (6%)
  local copies, waits for them, and re-layouts  5.52 us (3%)
    pallas_call x1, Pallas kernels, attend(): pl.pallas_call(functools.partial(attend_kernel, heads), out_shape=jax.Sha...  82.4 us
    pallas_call x5, Pallas kernels, pick(): pl.pallas_call(functools.partial(pick_kernel, rows, split, capacity), out...  60.8 us
    ppermute x6, starting transfers between devices, across(): lax.ppermute(value, both, joint(lambda s, m: (s ^ 2 * part ^ m % 2) * mp_...  13.7 us
    pallas_call x4, Pallas kernels, project(): pl.pallas_call(functools.partial(project_kernel, count), grid=(columns //...  13.2 us
    ppermute x6, waiting for transfers between devices, across(): lax.ppermute(value, both, joint(lambda s, m: (s ^ 2 * part ^ m % 2) * mp_...  11 us
    unnamed x17, local copies, waits for them, and re-layouts  5.52 us
    ppermute x9, starting transfers between devices, over_mp(): return lax.ppermute(value, 'mp', [(m, m ^ flip) for m in range(mp_count)])  4.76 us
  transfers between devices with their start and end apart: 17, of which 4 were waited for; matrix products, arithmetic and copies ran while one was open for 2% of the time, Pallas kernels for 32%

profile of v1, /device:TPU:0, one launch (start us, length us, event | category | flops | bytes accessed | tf_op | source)
XLA Modules:
  0.0 198.2 jit_solution(18101371546992753755)
XLA Ops:
  0.0 3.0 %collective-permute-start.10 = (s32[2,32]{1,0:T(2,128)}, s32[2,32]{1,0:T(2,128)S(1)}, u32[]{:S(2)}, u32[]{:S(2)}) collective-permute-start(s32[2,32]{1,0:T(2,128)} %bitcast.8), channel_id=1, source_target_pairs={{0,8},{1,13},{2,10},{3,15},{4,12},{5,9},{6,14},{7,11},{8,0},{9,5},... | collective-permute-start | bytes 776 | tf_op jit(solution)/shard_map/ppermute | solution.py:203
  3.0 1.8 collective-permute-done.10.ids_ref
  4.9 0.6 copy-done.4
  5.4 9.4 %pick.7 = bf16[8,16,896]{2,1,0:T(8,128)(2,1)} custom-call(s32[2,32]{1,0:T(2,128)} %copy-done.4, bf16[32,32,896]{2,1,0:T(8,128)(2,1)} %stored_ref.9), custom_call_target="tpu_custom_call" | custom-call | tf_op jit(solution)/shard_map/pick/pallas_call | solution.py:40
  14.8 2.0 %collective-permute-start.11 = (bf16[8,16,896]{2,1,0:T(8,128)(2,1)}, bf16[8,16,896]{2,1,0:T(8,128)(2,1)S(1)}, u32[]{:S(2)}, u32[]{:S(2)}) collective-permute-start(bf16[8,16,896]{2,1,0:T(8,128)(2,1)} %pick.7), channel_id=1, source_target_pairs={{0,8},{1,13},{2,10},{3,15},{4,12},{5,9},{6,14},{7,11},{8,0},{9,5},... | collective-permute-start | bytes 688136 | tf_op jit(solution)/shard_map/ppermute | solution.py:203
  16.8 1.5 collective-permute-start.15
  18.4 2.6 %collective-permute-start.5 = (s32[2,32]{1,0:T(2,128)}, s32[2,32]{1,0:T(2,128)S(1)}, u32[]{:S(2)}, u32[]{:S(2)}) collective-permute-start(s32[2,32]{1,0:T(2,128)} %bitcast.10), channel_id=1, source_target_pairs={{0,16},{1,21},{2,18},{3,23},{4,20},{5,17},{6,22},{7,19},{8,24},{9,... | collective-permute-start | bytes 776 | tf_op jit(solution)/shard_map/ppermute | solution.py:203
  20.9 0.6 copy-done.7
  21.5 16.3 %pick.9 = bf16[8,32,896]{2,1,0:T(8,128)(2,1)} custom-call(s32[2,32]{1,0:T(2,128)} %copy-done.7, bf16[32,32,896]{2,1,0:T(8,128)(2,1)} %stored_ref.9), custom_call_target="tpu_custom_call" | custom-call | tf_op jit(solution)/shard_map/pick/pallas_call | solution.py:40
  37.8 1.3 collective-permute-start.16
  39.1 0.6 copy-done.3
  39.7 9.4 %pick.6 = bf16[8,16,896]{2,1,0:T(8,128)(2,1)} custom-call(s32[2,32]{1,0:T(2,128)} %copy-done.3, bf16[32,32,896]{2,1,0:T(8,128)(2,1)} %stored_ref.9), custom_call_target="tpu_custom_call" | custom-call | tf_op jit(solution)/shard_map/pick/pallas_call | solution.py:40
  49.1 2.7 %collective-permute-start.6 = (bf16[8,16,896]{2,1,0:T(8,128)(2,1)}, bf16[8,16,896]{2,1,0:T(8,128)(2,1)S(1)}, u32[]{:S(2)}, u32[]{:S(2)}) collective-permute-start(bf16[8,16,896]{2,1,0:T(8,128)(2,1)} %pick.6), channel_id=1, source_target_pairs={{0,16},{1,21},{2,18},{3,23},{4,20},{5,17},{6,22},{7,19},{8,24},{9,... | collective-permute-start | bytes 688136 | tf_op jit(solution)/shard_map/ppermute | solution.py:203
  51.9 5.4 %collective-permute-done.ids_ref = s32[2,32]{1,0:T(2,128)S(1)} collective-permute-done((s32[2,32]{1,0:T(2,128)S(1)}, s32[2,32]{1,0:T(2,128)S(1)}, u32[]{:S(2)}, u32[]{:S(2)}) %collective-permute-start) | collective-permute-done | bytes 288 | tf_op jit(solution)/shard_map/ppermute | solution.py:203
  57.4 0.5 copy-done.5
  57.9 9.4 %pick.5 = bf16[8,16,896]{2,1,0:T(8,128)(2,1)} custom-call(s32[2,32]{1,0:T(2,128)} %copy-done.5, bf16[32,32,896]{2,1,0:T(8,128)(2,1)} %stored_ref.9), custom_call_target="tpu_custom_call" | custom-call | tf_op jit(solution)/shard_map/pick/pallas_call | solution.py:40
  67.3 3.2 %collective-permute-start.1 = (bf16[8,16,896]{2,1,0:T(8,128)(2,1)}, bf16[8,16,896]{2,1,0:T(8,128)(2,1)S(1)}, u32[]{:S(2)}, u32[]{:S(2)}) collective-permute-start(bf16[8,16,896]{2,1,0:T(8,128)(2,1)} %pick.5), channel_id=1, source_target_pairs={{0,24},{1,29},{2,26},{3,31},{4,28},{5,25},{6,30},{7,27},{8,16},{9,... | collective-permute-start | bytes 688136 | tf_op jit(solution)/shard_map/ppermute | solution.py:203
  70.5 1.5 collective-permute-start.12
  72.0 0.5 collective-permute-start.7
  72.6 3.7 %collective-permute-done.1.refs_0_ = bf16[8,16,896]{2,1,0:T(8,128)(2,1)S(1)} collective-permute-done((bf16[8,16,896]{2,1,0:T(8,128)(2,1)}, bf16[8,16,896]{2,1,0:T(8,128)(2,1)S(1)}, u32[]{:S(2)}, u32[]{:S(2)}) %collective-permute-start.1) | collective-permute-done | bytes 229408 | tf_op jit(solution)/shard_map/ppermute | solution.py:203
  76.3 1.5 collective-permute-start.2
  77.8 1.3 collective-permute-done.12.refs_1_
  79.1 16.3 %pick.8.refs_0_ = bf16[8,32,896]{2,1,0:T(8,128)(2,1)} custom-call(s32[2,32]{1,0:T(2,128)} %bitcast.11, bf16[32,32,896]{2,1,0:T(8,128)(2,1)} %stored_ref.9), custom_call_target="tpu_custom_call" | custom-call | tf_op jit(solution)/shard_map/pick/pallas_call | solution.py:40
  95.4 2.6 %slots.1.slots_ref = s32[64]{0:T(128)} custom-call(s32[2,32]{1,0:T(2,128)} %bitcast.12), custom_call_target="tpu_custom_call" | custom-call | tf_op jit(solution)/shard_map/slots/pallas_call | solution.py:69
  98.0 3.3 %copy.8 = bf16[112,8,2,1024]{3,1,2,0:T(8,128)(2,1)S(1)} copy(bf16[112,8,2,1024]{3,2,1,0:T(2,128)(2,1)} %bitcast.7) | data formatting | bytes 7340032
  101.3 0.6 collective-permute-start.8
  102.0 3.3 %project.4.refs_5_ = bf16[64,32,2048]{2,1,0:T(8,128)(2,1)S(1)} custom-call(bf16[8,32,896]{2,1,0:T(8,128)(2,1)S(1)} %copy-done.1, bf16[8,32,896]{2,1,0:T(8,128)(2,1)S(1)} %collective-permute-done.16.refs_1_, bf16[896,2048]{1,0:T(8,128)(2,1)S(1)} %bitcast.3), custom_call_target="tpu_custom_call" | custom-call | flops 1879048192 | bytes 8388608 | tf_op jit(solution)/shard_map/project/pallas_call | solution.py:109
  105.2 0.5 collective-permute-start.3
  105.8 3.3 %project.5.refs_5_ = bf16[64,32,2048]{2,1,0:T(8,128)(2,1)S(1)} custom-call(bf16[8,16,896]{2,1,0:T(8,128)(2,1)S(1)} %collective-permute-done.11.refs_0_, bf16[8,16,896]{2,1,0:T(8,128)(2,1)S(1)} %collective-permute-done.12.refs_1_, bf16[8,16,896]{2,1,0:T(8,128)(2,1)S(1)} %collective-permute-done.13.refs_2_, ...), custom_call_target="tpu_custom_call", output_to_operand_aliasing={{}: (5, {})} | custom-call | flops 1879048192 | bytes 8388608 | tf_op jit(solution)/shard_map/project/pallas_call | solution.py:109
  109.2 3.3 %project.6.refs_5_ = bf16[64,32,2048]{2,1,0:T(8,128)(2,1)S(1)} custom-call(bf16[8,16,896]{2,1,0:T(8,128)(2,1)S(1)} %collective-permute-done.6.refs_0_, bf16[8,16,896]{2,1,0:T(8,128)(2,1)S(1)} %collective-permute-done.7.refs_1_, bf16[8,16,896]{2,1,0:T(8,128)(2,1)S(1)} %collective-permute-done.8.refs_2_, ...), custom_call_target="tpu_custom_call", output_to_operand_aliasing={{}: (5, {})} | custom-call | flops 1879048192 | bytes 8388608 | tf_op jit(solution)/shard_map/project/pallas_call | solution.py:109
  112.5 3.3 %project.7.first_ref.second_ref = bf16[64,32,2048]{2,1,0:T(8,128)(2,1)S(1)} custom-call(bf16[8,16,896]{2,1,0:T(8,128)(2,1)S(1)} %collective-permute-done.1.refs_0_, bf16[8,16,896]{2,1,0:T(8,128)(2,1)S(1)} %collective-permute-done.2.refs_1_, bf16[8,16,896]{2,1,0:T(8,128)(2,1)S(1)} %collective-permute-done.3.refs_2_, ...), custom_call_target="tpu_custom_call", output_to_operand_aliasing={{}: (5, {})} | custom-call | flops 1879048192 | bytes 8388608 | tf_op jit(solution)/shard_map/project/pallas_call | solution.py:109
  115.9 82.4 %attend.1 = bf16[2048,1024]{1,0:T(8,128)(2,1)} custom-call(s32[64]{0:T(128)S(1)} %copy-done.2, bf16[2048,1024]{1,0:T(8,128)(2,1)S(1)} %copy-done, bf16[64,32,2048]{2,1,0:T(8,128)(2,1)S(1)} %project.7.first_ref.second_ref, bf16[64,32,2048]{2,1,0:T(8,128)(2,1)S(1)} %project.7.first_ref.second_ref), custom_call_target="tpu_custom_call" | custom-call | flops 1000000000 | bytes 16777216 | tf_op jit(solution)/shard_map/attend/pallas_call | solution.py:143
  (30 shorter events, 0.5 us)
Async XLA Ops:
  0.0 51.7 %copy-start.6 = (s32[32,2]{0,1:T(2,128)S(1)}, s32[32,2]{0,1:T(2,128)}, u32[]{:S(2)}) copy-start(s32[32,2]{0,1:T(2,128)} %param.7) | copy-start | bytes 772
  0.0 4.9 %collective-permute-start.10 = (s32[2,32]{1,0:T(2,128)}, s32[2,32]{1,0:T(2,128)S(1)}, u32[]{:S(2)}, u32[]{:S(2)}) collective-permute-start(s32[2,32]{1,0:T(2,128)} %bitcast.8), channel_id=1, source_target_pairs={{0,8},{1,13},{2,10},{3,15},{4,12},{5,9},{6,14},{7,11},{8,0},{9,5},... | collective-permute-start | bytes 776 | tf_op jit(solution)/shard_map/ppermute | solution.py:203
  4.9 0.6 copy-start.4
  14.8 55.7 %collective-permute-start.11 = (bf16[8,16,896]{2,1,0:T(8,128)(2,1)}, bf16[8,16,896]{2,1,0:T(8,128)(2,1)S(1)}, u32[]{:S(2)}, u32[]{:S(2)}) collective-permute-start(bf16[8,16,896]{2,1,0:T(8,128)(2,1)} %pick.7), channel_id=1, source_target_pairs={{0,8},{1,13},{2,10},{3,15},{4,12},{5,9},{6,14},{7,11},{8,0},{9,5},... | collective-permute-start | bytes 688136 | tf_op jit(solution)/shard_map/ppermute | solution.py:203
  16.8 4.1 %collective-permute-start.15 = (s32[2,32]{1,0:T(2,128)}, s32[2,32]{1,0:T(2,128)S(1)}, u32[]{:S(2)}, u32[]{:S(2)}) collective-permute-start(s32[2,32]{1,0:T(2,128)} %bitcast.9), channel_id=1, source_target_pairs={{0,4},{4,0},{8,12},{12,8},{16,20},{20,16},{24,28},{28,24},{1,5},{5... | collective-permute-start | bytes 776 | tf_op jit(solution)/shard_map/ppermute | solution.py:202
  18.4 20.8 %collective-permute-start.5 = (s32[2,32]{1,0:T(2,128)}, s32[2,32]{1,0:T(2,128)S(1)}, u32[]{:S(2)}, u32[]{:S(2)}) collective-permute-start(s32[2,32]{1,0:T(2,128)} %bitcast.10), channel_id=1, source_target_pairs={{0,16},{1,21},{2,18},{3,23},{4,20},{5,17},{6,22},{7,19},{8,24},{9,... | collective-permute-start | bytes 776 | tf_op jit(solution)/shard_map/ppermute | solution.py:203
  20.9 0.6 copy-start.7
  37.8 63.5 %collective-permute-start.16 = (bf16[8,32,896]{2,1,0:T(8,128)(2,1)}, bf16[8,32,896]{2,1,0:T(8,128)(2,1)S(1)}, u32[]{:S(2)}, u32[]{:S(2)}) collective-permute-start(bf16[8,32,896]{2,1,0:T(8,128)(2,1)} %pick.9), channel_id=1, source_target_pairs={{0,4},{4,0},{8,12},{12,8},{16,20},{20,16},{24,28},{28,24},{1,5},{5... | collective-permute-start | bytes 1376264 | tf_op jit(solution)/shard_map/ppermute | solution.py:202
  39.1 0.6 copy-start.3
  49.1 23.0 %collective-permute-start.6 = (bf16[8,16,896]{2,1,0:T(8,128)(2,1)}, bf16[8,16,896]{2,1,0:T(8,128)(2,1)S(1)}, u32[]{:S(2)}, u32[]{:S(2)}) collective-permute-start(bf16[8,16,896]{2,1,0:T(8,128)(2,1)} %pick.6), channel_id=1, source_target_pairs={{0,16},{1,21},{2,18},{3,23},{4,20},{5,17},{6,22},{7,19},{8,24},{9,... | collective-permute-start | bytes 688136 | tf_op jit(solution)/shard_map/ppermute | solution.py:203
  51.7 5.7 %collective-permute-start = (s32[2,32]{1,0:T(2,128)S(1)}, s32[2,32]{1,0:T(2,128)S(1)}, u32[]{:S(2)}, u32[]{:S(2)}) collective-permute-start(s32[2,32]{1,0:T(2,128)S(1)} %bitcast.13), channel_id=1, source_target_pairs={{0,24},{1,29},{2,26},{3,31},{4,28},{5,25},{6,30},{7,27},{8,16},{9,... | collective-permute-start | bytes 776 | tf_op jit(solution)/shard_map/ppermute | solution.py:203
  57.4 0.5 copy-start.5
  67.3 9.0 %collective-permute-start.1 = (bf16[8,16,896]{2,1,0:T(8,128)(2,1)}, bf16[8,16,896]{2,1,0:T(8,128)(2,1)S(1)}, u32[]{:S(2)}, u32[]{:S(2)}) collective-permute-start(bf16[8,16,896]{2,1,0:T(8,128)(2,1)} %pick.5), channel_id=1, source_target_pairs={{0,24},{1,29},{2,26},{3,31},{4,28},{5,25},{6,30},{7,27},{8,16},{9,... | collective-permute-start | bytes 688136 | tf_op jit(solution)/shard_map/ppermute | solution.py:203
  70.5 8.5 %collective-permute-start.12 = (bf16[8,16,896]{2,1,0:T(8,128)(2,1)S(1)}, bf16[8,16,896]{2,1,0:T(8,128)(2,1)S(1)}, u32[]{:S(2)}, u32[]{:S(2)}) collective-permute-start(bf16[8,16,896]{2,1,0:T(8,128)(2,1)S(1)} %collective-permute-done.11.refs_0_), channel_id=1, source_target_pairs={{0,2},{1,3},{2,0},{3,1},{4,6},{5,7},{6,4},{7,5},{8,10},{9,11},{10,... | collective-permute-start | bytes 688136 | tf_op jit(solution)/shard_map/ppermute | solution.py:206
  72.0 29.9 %collective-permute-start.7 = (bf16[8,16,896]{2,1,0:T(8,128)(2,1)S(1)}, bf16[8,16,896]{2,1,0:T(8,128)(2,1)S(1)}, u32[]{:S(2)}, u32[]{:S(2)}) collective-permute-start(bf16[8,16,896]{2,1,0:T(8,128)(2,1)S(1)} %collective-permute-done.6.refs_0_), channel_id=1, source_target_pairs={{0,2},{1,3},{2,0},{3,1},{4,6},{5,7},{6,4},{7,5},{8,10},{9,11},{10,... | collective-permute-start | bytes 688136 | tf_op jit(solution)/shard_map/ppermute | solution.py:206
  72.6 32.7 %collective-permute-start.13 = (bf16[8,16,896]{2,1,0:T(8,128)(2,1)S(1)}, bf16[8,16,896]{2,1,0:T(8,128)(2,1)S(1)}, u32[]{:S(2)}, u32[]{:S(2)}) collective-permute-start(bf16[8,16,896]{2,1,0:T(8,128)(2,1)S(1)} %collective-permute-done.11.refs_0_), channel_id=1, source_target_pairs={{0,1},{1,0},{2,3},{3,2},{4,5},{5,4},{6,7},{7,6},{8,9},{9,8},{10,11... | collective-permute-start | bytes 688136 | tf_op jit(solution)/shard_map/ppermute | solution.py:206
  76.3 29.4 %collective-permute-start.2 = (bf16[8,16,896]{2,1,0:T(8,128)(2,1)S(1)}, bf16[8,16,896]{2,1,0:T(8,128)(2,1)S(1)}, u32[]{:S(2)}, u32[]{:S(2)}) collective-permute-start(bf16[8,16,896]{2,1,0:T(8,128)(2,1)S(1)} %collective-permute-done.1.refs_0_), channel_id=1, source_target_pairs={{0,2},{1,3},{2,0},{3,1},{4,6},{5,7},{6,4},{7,5},{8,10},{9,11},{10,... | collective-permute-start | bytes 688136 | tf_op jit(solution)/shard_map/ppermute | solution.py:206
  79.1 26.8 %collective-permute-start.14 = (bf16[8,16,896]{2,1,0:T(8,128)(2,1)S(1)}, bf16[8,16,896]{2,1,0:T(8,128)(2,1)S(1)}, u32[]{:S(2)}, u32[]{:S(2)}) collective-permute-start(bf16[8,16,896]{2,1,0:T(8,128)(2,1)S(1)} %collective-permute-done.12.refs_1_), channel_id=1, source_target_pairs={{0,1},{1,0},{2,3},{3,2},{4,5},{5,4},{6,7},{7,6},{8,9},{9,8},{10,11... | collective-permute-start | bytes 688136 | tf_op jit(solution)/shard_map/ppermute | solution.py:206
  95.4 6.6 %copy-start.1 = (bf16[8,32,896]{2,1,0:T(8,128)(2,1)S(1)}, bf16[8,32,896]{2,1,0:T(8,128)(2,1)}, u32[]{:S(2)}) copy-start(bf16[8,32,896]{2,1,0:T(8,128)(2,1)} %pick.8.refs_0_) | copy-start | bytes 1376260
  101.3 7.8 %collective-permute-start.8 = (bf16[8,16,896]{2,1,0:T(8,128)(2,1)S(1)}, bf16[8,16,896]{2,1,0:T(8,128)(2,1)S(1)}, u32[]{:S(2)}, u32[]{:S(2)}) collective-permute-start(bf16[8,16,896]{2,1,0:T(8,128)(2,1)S(1)} %collective-permute-done.6.refs_0_), channel_id=1, source_target_pairs={{0,1},{1,0},{2,3},{3,2},{4,5},{5,4},{6,7},{7,6},{8,9},{9,8},{10,11... | collective-permute-start | bytes 688136 | tf_op jit(solution)/shard_map/ppermute | solution.py:206
  101.9 7.3 %collective-permute-start.9 = (bf16[8,16,896]{2,1,0:T(8,128)(2,1)S(1)}, bf16[8,16,896]{2,1,0:T(8,128)(2,1)S(1)}, u32[]{:S(2)}, u32[]{:S(2)}) collective-permute-start(bf16[8,16,896]{2,1,0:T(8,128)(2,1)S(1)} %collective-permute-done.7.refs_1_), channel_id=1, source_target_pairs={{0,1},{1,0},{2,3},{3,2},{4,5},{5,4},{6,7},{7,6},{8,9},{9,8},{10,11... | collective-permute-start | bytes 688136 | tf_op jit(solution)/shard_map/ppermute | solution.py:206
  105.2 7.3 %collective-permute-start.3 = (bf16[8,16,896]{2,1,0:T(8,128)(2,1)S(1)}, bf16[8,16,896]{2,1,0:T(8,128)(2,1)S(1)}, u32[]{:S(2)}, u32[]{:S(2)}) collective-permute-start(bf16[8,16,896]{2,1,0:T(8,128)(2,1)S(1)} %collective-permute-done.1.refs_0_), channel_id=1, source_target_pairs={{0,1},{1,0},{2,3},{3,2},{4,5},{5,4},{6,7},{7,6},{8,9},{9,8},{10,11... | collective-permute-start | bytes 688136 | tf_op jit(solution)/shard_map/ppermute | solution.py:206
  105.7 6.8 %collective-permute-start.4 = (bf16[8,16,896]{2,1,0:T(8,128)(2,1)S(1)}, bf16[8,16,896]{2,1,0:T(8,128)(2,1)S(1)}, u32[]{:S(2)}, u32[]{:S(2)}) collective-permute-start(bf16[8,16,896]{2,1,0:T(8,128)(2,1)S(1)} %collective-permute-done.2.refs_1_), channel_id=1, source_target_pairs={{0,1},{1,0},{2,3},{3,2},{4,5},{5,4},{6,7},{7,6},{8,9},{9,8},{10,11... | collective-permute-start | bytes 688136 | tf_op jit(solution)/shard_map/ppermute | solution.py:206
  112.5 3.4 %copy-start = (bf16[2048,1024]{1,0:T(8,128)(2,1)S(1)}, bf16[2048,1024]{1,0:T(8,128)(2,1)}, u32[]{:S(2)}) copy-start(bf16[2048,1024]{1,0:T(8,128)(2,1)} %queries_ref.1) | copy-start | bytes 12582916
  112.5 3.4 %copy-start.2 = (s32[64]{0:T(128)S(1)}, s32[64]{0:T(128)}, u32[]{:S(2)}) copy-start(s32[64]{0:T(128)} %slots.1.slots_ref) | copy-start | bytes 772

commit v2 on v1

--- a/solution.py
+++ b/solution.py
@@ -12,23 +12,23 @@
 MIB = 1024 * 1024
 
 
-def hits_of(ids_ref, table_ref, owner, tile_count, ref_count):
-    def step(i, count):
-        tile_id = ids_ref[lax.rem(i, 2), lax.div(i, 2)]
-        table_ref[count] = lax.rem(tile_id, tile_count)
-        return count + (lax.div(tile_id, tile_count) == owner).astype(jnp.int32)
-
-    lax.fori_loop(0, ref_count, step, jnp.int32(0), unroll=8)
-
-
-def pick_kernel(rows, split, capacity, ids_ref, stored_ref, out_ref, table_ref, sem):
-    seq_at, mp_at = lax.axis_index("seq"), lax.axis_index("mp")
+def pick_kernel(rows, split, capacity, ids_ref, stored_ref, out_ref, ids_at, table_ref, ids_sem, sem):
     tile_count = stored_ref.shape[0]
-    hits_of(ids_ref, table_ref, seq_at, tile_count, 2 * ids_ref.shape[1])
-    first = pl.multiple_of((mp_at // 2) * rows, rows) if split else 0
+    fetch = pltpu.make_async_copy(ids_ref, ids_at, ids_sem)
+    fetch.start()
+    lowest = lax.axis_index("seq") * tile_count
+    first = pl.multiple_of(lax.axis_index("mp") // 2 * rows, rows) if split else 0
+    fetch.wait()
+    count = jnp.int32(0)
+    for k in range(ids_ref.shape[0]):
+        for c in range(ids_ref.shape[1]):
+            local = ids_at[k, c] - lowest
+            table_ref[count] = local
+            count += ((local >= 0) & (local < tile_count)).astype(jnp.int32)
     copies = []
     for j in range(capacity):
-        source = stored_ref.at[table_ref[j], pl.ds(first, rows), :]
+        local = jnp.clip(table_ref[j], 0, tile_count - 1)
+        source = stored_ref.at[local, pl.ds(first, rows), :]
         copies.append(pltpu.make_async_copy(source, out_ref.at[j], sem.at[j]))
         copies[-1].start()
     for copy in copies:
@@ -40,9 +40,14 @@
     return pl.pallas_call(
         functools.partial(pick_kernel, rows, split, capacity),
         out_shape=jax.ShapeDtypeStruct((capacity, rows, stored.shape[2]), stored.dtype),
-        in_specs=[pl.BlockSpec(memory_space=pltpu.SMEM), pl.BlockSpec(memory_space=pl.ANY)],
-        out_specs=pl.BlockSpec(memory_space=pl.ANY),
-        scratch_shapes=[pltpu.SMEM((2 * ids.shape[1] + 1,), jnp.int32), pltpu.SemaphoreType.DMA((capacity,))],
+        in_specs=[pl.BlockSpec(memory_space=pl.ANY), pl.BlockSpec(memory_space=pl.ANY)],
+        out_specs=pl.BlockSpec(memory_space=pltpu.VMEM),
+        scratch_shapes=[
+            pltpu.SMEM(ids.shape, jnp.int32),
+            pltpu.SMEM((ids.size + 1,), jnp.int32),
+            pltpu.SemaphoreType.DMA,
+            pltpu.SemaphoreType.DMA((capacity,)),
+        ],
         name="pick",
     )(ids, stored)
 
@@ -52,17 +57,15 @@
     for owner in range(seq_count):
         rank_ref[owner] = 0
 
-    def step(i, carry):
-        owner = lax.div(ids_ref[lax.rem(i, 2), lax.div(i, 2)], tile_count)
-        rank = rank_ref[owner]
-        rank_ref[owner] = rank + 1
-        apart = owner ^ seq_at
-        part, side = lax.div(apart, 2), lax.rem(apart, 2)
-        side = jnp.where(part == 0, side, side ^ core)
-        slots_ref[i] = (part * 2 + side) * capacity + rank
-        return carry
-
-    lax.fori_loop(0, 2 * ids_ref.shape[1], step, 0)
+    for k in range(ids_ref.shape[0]):
+        for c in range(ids_ref.shape[1]):
+            owner = lax.div(ids_ref[k, c], tile_count)
+            rank = rank_ref[owner]
+            rank_ref[owner] = rank + 1
+            apart = owner ^ seq_at
+            part, side = lax.div(apart, 2), lax.rem(apart, 2)
+            side = jnp.where(part == 0, side, side ^ core)
+            slots_ref[2 * c + k] = (part * 2 + side) * capacity + rank
 
 
 def slots_of(ids, tile_count, seq_count, capacity):
@@ -119,44 +122,76 @@
     )(*operands)
 
 
-def attend_kernel(heads, slots_ref, queries_ref, first_ref, second_ref, out_ref):
-    width = heads * HEAD_DIM
-    scale = HEAD_DIM ** (-0.5)
-    for h in range(heads):
-        key_at, value_at = pl.ds(h * HEAD_DIM, HEAD_DIM), pl.ds(width + h * HEAD_DIM, HEAD_DIM)
-        keys = jnp.concatenate([first_ref[0, :, key_at], second_ref[0, :, key_at]], axis=0)
-        values = jnp.concatenate([first_ref[0, :, value_at], second_ref[0, :, value_at]], axis=0)
-        scores = lax.dot_general(
-            queries_ref[:, key_at], keys, (((1,), (1,)), ((), ())), preferred_element_type=jnp.float32
-        )
-        top = jnp.max(scores, axis=-1, keepdims=True)
-        expd = jnp.exp((scores - top) * scale)
-        probs = (expd / jnp.sum(expd, axis=-1, keepdims=True)).astype(jnp.bfloat16)
-        mixed = jnp.dot(probs, values, preferred_element_type=jnp.float32)
-        out_ref[:, key_at] = mixed.astype(jnp.bfloat16)
+def scores_of(queries, keys):
+    both = lax.dot_general(
+        jnp.concatenate(keys, axis=0),
+        jnp.concatenate(queries, axis=0),
+        (((1,), (1,)), ((), ())),
+        preferred_element_type=jnp.float32,
+    )
+    rows = both.shape[0] // 2
+    left = lax.broadcasted_iota(jnp.int32, (rows, both.shape[1]), 1) < both.shape[1] // 2
+    return jnp.where(left, both[:rows], both[rows:])
+
+
+def probs_of(scores):
+    expd = jnp.exp((scores - jnp.max(scores, axis=0, keepdims=True)) * HEAD_DIM ** (-0.5))
+    return (expd * (1.0 / jnp.sum(expd, axis=0, keepdims=True))).astype(jnp.bfloat16)
+
+
+def mix(probs, values):
+    both = lax.dot_general(
+        probs, jnp.concatenate(values, axis=1), (((0,), (0,)), ((), ())), preferred_element_type=jnp.float32
+    )
+    half = both.shape[0] // 2
+    return both[:half, :HEAD_DIM], both[half:, HEAD_DIM:]
+
+
+def attend_kernel(heads, many, slots_ref, queries_ref, held_ref, out_ref):
+    apart = 6
+    first = pl.program_id(0) * many
+    items = [(g, h) for g in range(many) for h in range(0, heads, 2)]
+
+    def part_of(g, h):
+        one, two = slots_ref[2 * (first + g)], slots_ref[2 * (first + g) + 1]
+        at = pl.ds(h * HEAD_DIM, HEAD_DIM)
+        return jnp.concatenate([held_ref[one, :, at], held_ref[two, :, at]], axis=0)
+
+    scores, probs = {}, {}
+    for now in range(len(items) + 2 * apart):
+        if now < len(items):
+            g, h = items[now]
+            queries = [queries_ref[pl.ds(g * GROUP, GROUP), pl.ds((h + i) * HEAD_DIM, HEAD_DIM)] for i in range(2)]
+            scores[now] = scores_of(queries, [part_of(g, h + i) for i in range(2)])
+        if apart <= now < len(items) + apart:
+            probs[now - apart] = probs_of(scores.pop(now - apart))
+        if 2 * apart <= now:
+            g, h = items[now - 2 * apart]
+            mixed = mix(probs.pop(now - 2 * apart), [part_of(g, heads + h + i) for i in range(2)])
+            for i in range(2):
+                out_ref[pl.ds(g * GROUP, GROUP), pl.ds((h + i) * HEAD_DIM, HEAD_DIM)] = mixed[i].astype(jnp.bfloat16)
 
 
 def attend(queries, held, slots, heads):
     groups = queries.shape[0] // GROUP
-    tile = (1, held.shape[1], held.shape[2])
-    block = (GROUP, queries.shape[1])
-    return pl.pallas_call(
-        functools.partial(attend_kernel, heads),
+    many = 8 if groups % 8 == 0 else 1
+    block = (many * GROUP, queries.shape[1])
+    return pl.pallas_call(
+        functools.partial(attend_kernel, heads, many),
         out_shape=jax.ShapeDtypeStruct(queries.shape, jnp.bfloat16),
         grid_spec=pltpu.PrefetchScalarGridSpec(
             num_scalar_prefetch=1,
-            grid=(groups,),
+            grid=(groups // many,),
             in_specs=[
                 pl.BlockSpec(block, lambda c, s: (c, 0)),
-                pl.BlockSpec(tile, lambda c, s: (s[2 * c], 0, 0)),
-                pl.BlockSpec(tile, lambda c, s: (s[2 * c + 1], 0, 0)),
+                pl.BlockSpec(held.shape, lambda c, s: (0, 0, 0), pipeline_mode=pl.Buffered(1)),
             ],
             out_specs=pl.BlockSpec(block, lambda c, s: (c, 0)),
         ),
-        compiler_params=pltpu.CompilerParams(vmem_limit_bytes=32 * MIB),
+        compiler_params=pltpu.CompilerParams(vmem_limit_bytes=40 * MIB),
         cost_estimate=pl.CostEstimate(flops=10**9, bytes_accessed=16 * MIB, transcendentals=10**6),
         name="attend",
-    )(slots, queries, held, held)
+    )(slots, queries, held)
 
 
 def ref_ranks(owners):
@@ -206,7 +241,6 @@
         return lax.ppermute(value, "mp", [(m, m ^ flip) for m in range(mp_count)])
 
     ids = retrieved.T
-    order = [p for p in range(parts - 1, 0, -1)] + [0]
     order = sorted(range(parts), key=lambda p: (-(p // 2), p))
     weights = w_kv.reshape(width, -1)
     slots = slots_of(ids, tile_count, seq_count, capacity)

time: 200 us -> 77.9 us (0.39)
  the two profiles are of different devices: /device:TPU:0 before, /device:TPU:9 now
where the time goes in v2:
time: 77.9 us; the launch traced here: 77.2 us
  Pallas kernels  34.5 us (44%)
  starting transfers between devices  18.6 us (24%)
  waiting for transfers between devices  18.5 us (24%)
  local copies, waits for them, and re-layouts  5.52 us (7%)
    ppermute x6, waiting for transfers between devices, across(): lax.ppermute(value, both, joint(lambda s, m: (s ^ 2 * part ^ m % 2) * mp_...  18.5 us
    pallas_call x4, Pallas kernels, project(): pl.pallas_call(functools.partial(project_kernel, count), grid=(columns //...  13.2 us
    pallas_call x5, Pallas kernels, pick(): pl.pallas_call(functools.partial(pick_kernel, rows, split, capacity), out...  12.9 us
    ppermute x6, starting transfers between devices, across(): lax.ppermute(value, both, joint(lambda s, m: (s ^ 2 * part ^ m % 2) * mp_...  9.39 us
    ppermute x9, starting transfers between devices, over_mp(): return lax.ppermute(value, 'mp', [(m, m ^ flip) for m in range(mp_count)])  8.64 us
    pallas_call x1, Pallas kernels, attend(): pl.pallas_call(functools.partial(attend_kernel, heads, many), out_shape=j...  6.51 us
    unnamed x17, local copies, waits for them, and re-layouts  5.52 us
    pallas_call x1, Pallas kernels, slots_of(): pl.pallas_call(functools.partial(slots_kernel, tile_count, seq_count, cap...  1.83 us
  transfers between devices with their start and end apart: 17, of which 3 were waited for; matrix products, arithmetic and copies ran while one was open for 4% of the time, Pallas kernels for 29%

profile of v2, /device:TPU:9, one launch (start us, length us, event | category | flops | bytes accessed | tf_op | source)
XLA Modules:
  0.0 77.2 jit_solution(15797509408921683215)
XLA Ops:
  0.0 1.1 %collective-permute-start.10 = (s32[2,32]{1,0:T(2,128)}, s32[2,32]{1,0:T(2,128)S(1)}, u32[]{:S(2)}, u32[]{:S(2)}) collective-permute-start(s32[2,32]{1,0:T(2,128)} %bitcast.8), channel_id=1, source_target_pairs={{0,8},{1,13},{2,10},{3,15},{4,12},{5,9},{6,14},{7,11},{8,0},{9,5},... | collective-permute-start | bytes 776 | tf_op jit(solution)/shard_map/ppermute | solution.py:238
  1.1 2.4 %collective-permute-done.10.ids_ref = s32[2,32]{1,0:T(2,128)S(1)} collective-permute-done((s32[2,32]{1,0:T(2,128)}, s32[2,32]{1,0:T(2,128)S(1)}, u32[]{:S(2)}, u32[]{:S(2)}) %collective-permute-start.10) | collective-permute-done | bytes 288 | tf_op jit(solution)/shard_map/ppermute | solution.py:238
  3.5 0.6 copy-done.4
  4.1 2.5 %pick.7 = bf16[8,16,896]{2,1,0:T(8,128)(2,1)} custom-call(s32[2,32]{1,0:T(2,128)} %copy-done.4, bf16[32,32,896]{2,1,0:T(8,128)(2,1)} %stored_ref.9), custom_call_target="tpu_custom_call" | custom-call | tf_op jit(solution)/shard_map/pick/pallas_call | solution.py:40
  6.6 1.2 %collective-permute-start.11 = (bf16[8,16,896]{2,1,0:T(8,128)(2,1)}, bf16[8,16,896]{2,1,0:T(8,128)(2,1)S(1)}, u32[]{:S(2)}, u32[]{:S(2)}) collective-permute-start(bf16[8,16,896]{2,1,0:T(8,128)(2,1)} %pick.7), channel_id=1, source_target_pairs={{0,8},{1,13},{2,10},{3,15},{4,12},{5,9},{6,14},{7,11},{8,0},{9,5},... | collective-permute-start | bytes 688136 | tf_op jit(solution)/shard_map/ppermute | solution.py:238
  8.0 3.3 %collective-permute-start.5 = (s32[2,32]{1,0:T(2,128)}, s32[2,32]{1,0:T(2,128)S(1)}, u32[]{:S(2)}, u32[]{:S(2)}) collective-permute-start(s32[2,32]{1,0:T(2,128)} %bitcast.10), channel_id=1, source_target_pairs={{0,16},{1,21},{2,18},{3,23},{4,20},{5,17},{6,22},{7,19},{8,24},{9,... | collective-permute-start | bytes 776 | tf_op jit(solution)/shard_map/ppermute | solution.py:238
  11.3 0.6 copy-done.7
  11.8 2.7 %pick.9 = bf16[8,32,896]{2,1,0:T(8,128)(2,1)} custom-call(s32[2,32]{1,0:T(2,128)} %copy-done.7, bf16[32,32,896]{2,1,0:T(8,128)(2,1)} %stored_ref.9), custom_call_target="tpu_custom_call" | custom-call | tf_op jit(solution)/shard_map/pick/pallas_call | solution.py:40
  14.6 0.3 collective-permute-start.16
  14.9 0.6 copy-done.3
  15.4 2.5 %pick.6 = bf16[8,16,896]{2,1,0:T(8,128)(2,1)} custom-call(s32[2,32]{1,0:T(2,128)} %copy-done.3, bf16[32,32,896]{2,1,0:T(8,128)(2,1)} %stored_ref.9), custom_call_target="tpu_custom_call" | custom-call | tf_op jit(solution)/shard_map/pick/pallas_call | solution.py:40
  17.9 2.6 %collective-permute-start.6 = (bf16[8,16,896]{2,1,0:T(8,128)(2,1)}, bf16[8,16,896]{2,1,0:T(8,128)(2,1)S(1)}, u32[]{:S(2)}, u32[]{:S(2)}) collective-permute-start(bf16[8,16,896]{2,1,0:T(8,128)(2,1)} %pick.6), channel_id=1, source_target_pairs={{0,16},{1,21},{2,18},{3,23},{4,20},{5,17},{6,22},{7,19},{8,24},{9,... | collective-permute-start | bytes 688136 | tf_op jit(solution)/shard_map/ppermute | solution.py:238
  20.5 0.9 %collective-permute-start = (s32[2,32]{1,0:T(2,128)S(1)}, s32[2,32]{1,0:T(2,128)S(1)}, u32[]{:S(2)}, u32[]{:S(2)}) collective-permute-start(s32[2,32]{1,0:T(2,128)S(1)} %bitcast.13), channel_id=1, source_target_pairs={{0,24},{1,29},{2,26},{3,31},{4,28},{5,25},{6,30},{7,27},{8,16},{9,... | collective-permute-start | bytes 776 | tf_op jit(solution)/shard_map/ppermute | solution.py:238
  21.4 10.8 %collective-permute-done.ids_ref = s32[2,32]{1,0:T(2,128)S(1)} collective-permute-done((s32[2,32]{1,0:T(2,128)S(1)}, s32[2,32]{1,0:T(2,128)S(1)}, u32[]{:S(2)}, u32[]{:S(2)}) %collective-permute-start) | collective-permute-done | bytes 288 | tf_op jit(solution)/shard_map/ppermute | solution.py:238
  32.2 0.5 copy-done.5
  32.7 2.5 %pick.5 = bf16[8,16,896]{2,1,0:T(8,128)(2,1)} custom-call(s32[2,32]{1,0:T(2,128)} %copy-done.5, bf16[32,32,896]{2,1,0:T(8,128)(2,1)} %stored_ref.9), custom_call_target="tpu_custom_call" | custom-call | tf_op jit(solution)/shard_map/pick/pallas_call | solution.py:40
  35.2 0.3 collective-permute-start.1
  35.6 1.2 %collective-permute-start.12 = (bf16[8,16,896]{2,1,0:T(8,128)(2,1)S(1)}, bf16[8,16,896]{2,1,0:T(8,128)(2,1)S(1)}, u32[]{:S(2)}, u32[]{:S(2)}) collective-permute-start(bf16[8,16,896]{2,1,0:T(8,128)(2,1)S(1)} %collective-permute-done.11.refs_0_), channel_id=1, source_target_pairs={{0,2},{1,3},{2,0},{3,1},{4,6},{5,7},{6,4},{7,5},{8,10},{9,11},{10,... | collective-permute-start | bytes 688136 | tf_op jit(solution)/shard_map/ppermute | solution.py:241
  37.0 2.1 %collective-permute-start.13 = (bf16[8,16,896]{2,1,0:T(8,128)(2,1)S(1)}, bf16[8,16,896]{2,1,0:T(8,128)(2,1)S(1)}, u32[]{:S(2)}, u32[]{:S(2)}) collective-permute-start(bf16[8,16,896]{2,1,0:T(8,128)(2,1)S(1)} %collective-permute-done.11.refs_0_), channel_id=1, source_target_pairs={{0,1},{1,0},{2,3},{3,2},{4,5},{5,4},{6,7},{7,6},{8,9},{9,8},{10,11... | collective-permute-start | bytes 688136 | tf_op jit(solution)/shard_map/ppermute | solution.py:241
  39.1 5.3 %collective-permute-done.1.refs_0_ = bf16[8,16,896]{2,1,0:T(8,128)(2,1)S(1)} collective-permute-done((bf16[8,16,896]{2,1,0:T(8,128)(2,1)}, bf16[8,16,896]{2,1,0:T(8,128)(2,1)S(1)}, u32[]{:S(2)}, u32[]{:S(2)}) %collective-permute-start.1) | collective-permute-done | bytes 229408 | tf_op jit(solution)/shard_map/ppermute | solution.py:238
  44.4 1.2 %collective-permute-start.2 = (bf16[8,16,896]{2,1,0:T(8,128)(2,1)S(1)}, bf16[8,16,896]{2,1,0:T(8,128)(2,1)S(1)}, u32[]{:S(2)}, u32[]{:S(2)}) collective-permute-start(bf16[8,16,896]{2,1,0:T(8,128)(2,1)S(1)} %collective-permute-done.1.refs_0_), channel_id=1, source_target_pairs={{0,2},{1,3},{2,0},{3,1},{4,6},{5,7},{6,4},{7,5},{8,10},{9,11},{10,... | collective-permute-start | bytes 688136 | tf_op jit(solution)/shard_map/ppermute | solution.py:241
  45.6 2.7 %collective-permute-start.14 = (bf16[8,16,896]{2,1,0:T(8,128)(2,1)S(1)}, bf16[8,16,896]{2,1,0:T(8,128)(2,1)S(1)}, u32[]{:S(2)}, u32[]{:S(2)}) collective-permute-start(bf16[8,16,896]{2,1,0:T(8,128)(2,1)S(1)} %collective-permute-done.12.refs_1_), channel_id=1, source_target_pairs={{0,1},{1,0},{2,3},{3,2},{4,5},{5,4},{6,7},{7,6},{8,9},{9,8},{10,11... | collective-permute-start | bytes 688136 | tf_op jit(solution)/shard_map/ppermute | solution.py:241
  48.3 2.7 %pick.8.refs_0_ = bf16[8,32,896]{2,1,0:T(8,128)(2,1)} custom-call(s32[2,32]{1,0:T(2,128)} %bitcast.11, bf16[32,32,896]{2,1,0:T(8,128)(2,1)} %stored_ref.9), custom_call_target="tpu_custom_call" | custom-call | tf_op jit(solution)/shard_map/pick/pallas_call | solution.py:40
  51.1 1.8 %slots.1.slots_ref = s32[64]{0:T(128)} custom-call(s32[2,32]{1,0:T(2,128)} %bitcast.12), custom_call_target="tpu_custom_call" | custom-call | tf_op jit(solution)/shard_map/slots/pallas_call | solution.py:72
  52.9 3.3 %copy.8 = bf16[112,8,2,1024]{3,1,2,0:T(8,128)(2,1)S(1)} copy(bf16[112,8,2,1024]{3,2,1,0:T(2,128)(2,1)} %bitcast.7) | data formatting | bytes 7340032
  56.3 0.5 collective-permute-start.9
  56.8 3.3 %project.4.refs_5_ = bf16[64,32,2048]{2,1,0:T(8,128)(2,1)S(1)} custom-call(bf16[8,32,896]{2,1,0:T(8,128)(2,1)S(1)} %copy-done.1, bf16[8,32,896]{2,1,0:T(8,128)(2,1)S(1)} %collective-permute-done.16.refs_1_, bf16[896,2048]{1,0:T(8,128)(2,1)S(1)} %bitcast.3), custom_call_target="tpu_custom_call" | custom-call | flops 1879048192 | bytes 8388608 | tf_op jit(solution)/shard_map/project/pallas_call | solution.py:112
  60.2 0.4 collective-permute-start.4
  60.7 3.3 %project.5.refs_5_ = bf16[64,32,2048]{2,1,0:T(8,128)(2,1)S(1)} custom-call(bf16[8,16,896]{2,1,0:T(8,128)(2,1)S(1)} %collective-permute-done.11.refs_0_, bf16[8,16,896]{2,1,0:T(8,128)(2,1)S(1)} %collective-permute-done.12.refs_1_, bf16[8,16,896]{2,1,0:T(8,128)(2,1)S(1)} %collective-permute-done.13.refs_2_, ...), custom_call_target="tpu_custom_call", output_to_operand_aliasing={{}: (5, {})} | custom-call | flops 1879048192 | bytes 8388608 | tf_op jit(solution)/shard_map/project/pallas_call | solution.py:112
  64.0 3.3 %project.6.refs_5_ = bf16[64,32,2048]{2,1,0:T(8,128)(2,1)S(1)} custom-call(bf16[8,16,896]{2,1,0:T(8,128)(2,1)S(1)} %collective-permute-done.6.refs_0_, bf16[8,16,896]{2,1,0:T(8,128)(2,1)S(1)} %collective-permute-done.7.refs_1_, bf16[8,16,896]{2,1,0:T(8,128)(2,1)S(1)} %collective-permute-done.8.refs_2_, ...), custom_call_target="tpu_custom_call", output_to_operand_aliasing={{}: (5, {})} | custom-call | flops 1879048192 | bytes 8388608 | tf_op jit(solution)/shard_map/project/pallas_call | solution.py:112
  67.4 3.3 %project.7.held_ref = bf16[64,32,2048]{2,1,0:T(8,128)(2,1)S(1)} custom-call(bf16[8,16,896]{2,1,0:T(8,128)(2,1)S(1)} %collective-permute-done.1.refs_0_, bf16[8,16,896]{2,1,0:T(8,128)(2,1)S(1)} %collective-permute-done.2.refs_1_, bf16[8,16,896]{2,1,0:T(8,128)(2,1)S(1)} %collective-permute-done.3.refs_2_, ...), custom_call_target="tpu_custom_call", output_to_operand_aliasing={{}: (5, {})} | custom-call | flops 1879048192 | bytes 8388608 | tf_op jit(solution)/shard_map/project/pallas_call | solution.py:112
  70.7 6.5 %attend.1 = bf16[2048,1024]{1,0:T(8,128)(2,1)} custom-call(s32[64]{0:T(128)S(1)} %copy-done.2, bf16[2048,1024]{1,0:T(8,128)(2,1)S(1)} %copy-done, bf16[64,32,2048]{2,1,0:T(8,128)(2,1)S(1)} %project.7.held_ref), custom_call_target="tpu_custom_call" | custom-call | flops 1000000000 | bytes 16777216 | tf_op jit(solution)/shard_map/attend/pallas_call | solution.py:179
  (30 shorter events, 0.8 us)
Async XLA Ops:
  0.0 20.5 %copy-start.6 = (s32[32,2]{0,1:T(2,128)S(1)}, s32[32,2]{0,1:T(2,128)}, u32[]{:S(2)}) copy-start(s32[32,2]{0,1:T(2,128)} %param.7) | copy-start | bytes 772
  0.0 3.5 %collective-permute-start.10 = (s32[2,32]{1,0:T(2,128)}, s32[2,32]{1,0:T(2,128)S(1)}, u32[]{:S(2)}, u32[]{:S(2)}) collective-permute-start(s32[2,32]{1,0:T(2,128)} %bitcast.8), channel_id=1, source_target_pairs={{0,8},{1,13},{2,10},{3,15},{4,12},{5,9},{6,14},{7,11},{8,0},{9,5},... | collective-permute-start | bytes 776 | tf_op jit(solution)/shard_map/ppermute | solution.py:238
  3.5 0.6 copy-start.4
  6.6 29.0 %collective-permute-start.11 = (bf16[8,16,896]{2,1,0:T(8,128)(2,1)}, bf16[8,16,896]{2,1,0:T(8,128)(2,1)S(1)}, u32[]{:S(2)}, u32[]{:S(2)}) collective-permute-start(bf16[8,16,896]{2,1,0:T(8,128)(2,1)} %pick.7), channel_id=1, source_target_pairs={{0,8},{1,13},{2,10},{3,15},{4,12},{5,9},{6,14},{7,11},{8,0},{9,5},... | collective-permute-start | bytes 688136 | tf_op jit(solution)/shard_map/ppermute | solution.py:238
  7.8 3.5 %collective-permute-start.15 = (s32[2,32]{1,0:T(2,128)}, s32[2,32]{1,0:T(2,128)S(1)}, u32[]{:S(2)}, u32[]{:S(2)}) collective-permute-start(s32[2,32]{1,0:T(2,128)} %bitcast.9), channel_id=1, source_target_pairs={{0,4},{4,0},{8,12},{12,8},{16,20},{20,16},{24,28},{28,24},{1,5},{5... | collective-permute-start | bytes 776 | tf_op jit(solution)/shard_map/ppermute | solution.py:237
  8.0 6.9 %collective-permute-start.5 = (s32[2,32]{1,0:T(2,128)}, s32[2,32]{1,0:T(2,128)S(1)}, u32[]{:S(2)}, u32[]{:S(2)}) collective-permute-start(s32[2,32]{1,0:T(2,128)} %bitcast.10), channel_id=1, source_target_pairs={{0,16},{1,21},{2,18},{3,23},{4,20},{5,17},{6,22},{7,19},{8,24},{9,... | collective-permute-start | bytes 776 | tf_op jit(solution)/shard_map/ppermute | solution.py:238
  11.3 0.6 copy-start.7
  14.6 41.6 %collective-permute-start.16 = (bf16[8,32,896]{2,1,0:T(8,128)(2,1)}, bf16[8,32,896]{2,1,0:T(8,128)(2,1)S(1)}, u32[]{:S(2)}, u32[]{:S(2)}) collective-permute-start(bf16[8,32,896]{2,1,0:T(8,128)(2,1)} %pick.9), channel_id=1, source_target_pairs={{0,4},{4,0},{8,12},{12,8},{16,20},{20,16},{24,28},{28,24},{1,5},{5... | collective-permute-start | bytes 1376264 | tf_op jit(solution)/shard_map/ppermute | solution.py:237
  14.9 0.6 copy-start.3
  17.9 18.8 %collective-permute-start.6 = (bf16[8,16,896]{2,1,0:T(8,128)(2,1)}, bf16[8,16,896]{2,1,0:T(8,128)(2,1)S(1)}, u32[]{:S(2)}, u32[]{:S(2)}) collective-permute-start(bf16[8,16,896]{2,1,0:T(8,128)(2,1)} %pick.6), channel_id=1, source_target_pairs={{0,16},{1,21},{2,18},{3,23},{4,20},{5,17},{6,22},{7,19},{8,24},{9,... | collective-permute-start | bytes 688136 | tf_op jit(solution)/shard_map/ppermute | solution.py:238
  20.5 11.7 %collective-permute-start = (s32[2,32]{1,0:T(2,128)S(1)}, s32[2,32]{1,0:T(2,128)S(1)}, u32[]{:S(2)}, u32[]{:S(2)}) collective-permute-start(s32[2,32]{1,0:T(2,128)S(1)} %bitcast.13), channel_id=1, source_target_pairs={{0,24},{1,29},{2,26},{3,31},{4,28},{5,25},{6,30},{7,27},{8,16},{9,... | collective-permute-start | bytes 776 | tf_op jit(solution)/shard_map/ppermute | solution.py:238
  32.2 0.5 copy-start.5
  35.2 9.2 %collective-permute-start.1 = (bf16[8,16,896]{2,1,0:T(8,128)(2,1)}, bf16[8,16,896]{2,1,0:T(8,128)(2,1)S(1)}, u32[]{:S(2)}, u32[]{:S(2)}) collective-permute-start(bf16[8,16,896]{2,1,0:T(8,128)(2,1)} %pick.5), channel_id=1, source_target_pairs={{0,24},{1,29},{2,26},{3,31},{4,28},{5,25},{6,30},{7,27},{8,16},{9,... | collective-permute-start | bytes 688136 | tf_op jit(solution)/shard_map/ppermute | solution.py:238
  35.6 10.0 %collective-permute-start.12 = (bf16[8,16,896]{2,1,0:T(8,128)(2,1)S(1)}, bf16[8,16,896]{2,1,0:T(8,128)(2,1)S(1)}, u32[]{:S(2)}, u32[]{:S(2)}) collective-permute-start(bf16[8,16,896]{2,1,0:T(8,128)(2,1)S(1)} %collective-permute-done.11.refs_0_), channel_id=1, source_target_pairs={{0,2},{1,3},{2,0},{3,1},{4,6},{5,7},{6,4},{7,5},{8,10},{9,11},{10,... | collective-permute-start | bytes 688136 | tf_op jit(solution)/shard_map/ppermute | solution.py:241
  36.8 19.5 %collective-permute-start.7 = (bf16[8,16,896]{2,1,0:T(8,128)(2,1)S(1)}, bf16[8,16,896]{2,1,0:T(8,128)(2,1)S(1)}, u32[]{:S(2)}, u32[]{:S(2)}) collective-permute-start(bf16[8,16,896]{2,1,0:T(8,128)(2,1)S(1)} %collective-permute-done.6.refs_0_), channel_id=1, source_target_pairs={{0,2},{1,3},{2,0},{3,1},{4,6},{5,7},{6,4},{7,5},{8,10},{9,11},{10,... | collective-permute-start | bytes 688136 | tf_op jit(solution)/shard_map/ppermute | solution.py:241
  37.0 23.0 %collective-permute-start.13 = (bf16[8,16,896]{2,1,0:T(8,128)(2,1)S(1)}, bf16[8,16,896]{2,1,0:T(8,128)(2,1)S(1)}, u32[]{:S(2)}, u32[]{:S(2)}) collective-permute-start(bf16[8,16,896]{2,1,0:T(8,128)(2,1)S(1)} %collective-permute-done.11.refs_0_), channel_id=1, source_target_pairs={{0,1},{1,0},{2,3},{3,2},{4,5},{5,4},{6,7},{7,6},{8,9},{9,8},{10,11... | collective-permute-start | bytes 688136 | tf_op jit(solution)/shard_map/ppermute | solution.py:241
  44.4 15.8 %collective-permute-start.2 = (bf16[8,16,896]{2,1,0:T(8,128)(2,1)S(1)}, bf16[8,16,896]{2,1,0:T(8,128)(2,1)S(1)}, u32[]{:S(2)}, u32[]{:S(2)}) collective-permute-start(bf16[8,16,896]{2,1,0:T(8,128)(2,1)S(1)} %collective-permute-done.1.refs_0_), channel_id=1, source_target_pairs={{0,2},{1,3},{2,0},{3,1},{4,6},{5,7},{6,4},{7,5},{8,10},{9,11},{10,... | collective-permute-start | bytes 688136 | tf_op jit(solution)/shard_map/ppermute | solution.py:241
  45.6 15.0 %collective-permute-start.14 = (bf16[8,16,896]{2,1,0:T(8,128)(2,1)S(1)}, bf16[8,16,896]{2,1,0:T(8,128)(2,1)S(1)}, u32[]{:S(2)}, u32[]{:S(2)}) collective-permute-start(bf16[8,16,896]{2,1,0:T(8,128)(2,1)S(1)} %collective-permute-done.12.refs_1_), channel_id=1, source_target_pairs={{0,1},{1,0},{2,3},{3,2},{4,5},{5,4},{6,7},{7,6},{8,9},{9,8},{10,11... | collective-permute-start | bytes 688136 | tf_op jit(solution)/shard_map/ppermute | solution.py:241
  51.1 5.7 %copy-start.1 = (bf16[8,32,896]{2,1,0:T(8,128)(2,1)S(1)}, bf16[8,32,896]{2,1,0:T(8,128)(2,1)}, u32[]{:S(2)}) copy-start(bf16[8,32,896]{2,1,0:T(8,128)(2,1)} %pick.8.refs_0_) | copy-start | bytes 1376260
  56.2 7.8 %collective-permute-start.8 = (bf16[8,16,896]{2,1,0:T(8,128)(2,1)S(1)}, bf16[8,16,896]{2,1,0:T(8,128)(2,1)S(1)}, u32[]{:S(2)}, u32[]{:S(2)}) collective-permute-start(bf16[8,16,896]{2,1,0:T(8,128)(2,1)S(1)} %collective-permute-done.6.refs_0_), channel_id=1, source_target_pairs={{0,1},{1,0},{2,3},{3,2},{4,5},{5,4},{6,7},{7,6},{8,9},{9,8},{10,11... | collective-permute-start | bytes 688136 | tf_op jit(solution)/shard_map/ppermute | solution.py:241
  56.3 7.7 %collective-permute-start.9 = (bf16[8,16,896]{2,1,0:T(8,128)(2,1)S(1)}, bf16[8,16,896]{2,1,0:T(8,128)(2,1)S(1)}, u32[]{:S(2)}, u32[]{:S(2)}) collective-permute-start(bf16[8,16,896]{2,1,0:T(8,128)(2,1)S(1)} %collective-permute-done.7.refs_1_), channel_id=1, source_target_pairs={{0,1},{1,0},{2,3},{3,2},{4,5},{5,4},{6,7},{7,6},{8,9},{9,8},{10,11... | collective-permute-start | bytes 688136 | tf_op jit(solution)/shard_map/ppermute | solution.py:241
  60.1 7.3 %collective-permute-start.3 = (bf16[8,16,896]{2,1,0:T(8,128)(2,1)S(1)}, bf16[8,16,896]{2,1,0:T(8,128)(2,1)S(1)}, u32[]{:S(2)}, u32[]{:S(2)}) collective-permute-start(bf16[8,16,896]{2,1,0:T(8,128)(2,1)S(1)} %collective-permute-done.1.refs_0_), channel_id=1, source_target_pairs={{0,1},{1,0},{2,3},{3,2},{4,5},{5,4},{6,7},{7,6},{8,9},{9,8},{10,11... | collective-permute-start | bytes 688136 | tf_op jit(solution)/shard_map/ppermute | solution.py:241
  60.2 7.1 %collective-permute-start.4 = (bf16[8,16,896]{2,1,0:T(8,128)(2,1)S(1)}, bf16[8,16,896]{2,1,0:T(8,128)(2,1)S(1)}, u32[]{:S(2)}, u32[]{:S(2)}) collective-permute-start(bf16[8,16,896]{2,1,0:T(8,128)(2,1)S(1)} %collective-permute-done.2.refs_1_), channel_id=1, source_target_pairs={{0,1},{1,0},{2,3},{3,2},{4,5},{5,4},{6,7},{7,6},{8,9},{9,8},{10,11... | collective-permute-start | bytes 688136 | tf_op jit(solution)/shard_map/ppermute | solution.py:241
  67.3 3.4 %copy-start = (bf16[2048,1024]{1,0:T(8,128)(2,1)S(1)}, bf16[2048,1024]{1,0:T(8,128)(2,1)}, u32[]{:S(2)}) copy-start(bf16[2048,1024]{1,0:T(8,128)(2,1)} %queries_ref.1) | copy-start | bytes 12582916
  67.3 3.4 %copy-start.2 = (s32[64]{0:T(128)S(1)}, s32[64]{0:T(128)}, u32[]{:S(2)}) copy-start(s32[64]{0:T(128)} %slots.1.slots_ref) | copy-start | bytes 772

commit v3 on v2

v3 whole, which is shorter than its diff:
```python
import functools

import jax
import jax.numpy as jnp
from jax import lax
from jax.experimental import pallas as pl
from jax.experimental.pallas import tpu as pltpu
from jax.sharding import PartitionSpec as P

GROUP = 64
HEAD_DIM = 128
MIB = 1024 * 1024
LIGHT = pl.CostEstimate(flops=1, bytes_accessed=1, transcendentals=0)


def in_vmem(value):
    return pltpu.with_memory_space_constraint(value, pltpu.VMEM)


def plan_kernel(capacity, tile_count, ids_ref, slots_ref):
    seq_at, core = lax.axis_index("seq"), lax.rem(lax.axis_index("mp"), 2)
    bits = tile_count.bit_length() - 1
    half = capacity // 2
    counts = jnp.int32(0)
    for k in range(ids_ref.shape[0]):
        for c in range(ids_ref.shape[1]):
            owner = lax.shift_right_logical(ids_ref[k, c], bits)
            shift = owner * 4
            rank = lax.shift_right_logical(counts, shift) & (capacity - 1)
            counts += jnp.int32(1) << shift
            apart = owner ^ seq_at
            near = ((apart & 1) * capacity) + (rank ^ ((apart & 1) * core * half))
            far = ((apart & -2) + ((apart & 1) ^ core)) * capacity + rank
            slots_ref[2 * c + k] = jnp.where(apart < 2, near, far)


def plan(ids, tile_count, capacity):
    smem = pl.BlockSpec(memory_space=pltpu.SMEM)
    return pl.pallas_call(
        functools.partial(plan_kernel, capacity, tile_count),
        out_shape=jax.ShapeDtypeStruct((ids.size,), jnp.int32),
        in_specs=[smem],
        out_specs=smem,
        cost_estimate=LIGHT,
        name="plan",
    )(ids)


def pick_kernel(plans, keep, *refs):
    count = len(plans)
    asked, stored_ref, pieces = refs[:count], refs[count], refs[count + 1 : -4]
    here_ref = refs[-5] if keep else stored_ref
    ids_at, table_ref, ids_sem, sem = refs[-4:]
    tile_count, rows, _ = stored_ref.shape
    fetches = [pltpu.make_async_copy(ref, ids_at.at[i], ids_sem.at[i]) for i, ref in enumerate(asked)]
    for fetch in fetches:
        fetch.start()
    if keep:
        load = pltpu.make_async_copy(stored_ref, here_ref, sem)
        load.start()
    lowest, mp_at = lax.axis_index("seq") * tile_count, lax.axis_index("mp")
    half = pl.multiple_of(mp_at // 2 * (rows // 2), rows // 2)
    for i in range(count):
        fetches[i].wait()
        found = jnp.int32(0)
        for k in range(ids_at.shape[1]):
            for c in range(ids_at.shape[2]):
                local = ids_at[i, k, c] - lowest
                table_ref[i, found] = local
                found += ((local >= 0) & (local < tile_count)).astype(jnp.int32)
    if keep:
        load.wait()
    at = 0
    for i, (kind, sizes) in enumerate(plans):
        rank = (mp_at % 2) * sizes[0] if kind == "tiles" else 0
        for size in sizes:
            for j in range(size):
                local = jnp.clip(table_ref[i, rank + j], 0, tile_count - 1)
                pieces[at][j] = here_ref[local, pl.ds(half, rows // 2), :] if kind == "rows" else here_ref[local]
            rank += size
            at += 1


def pick(asked, stored, plans, keep):
    _, rows, width = stored.shape
    vmem = pl.BlockSpec(memory_space=pltpu.VMEM)
    shapes = [(size, rows // 2 if kind == "rows" else rows, width) for kind, sizes in plans for size in sizes]
    shapes += [stored.shape] * keep
    ids = asked[0]
    return pl.pallas_call(
        functools.partial(pick_kernel, plans, keep),
        out_shape=[pltpu.VMEM(shape, stored.dtype) for shape in shapes],
        in_specs=[vmem] * len(asked) + [pl.BlockSpec(memory_space=pl.ANY) if keep else vmem],
        out_specs=[vmem] * len(shapes),
        scratch_shapes=[
            pltpu.SMEM((len(asked), *ids.shape), jnp.int32),
            pltpu.SMEM((len(asked), ids.size + 1), jnp.int32),
            pltpu.SemaphoreType.DMA((len(asked),)),
            pltpu.SemaphoreType.DMA,
        ],
        compiler_params=pltpu.CompilerParams(vmem_limit_bytes=(52 if keep else 16) * MIB),
        cost_estimate=LIGHT,
        name="pick",
    )(*[in_vmem(a) for a in asked], stored)


def pace_kernel(slots_ref, turn_ref):
    turn_ref[0] = slots_ref[0]


def pace(slots):
    smem = pl.BlockSpec(memory_space=pltpu.SMEM)
    return pl.pallas_call(
        pace_kernel,
        out_shape=jax.ShapeDtypeStruct((1,), jnp.int32),
        in_specs=[smem],
        out_specs=smem,
        cost_estimate=pl.CostEstimate(flops=3 * 10**9, bytes_accessed=0, transcendentals=0),
        name="pace",
    )(slots)


def project_kernel(places, *refs):
    pieces, weights_ref, out_ref = refs[: len(places)], refs[len(places)], refs[-1]
    flat = jnp.concatenate([piece[...].reshape(-1, piece.shape[2]) for piece in pieces], axis=0)
    step = min(512, weights_ref.shape[1])
    for at in range(0, weights_ref.shape[1], step):
        columns = pl.ds(at, step)
        made = jnp.dot(flat, weights_ref[:, columns], preferred_element_type=jnp.float32).astype(jnp.bfloat16)
        done = 0
        for (tile, row), piece in zip(places, pieces):
            tiles, rows, _ = piece.shape
            part = made[done : done + tiles * rows].reshape(tiles, rows, -1)
            out_ref[pl.ds(tile, tiles), pl.ds(row, rows), columns] = part
            done += tiles * rows


def project(pieces, weights, held, shape, weight):
    count = len(pieces)
    vmem = pl.BlockSpec(memory_space=pltpu.VMEM)
    operands = [in_vmem(p) for _, _, p in pieces] + [weights]
    aliases = {}
    if held is not None:
        operands.append(held)
        aliases = {count + 1: 0}
    many = sum(p.shape[0] * p.shape[1] for _, _, p in pieces)
    return pl.pallas_call(
        functools.partial(project_kernel, [(tile, row) for tile, row, _ in pieces]),
        out_shape=pltpu.VMEM(shape, jnp.bfloat16),
        in_specs=[vmem] * len(operands),
        out_specs=vmem,
        input_output_aliases=aliases,
        compiler_params=pltpu.CompilerParams(vmem_limit_bytes=16 * MIB),
        cost_estimate=pl.CostEstimate(flops=many * weights.size * weight // 4, bytes_accessed=0, transcendentals=0),
        name="project",
    )(*operands)


def scores_of(queries, keys):
    both = lax.dot_general(
        jnp.concatenate(keys, axis=0),
        jnp.concatenate(queries, axis=0),
        (((1,), (1,)), ((), ())),
        preferred_element_type=jnp.float32,
    )
    rows = both.shape[0] // 2
    left = lax.broadcasted_iota(jnp.int32, (rows, both.shape[1]), 1) < both.shape[1] // 2
    return jnp.where(left, both[:rows], both[rows:])


def probs_of(scores):
    expd = jnp.exp((scores - jnp.max(scores, axis=0, keepdims=True)) * HEAD_DIM ** (-0.5))
    return (expd * (1.0 / jnp.sum(expd, axis=0, keepdims=True))).astype(jnp.bfloat16)


def mix(probs, values):
    both = lax.dot_general(
        probs, jnp.concatenate(values, axis=1), (((0,), (0,)), ((), ())), preferred_element_type=jnp.float32
    )
    half = both.shape[0] // 2
    return both[:half, :HEAD_DIM], both[half:, HEAD_DIM:]


def attend_kernel(heads, many, slots_ref, queries_ref, held_ref, out_ref):
    apart = 6
    first = pl.program_id(0) * many
    items = [(g, h) for g in range(many) for h in range(0, heads, 2)]

    def part_of(g, h):
        one, two = slots_ref[2 * (first + g)], slots_ref[2 * (first + g) + 1]
        at = pl.ds(h * HEAD_DIM, HEAD_DIM)
        return jnp.concatenate([held_ref[one, :, at], held_ref[two, :, at]], axis=0)

    scores, probs = {}, {}
    for now in range(len(items) + 2 * apart):
        if now < len(items):
            g, h = items[now]
            queries = [queries_ref[pl.ds(g * GROUP, GROUP), pl.ds((h + i) * HEAD_DIM, HEAD_DIM)] for i in range(2)]
            scores[now] = scores_of(queries, [part_of(g, h + i) for i in range(2)])
        if apart <= now < len(items) + apart:
            probs[now - apart] = probs_of(scores.pop(now - apart))
        if 2 * apart <= now:
            g, h = items[now - 2 * apart]
            mixed = mix(probs.pop(now - 2 * apart), [part_of(g, heads + h + i) for i in range(2)])
            for i in range(2):
                out_ref[pl.ds(g * GROUP, GROUP), pl.ds((h + i) * HEAD_DIM, HEAD_DIM)] = mixed[i].astype(jnp.bfloat16)


def attend(queries, held, slots, heads):
    groups = queries.shape[0] // GROUP
    many = 8 if groups % 8 == 0 else 1
    block = (many * GROUP, queries.shape[1])
    return pl.pallas_call(
        functools.partial(attend_kernel, heads, many),
        out_shape=jax.ShapeDtypeStruct(queries.shape, jnp.bfloat16),
        grid_spec=pltpu.PrefetchScalarGridSpec(
            num_scalar_prefetch=1,
            grid=(groups // many,),
            in_specs=[
                pl.BlockSpec(block, lambda c, s: (c, 0)),
                pl.BlockSpec(memory_space=pltpu.VMEM),
            ],
            out_specs=pl.BlockSpec(block, lambda c, s: (c, 0)),
        ),
        compiler_params=pltpu.CompilerParams(vmem_limit_bytes=24 * MIB),
        cost_estimate=pl.CostEstimate(flops=10**9, bytes_accessed=16 * MIB, transcendentals=10**6),
        name="attend",
    )(slots, queries, in_vmem(held))


def ref_ranks(owners):
    length = owners.shape[-1]
    position = jnp.arange(length)
    earlier = position[None, :] < position[:, None]
    same_owner = owners[..., :, None] == owners[..., None, :]
    return jnp.sum(same_owner & earlier, axis=-1)


def plain_body(queries, encoded, w_kv, retrieved):
    seq_count = lax.axis_size("seq")
    ref_count = 2 * retrieved.shape[0]
    tile_count = encoded.shape[0]
    capacity = (ref_count + seq_count - 1) // seq_count
    tile_ids = retrieved.reshape(ref_count)
    owners = tile_ids // tile_count
    slot_ids = owners * capacity + ref_ranks(owners)
    wanted = jnp.arange(seq_count * capacity, dtype=jnp.int32)[:, None] == slot_ids[None, :]
    request = jnp.sum(jnp.where(wanted, (tile_ids % tile_count)[None, :], 0), axis=1)
    asked = lax.all_to_all(request, "seq", split_axis=0, concat_axis=0, tiled=True)
    outgoing = jnp.take(encoded, asked, axis=0, mode="clip")
    tiles = lax.all_to_all(outgoing, "seq", split_axis=0, concat_axis=0, tiled=True)
    weights = w_kv.reshape(w_kv.shape[0], -1)
    flat = jnp.dot(tiles.reshape(-1, tiles.shape[2]), weights, preferred_element_type=jnp.float32)
    held = flat.astype(jnp.bfloat16).reshape(tiles.shape[0], tiles.shape[1], -1)
    return attend(queries, held, slot_ids, queries.shape[1] // HEAD_DIM)


def split_body(queries, encoded, w_kv, retrieved):
    seq_count, mp_count = lax.axis_size("seq"), lax.axis_size("mp")
    ref_count = 2 * retrieved.shape[0]
    tile_count, rows, width = encoded.shape
    capacity = ref_count // seq_count
    both = ("seq", "mp")

    def joint(move):
        return [(s * mp_count + m, move(s, m)) for s in range(seq_count) for m in range(mp_count)]

    def across(value, part):
        if part == 0:
            return lax.ppermute(value, "seq", [(s, s ^ 1) for s in range(seq_count)])
        return lax.ppermute(value, both, joint(lambda s, m: (s ^ (2 * part) ^ (m % 2)) * mp_count + m))

    def over_mp(value, flip):
        return lax.ppermute(value, "mp", [(m, m ^ flip) for m in range(mp_count)])

    def after(value, *others):
        return lax.optimization_barrier((value, *others))[0]

    ids = retrieved.T
    size = capacity // 2

    def spread(mine, first):
        theirs = over_mp(mine, 2)
        return [
            (first, 0, mine),
            (first, rows // 2, theirs),
            (first + capacity, 0, over_mp(mine, 1)),
            (first + capacity, rows // 2, over_mp(theirs, 1)),
        ]

    asked = [across(ids, p) for p in (2, 1)]
    picked2, *picked1, stored = pick(asked, encoded, [("rows", [capacity]), ("all", [size, size])], True)
    got2, got1 = across(picked2, 2), across(picked1[0], 1)
    ids, w_kv = after(ids, picked2), after(w_kv, picked2)
    weights = in_vmem(w_kv.reshape(width, -1))
    slots = plan(ids, tile_count, capacity)
    asked = lax.optimization_barrier((across(ids, 3), across(ids, 0), weights, slots))[:2]
    picked3, beside, own = pick(
        [*asked, ids], stored, [("rows", [capacity]), ("tiles", [size]), ("all", [capacity])], False
    )
    picked3, picked1[1], beside, got2, got1 = lax.optimization_barrier((picked3, picked1[1], beside, got2, got1))
    got3 = across(picked3, 3)
    rest1 = across(picked1[1], 1)
    theirs2 = over_mp(got2, 2)
    beside = across(beside, 0)
    shape = (ref_count, rows, weights.shape[1])
    theirs3 = over_mp(got3, 2)
    turn = pace(after(slots, got3))
    got1, rest1, beside, got2, theirs2 = lax.optimization_barrier((got1, rest1, beside, got2, theirs2, turn))[:5]
    first = 4 * capacity
    part2 = [
        (first, 0, got2),
        (first, rows // 2, theirs2),
        (first + capacity, 0, over_mp(got2, 1)),
        (first + capacity, rows // 2, over_mp(theirs2, 1)),
    ]
    first = 2 * capacity
    part1 = [
        (first, 0, got1),
        (first + size, 0, rest1),
        (first + capacity, 0, over_mp(got1, 1)),
        (first + capacity + size, 0, over_mp(rest1, 1)),
    ]
    part0 = [(0, 0, own), (capacity, 0, beside), (capacity + size, 0, over_mp(beside, 1))]
    held = None
    for pieces in (part0, part2, part1):
        held = project(pieces, weights, held, shape, 1)
    theirs3 = after(theirs3, held)
    first = 6 * capacity
    part3 = [(first, 0, got3), (first + capacity, 0, over_mp(got3, 1))]
    rest3 = [(first, rows // 2, theirs3), (first + capacity, rows // 2, over_mp(theirs3, 1))]
    held = project(part3, weights, held, shape, 64)
    held = project(rest3, weights, held, shape, 8)
    return attend(queries, held, slots, queries.shape[1] // HEAD_DIM)


def body(queries, encoded, w_kv, retrieved):
    seq_count, mp_count = lax.axis_size("seq"), lax.axis_size("mp")
    ref_count = 2 * retrieved.shape[0]
    few = seq_count == 8 and mp_count == 4
    capacity, tile_count = ref_count // seq_count, encoded.shape[0]
    even = capacity * seq_count == ref_count and capacity == 8 and tile_count & (tile_count - 1) == 0
    if few and even and encoded.shape[1] % 32 == 0:
        return split_body(queries, encoded, w_kv, retrieved)
    return plain_body(queries, encoded, w_kv, retrieved)


def solution(mesh):
    in_specs = (P("seq", "mp"), P("seq", None, None), P(None, None, "mp"), P("seq", None))
    out_specs = P("seq", "mp")
    return jax.shard_map(body, mesh=mesh, in_specs=in_specs, out_specs=out_specs, check_vma=False)
```

time: 77.9 us -> 59.1 us (0.76)
  the two profiles are of different devices: /device:TPU:9 before, /device:TPU:0 now
where the time goes in v3:
time: 59.1 us; the launch traced here: 58.9 us
  Pallas kernels  20.7 us (35%)
  starting transfers between devices  17.6 us (30%)
  waiting for transfers between devices  16.3 us (28%)
  local copies, waits for them, and re-layouts  4.17 us (7%)
    ppermute x7, starting transfers between devices, across(): lax.ppermute(value, both, joint(lambda s, m: (s ^ 2 * part ^ m % 2) * mp_...  10.9 us
    pallas_call x5, Pallas kernels, project(): pl.pallas_call(functools.partial(project_kernel, [(tile, row) for tile, r...  9.57 us
    ppermute x7, waiting for transfers between devices, across(): lax.ppermute(value, both, joint(lambda s, m: (s ^ 2 * part ^ m % 2) * mp_...  7.4 us
    pallas_call x1, Pallas kernels, attend(): pl.pallas_call(functools.partial(attend_kernel, heads, many), out_shape=j...  6.53 us
    ppermute x2, waiting for transfers between devices, across(): return lax.ppermute(value, 'seq', [(s, s ^ 1) for s in range(seq_count)])  4.73 us
    ppermute x9, waiting for transfers between devices, over_mp(): return lax.ppermute(value, 'mp', [(m, m ^ flip) for m in range(mp_count)])  4.21 us
    unnamed x7, local copies, waits for them, and re-layouts  4.17 us
    ppermute x9, starting transfers between devices, over_mp(): return lax.ppermute(value, 'mp', [(m, m ^ flip) for m in range(mp_count)])  3.68 us
  transfers between devices with their start and end apart: 18, of which 7 were waited for; matrix products, arithmetic and copies ran while one was open for 6% of the time, Pallas kernels for 19%

profile of v3, /device:TPU:0, one launch (start us, length us, event | category | flops | bytes accessed | tf_op | source)
XLA Modules:
  0.0 58.9 jit_solution(3425143422334028620)
XLA Ops:
  0.0 4.0 %collective-permute-start = (s32[2,32]{1,0:T(2,128)}, s32[2,32]{1,0:T(2,128)S(1)}, u32[]{:S(2)}, u32[]{:S(2)}) collective-permute-start(s32[2,32]{1,0:T(2,128)} %bitcast.8), channel_id=1, source_target_pairs={{0,16},{1,21},{2,18},{3,23},{4,20},{5,17},{6,22},{7,19},{8,24},{9,... | collective-permute-start | bytes 776 | tf_op jit(solution)/shard_map/ppermute | solution.py:271
  4.0 1.6 %collective-permute-start.1 = (s32[2,32]{1,0:T(2,128)}, s32[2,32]{1,0:T(2,128)S(1)}, u32[]{:S(2)}, u32[]{:S(2)}) collective-permute-start(s32[2,32]{1,0:T(2,128)} %bitcast.9), channel_id=1, source_target_pairs={{0,8},{1,13},{2,10},{3,15},{4,12},{5,9},{6,14},{7,11},{8,0},{9,5},... | collective-permute-start | bytes 776 | tf_op jit(solution)/shard_map/ppermute | solution.py:271
  5.6 0.2 collective-permute-done.refs_0_
  5.9 2.0 %collective-permute-done.1.refs_1_ = s32[2,32]{1,0:T(2,128)S(1)} collective-permute-done((s32[2,32]{1,0:T(2,128)}, s32[2,32]{1,0:T(2,128)S(1)}, u32[]{:S(2)}, u32[]{:S(2)}) %collective-permute-start.1) | collective-permute-done | bytes 288 | tf_op jit(solution)/shard_map/ppermute | solution.py:271
  7.8 1.6 %pick.2 = (bf16[8,16,896]{2,1,0:T(8,128)(2,1)S(1)}, bf16[4,32,896]{2,1,0:T(8,128)(2,1)S(1)}, bf16[4,32,896]{2,1,0:T(8,128)(2,1)S(1)}, bf16[32,32,896]{2,1,0:T(8,128)(2,1)S(1)}) custom-call(s32[2,32]{1,0:T(2,128)S(1)} %collective-permute-done.refs_0_, s32[2,32]{1,0:T(2,128)S(1)} %collective-permute-done.1.refs_1_, bf16[32,32,896]{2,1,0:T(8,128)(2,1)} %refs_2_.1), custom_call_target="tpu_custom_call" | custom-call | flops 1 | bytes 1 | tf_op jit(solution)/shard_map/pick/pallas_call | solution.py:90
  9.4 1.0 %collective-permute-start.4 = (bf16[8,16,896]{2,1,0:T(8,128)(2,1)S(1)}, bf16[8,16,896]{2,1,0:T(8,128)(2,1)S(1)}, u32[]{:S(2)}, u32[]{:S(2)}) collective-permute-start(bf16[8,16,896]{2,1,0:T(8,128)(2,1)S(1)} %get-tuple-element.27), channel_id=1, source_target_pairs={{0,16},{1,21},{2,18},{3,23},{4,20},{5,17},{6,22},{7,19},{8,24},{9,... | collective-permute-start | bytes 688136 | tf_op jit(solution)/shard_map/ppermute | solution.py:271
  10.4 1.6 %collective-permute-start.5 = (bf16[4,32,896]{2,1,0:T(8,128)(2,1)S(1)}, bf16[4,32,896]{2,1,0:T(8,128)(2,1)S(1)}, u32[]{:S(2)}, u32[]{:S(2)}) collective-permute-start(bf16[4,32,896]{2,1,0:T(8,128)(2,1)S(1)} %get-tuple-element.36), channel_id=1, source_target_pairs={{0,8},{1,13},{2,10},{3,15},{4,12},{5,9},{6,14},{7,11},{8,0},{9,5},... | collective-permute-start | bytes 688136 | tf_op jit(solution)/shard_map/ppermute | solution.py:271
  12.0 1.9 %collective-permute-start.2 = (s32[2,32]{1,0:T(2,128)}, s32[2,32]{1,0:T(2,128)S(1)}, u32[]{:S(2)}, u32[]{:S(2)}) collective-permute-start(s32[2,32]{1,0:T(2,128)} %bitcast.10), channel_id=1, source_target_pairs={{0,24},{1,29},{2,26},{3,31},{4,28},{5,25},{6,30},{7,27},{8,16},{9,... | collective-permute-start | bytes 776 | tf_op jit(solution)/shard_map/ppermute | solution.py:271
  13.9 1.5 %collective-permute-start.3 = (s32[2,32]{1,0:T(2,128)}, s32[2,32]{1,0:T(2,128)S(1)}, u32[]{:S(2)}, u32[]{:S(2)}) collective-permute-start(s32[2,32]{1,0:T(2,128)} %bitcast.11), channel_id=1, source_target_pairs={{0,4},{4,0},{8,12},{12,8},{16,20},{20,16},{24,28},{28,24},{1,5},{5... | collective-permute-start | bytes 776 | tf_op jit(solution)/shard_map/ppermute | solution.py:270
  15.4 1.6 %plan.1.slots_ref = s32[64]{0:T(128)} custom-call(s32[2,32]{1,0:T(2,128)} %bitcast.12), custom_call_target="tpu_custom_call" | custom-call | flops 1 | bytes 1 | tf_op jit(solution)/shard_map/plan/pallas_call | solution.py:39
  17.0 3.3 %copy.9 = bf16[112,8,2,1024]{3,1,2,0:T(8,128)(2,1)S(1)} copy(bf16[112,8,2,1024]{3,2,1,0:T(2,128)(2,1)} %bitcast.14) | data formatting | bytes 7340032
  20.3 3.8 %collective-permute-done.2.refs_0_ = s32[2,32]{1,0:T(2,128)S(1)} collective-permute-done((s32[2,32]{1,0:T(2,128)}, s32[2,32]{1,0:T(2,128)S(1)}, u32[]{:S(2)}, u32[]{:S(2)}) %collective-permute-start.2) | collective-permute-done | bytes 288 | tf_op jit(solution)/shard_map/ppermute | solution.py:271
  24.1 1.4 %pick.3 = (bf16[8,16,896]{2,1,0:T(8,128)(2,1)S(1)}, bf16[4,32,896]{2,1,0:T(8,128)(2,1)S(1)}, bf16[8,32,896]{2,1,0:T(8,128)(2,1)S(1)}) custom-call(s32[2,32]{1,0:T(2,128)S(1)} %collective-permute-done.2.refs_0_, s32[2,32]{1,0:T(2,128)S(1)} %collective-permute-done.3.refs_1_, s32[2,32]{1,0:T(2,128)S(1)} %bitcast.13, ...), custom_call_target="tpu_custom_call" | custom-call | flops 1 | bytes 1 | tf_op jit(solution)/shard_map/pick/pallas_call | solution.py:90
  25.5 1.6 %collective-permute-start.10 = (bf16[8,16,896]{2,1,0:T(8,128)(2,1)S(1)}, bf16[8,16,896]{2,1,0:T(8,128)(2,1)S(1)}, u32[]{:S(2)}, u32[]{:S(2)}) collective-permute-start(bf16[8,16,896]{2,1,0:T(8,128)(2,1)S(1)} %collective-permute-done.4.refs_0_), channel_id=1, source_target_pairs={{0,2},{1,3},{2,0},{3,1},{4,6},{5,7},{6,4},{7,5},{8,10},{9,11},{10,... | collective-permute-start | bytes 688136 | tf_op jit(solution)/shard_map/ppermute | solution.py:274
  27.0 1.5 %collective-permute-start.9 = (bf16[4,32,896]{2,1,0:T(8,128)(2,1)S(1)}, bf16[4,32,896]{2,1,0:T(8,128)(2,1)S(1)}, u32[]{:S(2)}, u32[]{:S(2)}) collective-permute-start(bf16[4,32,896]{2,1,0:T(8,128)(2,1)S(1)} %get-tuple-element.40), channel_id=1, source_target_pairs={{0,4},{4,0},{8,12},{12,8},{16,20},{20,16},{24,28},{28,24},{1,5},{5... | collective-permute-start | bytes 688136 | tf_op jit(solution)/shard_map/ppermute | solution.py:270
  28.6 0.8 %collective-permute-start.6 = (bf16[8,16,896]{2,1,0:T(8,128)(2,1)S(1)}, bf16[8,16,896]{2,1,0:T(8,128)(2,1)S(1)}, u32[]{:S(2)}, u32[]{:S(2)}) collective-permute-start(bf16[8,16,896]{2,1,0:T(8,128)(2,1)S(1)} %get-tuple-element.37), channel_id=1, source_target_pairs={{0,24},{1,29},{2,26},{3,31},{4,28},{5,25},{6,30},{7,27},{8,16},{9,... | collective-permute-start | bytes 688136 | tf_op jit(solution)/shard_map/ppermute | solution.py:271
  29.4 3.7 %collective-permute-done.10.refs_1_ = bf16[8,16,896]{2,1,0:T(8,128)(2,1)S(1)} collective-permute-done((bf16[8,16,896]{2,1,0:T(8,128)(2,1)S(1)}, bf16[8,16,896]{2,1,0:T(8,128)(2,1)S(1)}, u32[]{:S(2)}, u32[]{:S(2)}) %collective-permute-start.10) | collective-permute-done | bytes 229408 | tf_op jit(solution)/shard_map/ppermute | solution.py:274
  33.1 1.4 %collective-permute-done.8.refs_1_ = bf16[4,32,896]{2,1,0:T(8,128)(2,1)S(1)} collective-permute-done((bf16[4,32,896]{2,1,0:T(8,128)(2,1)S(1)}, bf16[4,32,896]{2,1,0:T(8,128)(2,1)S(1)}, u32[]{:S(2)}, u32[]{:S(2)}) %collective-permute-start.8) | collective-permute-done | bytes 229408 | tf_op jit(solution)/shard_map/ppermute | solution.py:271
  34.5 4.7 %collective-permute-done.9.refs_1_ = bf16[4,32,896]{2,1,0:T(8,128)(2,1)S(1)} collective-permute-done((bf16[4,32,896]{2,1,0:T(8,128)(2,1)S(1)}, bf16[4,32,896]{2,1,0:T(8,128)(2,1)S(1)}, u32[]{:S(2)}, u32[]{:S(2)}) %collective-permute-start.9) | collective-permute-done | bytes 229408 | tf_op jit(solution)/shard_map/ppermute | solution.py:270
  39.2 0.5 collective-permute-start.13
  39.7 0.5 collective-permute-start.11
  40.3 0.5 collective-permute-done.15.refs_2_
  40.7 0.5 collective-permute-start.7
  41.3 2.3 %project.5.refs_5_ = bf16[64,32,2048]{2,1,0:T(8,128)(2,1)S(1)} custom-call(bf16[8,32,896]{2,1,0:T(8,128)(2,1)S(1)} %get-tuple-element.46.refs_0_, bf16[4,32,896]{2,1,0:T(8,128)(2,1)S(1)} %collective-permute-done.9.refs_1_, bf16[4,32,896]{2,1,0:T(8,128)(2,1)S(1)} %collective-permute-done.15.refs_2_, bf16[896,2048]{1,0:T(8,128)(2,1)S(1)} %bitcast.3), custom_call_target="tpu_custom_call" | custom-call | flops 234881024 | tf_op jit(solution)/shard_map/project/pallas_call | solution.py:147
  43.6 2.4 %project.6.refs_5_ = bf16[64,32,2048]{2,1,0:T(8,128)(2,1)S(1)} custom-call(bf16[8,16,896]{2,1,0:T(8,128)(2,1)S(1)} %collective-permute-done.4.refs_0_, bf16[8,16,896]{2,1,0:T(8,128)(2,1)S(1)} %collective-permute-done.10.refs_1_, bf16[8,16,896]{2,1,0:T(8,128)(2,1)S(1)} %collective-permute-done.13.refs_2_, ...), custom_call_target="tpu_custom_call", output_to_operand_aliasing={{}: (5, {})} | custom-call | flops 234881024 | tf_op jit(solution)/shard_map/project/pallas_call | solution.py:147
  46.0 2.4 %project.7.refs_3_ = bf16[64,32,2048]{2,1,0:T(8,128)(2,1)S(1)} custom-call(bf16[4,32,896]{2,1,0:T(8,128)(2,1)S(1)} %collective-permute-done.5.refs_0_, bf16[4,32,896]{2,1,0:T(8,128)(2,1)S(1)} %collective-permute-done.8.refs_1_, bf16[4,32,896]{2,1,0:T(8,128)(2,1)S(1)} %collective-permute-done.11.refs_2_, ...), custom_call_target="tpu_custom_call", output_to_operand_aliasing={{}: (5, {})} | custom-call | flops 234881024 | tf_op jit(solution)/shard_map/project/pallas_call | solution.py:147
  48.4 0.6 collective-permute-start.16
  48.9 1.3 %project.8.refs_3_ = bf16[64,32,2048]{2,1,0:T(8,128)(2,1)S(1)} custom-call(bf16[8,16,896]{2,1,0:T(8,128)(2,1)S(1)} %collective-permute-done.6.refs_0_, bf16[8,16,896]{2,1,0:T(8,128)(2,1)S(1)} %collective-permute-done.17.refs_1_, bf16[896,2048]{1,0:T(8,128)(2,1)S(1)} %bitcast.6, bf16[64,32,2048]{2,1,0:T(8,128)(2,1)S(1)} %project.7.refs_3_), custom_call_target="tpu_custom_call", output_to_operand_aliasing={{}: (3, {})} | custom-call | flops 7516192768 | tf_op jit(solution)/shard_map/project/pallas_call | solution.py:147
  50.2 0.0 copy-start
  50.2 1.3 %project.9.held_ref = bf16[64,32,2048]{2,1,0:T(8,128)(2,1)S(1)} custom-call(bf16[8,16,896]{2,1,0:T(8,128)(2,1)S(1)} %collective-permute-done.7.refs_0_, bf16[8,16,896]{2,1,0:T(8,128)(2,1)S(1)} %collective-permute-done.16.refs_1_, bf16[896,2048]{1,0:T(8,128)(2,1)S(1)} %bitcast.7, bf16[64,32,2048]{2,1,0:T(8,128)(2,1)S(1)} %project.8.refs_3_), custom_call_target="tpu_custom_call", output_to_operand_aliasing={{}: (3, {})} | custom-call | flops 939524096 | tf_op jit(solution)/shard_map/project/pallas_call | solution.py:147
  51.5 0.9 %copy-done = bf16[2048,1024]{1,0:T(8,128)(2,1)S(1)} copy-done((bf16[2048,1024]{1,0:T(8,128)(2,1)S(1)}, bf16[2048,1024]{1,0:T(8,128)(2,1)}, u32[]{:S(2)}) %copy-start) | copy-done | bytes 4194328
  52.4 6.5 %attend.1 = bf16[2048,1024]{1,0:T(8,128)(2,1)} custom-call(s32[64]{0:T(128)S(1)} %copy-done.2, bf16[2048,1024]{1,0:T(8,128)(2,1)S(1)} %copy-done, bf16[64,32,2048]{2,1,0:T(8,128)(2,1)S(1)} %project.9.held_ref), custom_call_target="tpu_custom_call" | custom-call | flops 1000000000 | bytes 16777216 | tf_op jit(solution)/shard_map/attend/pallas_call | solution.py:213
  (20 shorter events, 0.1 us)
Async XLA Ops:
  0.0 24.1 %copy-start.1 = (s32[32,2]{0,1:T(2,128)S(1)}, s32[32,2]{0,1:T(2,128)}, u32[]{:S(2)}) copy-start(s32[32,2]{0,1:T(2,128)} %param.7) | copy-start | bytes 772
  0.0 5.9 %collective-permute-start = (s32[2,32]{1,0:T(2,128)}, s32[2,32]{1,0:T(2,128)S(1)}, u32[]{:S(2)}, u32[]{:S(2)}) collective-permute-start(s32[2,32]{1,0:T(2,128)} %bitcast.8), channel_id=1, source_target_pairs={{0,16},{1,21},{2,18},{3,23},{4,20},{5,17},{6,22},{7,19},{8,24},{9,... | collective-permute-start | bytes 776 | tf_op jit(solution)/shard_map/ppermute | solution.py:271
  4.0 3.8 %collective-permute-start.1 = (s32[2,32]{1,0:T(2,128)}, s32[2,32]{1,0:T(2,128)S(1)}, u32[]{:S(2)}, u32[]{:S(2)}) collective-permute-start(s32[2,32]{1,0:T(2,128)} %bitcast.9), channel_id=1, source_target_pairs={{0,8},{1,13},{2,10},{3,15},{4,12},{5,9},{6,14},{7,11},{8,0},{9,5},... | collective-permute-start | bytes 776 | tf_op jit(solution)/shard_map/ppermute | solution.py:271
  9.4 16.1 %collective-permute-start.4 = (bf16[8,16,896]{2,1,0:T(8,128)(2,1)S(1)}, bf16[8,16,896]{2,1,0:T(8,128)(2,1)S(1)}, u32[]{:S(2)}, u32[]{:S(2)}) collective-permute-start(bf16[8,16,896]{2,1,0:T(8,128)(2,1)S(1)} %get-tuple-element.27), channel_id=1, source_target_pairs={{0,16},{1,21},{2,18},{3,23},{4,20},{5,17},{6,22},{7,19},{8,24},{9,... | collective-permute-start | bytes 688136 | tf_op jit(solution)/shard_map/ppermute | solution.py:271
  10.4 15.1 %collective-permute-start.5 = (bf16[4,32,896]{2,1,0:T(8,128)(2,1)S(1)}, bf16[4,32,896]{2,1,0:T(8,128)(2,1)S(1)}, u32[]{:S(2)}, u32[]{:S(2)}) collective-permute-start(bf16[4,32,896]{2,1,0:T(8,128)(2,1)S(1)} %get-tuple-element.36), channel_id=1, source_target_pairs={{0,8},{1,13},{2,10},{3,15},{4,12},{5,9},{6,14},{7,11},{8,0},{9,5},... | collective-permute-start | bytes 688136 | tf_op jit(solution)/shard_map/ppermute | solution.py:271
  12.0 12.1 %collective-permute-start.2 = (s32[2,32]{1,0:T(2,128)}, s32[2,32]{1,0:T(2,128)S(1)}, u32[]{:S(2)}, u32[]{:S(2)}) collective-permute-start(s32[2,32]{1,0:T(2,128)} %bitcast.10), channel_id=1, source_target_pairs={{0,24},{1,29},{2,26},{3,31},{4,28},{5,25},{6,30},{7,27},{8,16},{9,... | collective-permute-start | bytes 776 | tf_op jit(solution)/shard_map/ppermute | solution.py:271
  13.9 10.2 %collective-permute-start.3 = (s32[2,32]{1,0:T(2,128)}, s32[2,32]{1,0:T(2,128)S(1)}, u32[]{:S(2)}, u32[]{:S(2)}) collective-permute-start(s32[2,32]{1,0:T(2,128)} %bitcast.11), channel_id=1, source_target_pairs={{0,4},{4,0},{8,12},{12,8},{16,20},{20,16},{24,28},{28,24},{1,5},{5... | collective-permute-start | bytes 776 | tf_op jit(solution)/shard_map/ppermute | solution.py:270
  25.5 7.6 %collective-permute-start.10 = (bf16[8,16,896]{2,1,0:T(8,128)(2,1)S(1)}, bf16[8,16,896]{2,1,0:T(8,128)(2,1)S(1)}, u32[]{:S(2)}, u32[]{:S(2)}) collective-permute-start(bf16[8,16,896]{2,1,0:T(8,128)(2,1)S(1)} %collective-permute-done.4.refs_0_), channel_id=1, source_target_pairs={{0,2},{1,3},{2,0},{3,1},{4,6},{5,7},{6,4},{7,5},{8,10},{9,11},{10,... | collective-permute-start | bytes 688136 | tf_op jit(solution)/shard_map/ppermute | solution.py:274
  27.0 7.5 %collective-permute-start.8 = (bf16[4,32,896]{2,1,0:T(8,128)(2,1)S(1)}, bf16[4,32,896]{2,1,0:T(8,128)(2,1)S(1)}, u32[]{:S(2)}, u32[]{:S(2)}) collective-permute-start(bf16[4,32,896]{2,1,0:T(8,128)(2,1)S(1)} %get-tuple-element.39), channel_id=1, source_target_pairs={{0,8},{1,13},{2,10},{3,15},{4,12},{5,9},{6,14},{7,11},{8,0},{9,5},... | collective-permute-start | bytes 688136 | tf_op jit(solution)/shard_map/ppermute | solution.py:271
  27.0 12.2 %collective-permute-start.9 = (bf16[4,32,896]{2,1,0:T(8,128)(2,1)S(1)}, bf16[4,32,896]{2,1,0:T(8,128)(2,1)S(1)}, u32[]{:S(2)}, u32[]{:S(2)}) collective-permute-start(bf16[4,32,896]{2,1,0:T(8,128)(2,1)S(1)} %get-tuple-element.40), channel_id=1, source_target_pairs={{0,4},{4,0},{8,12},{12,8},{16,20},{20,16},{24,28},{28,24},{1,5},{5... | collective-permute-start | bytes 688136 | tf_op jit(solution)/shard_map/ppermute | solution.py:270
  28.6 11.7 %collective-permute-start.6 = (bf16[8,16,896]{2,1,0:T(8,128)(2,1)S(1)}, bf16[8,16,896]{2,1,0:T(8,128)(2,1)S(1)}, u32[]{:S(2)}, u32[]{:S(2)}) collective-permute-start(bf16[8,16,896]{2,1,0:T(8,128)(2,1)S(1)} %get-tuple-element.37), channel_id=1, source_target_pairs={{0,24},{1,29},{2,26},{3,31},{4,28},{5,25},{6,30},{7,27},{8,16},{9,... | collective-permute-start | bytes 688136 | tf_op jit(solution)/shard_map/ppermute | solution.py:271
  39.2 1.5 %collective-permute-start.15 = (bf16[4,32,896]{2,1,0:T(8,128)(2,1)S(1)}, bf16[4,32,896]{2,1,0:T(8,128)(2,1)S(1)}, u32[]{:S(2)}, u32[]{:S(2)}) collective-permute-start(bf16[4,32,896]{2,1,0:T(8,128)(2,1)S(1)} %collective-permute-done.9.refs_1_), channel_id=1, source_target_pairs={{0,1},{1,0},{2,3},{3,2},{4,5},{5,4},{6,7},{7,6},{8,9},{9,8},{10,11... | collective-permute-start | bytes 688136 | tf_op jit(solution)/shard_map/ppermute | solution.py:274
  39.2 2.0 %collective-permute-start.13 = (bf16[8,16,896]{2,1,0:T(8,128)(2,1)S(1)}, bf16[8,16,896]{2,1,0:T(8,128)(2,1)S(1)}, u32[]{:S(2)}, u32[]{:S(2)}) collective-permute-start(bf16[8,16,896]{2,1,0:T(8,128)(2,1)S(1)} %collective-permute-done.4.refs_0_), channel_id=1, source_target_pairs={{0,1},{1,0},{2,3},{3,2},{4,5},{5,4},{6,7},{7,6},{8,9},{9,8},{10,11... | collective-permute-start | bytes 688136 | tf_op jit(solution)/shard_map/ppermute | solution.py:274
  39.7 3.9 %collective-permute-start.14 = (bf16[8,16,896]{2,1,0:T(8,128)(2,1)S(1)}, bf16[8,16,896]{2,1,0:T(8,128)(2,1)S(1)}, u32[]{:S(2)}, u32[]{:S(2)}) collective-permute-start(bf16[8,16,896]{2,1,0:T(8,128)(2,1)S(1)} %collective-permute-done.10.refs_1_), channel_id=1, source_target_pairs={{0,1},{1,0},{2,3},{3,2},{4,5},{5,4},{6,7},{7,6},{8,9},{9,8},{10,11... | collective-permute-start | bytes 688136 | tf_op jit(solution)/shard_map/ppermute | solution.py:274
  39.7 6.2 %collective-permute-start.11 = (bf16[4,32,896]{2,1,0:T(8,128)(2,1)S(1)}, bf16[4,32,896]{2,1,0:T(8,128)(2,1)S(1)}, u32[]{:S(2)}, u32[]{:S(2)}) collective-permute-start(bf16[4,32,896]{2,1,0:T(8,128)(2,1)S(1)} %collective-permute-done.5.refs_0_), channel_id=1, source_target_pairs={{0,1},{1,0},{2,3},{3,2},{4,5},{5,4},{6,7},{7,6},{8,9},{9,8},{10,11... | collective-permute-start | bytes 688136 | tf_op jit(solution)/shard_map/ppermute | solution.py:274
  40.2 5.7 %collective-permute-start.12 = (bf16[4,32,896]{2,1,0:T(8,128)(2,1)S(1)}, bf16[4,32,896]{2,1,0:T(8,128)(2,1)S(1)}, u32[]{:S(2)}, u32[]{:S(2)}) collective-permute-start(bf16[4,32,896]{2,1,0:T(8,128)(2,1)S(1)} %collective-permute-done.8.refs_1_), channel_id=1, source_target_pairs={{0,1},{1,0},{2,3},{3,2},{4,5},{5,4},{6,7},{7,6},{8,9},{9,8},{10,11... | collective-permute-start | bytes 688136 | tf_op jit(solution)/shard_map/ppermute | solution.py:274
  40.7 7.6 %collective-permute-start.7 = (bf16[8,16,896]{2,1,0:T(8,128)(2,1)S(1)}, bf16[8,16,896]{2,1,0:T(8,128)(2,1)S(1)}, u32[]{:S(2)}, u32[]{:S(2)}) collective-permute-start(bf16[8,16,896]{2,1,0:T(8,128)(2,1)S(1)} %collective-permute-done.6.refs_0_), channel_id=1, source_target_pairs={{0,2},{1,3},{2,0},{3,1},{4,6},{5,7},{6,4},{7,5},{8,10},{9,11},{10,... | collective-permute-start | bytes 688136 | tf_op jit(solution)/shard_map/ppermute | solution.py:274
  41.3 7.7 %collective-permute-start.17 = (bf16[8,16,896]{2,1,0:T(8,128)(2,1)S(1)}, bf16[8,16,896]{2,1,0:T(8,128)(2,1)S(1)}, u32[]{:S(2)}, u32[]{:S(2)}) collective-permute-start(bf16[8,16,896]{2,1,0:T(8,128)(2,1)S(1)} %collective-permute-done.6.refs_0_), channel_id=1, source_target_pairs={{0,1},{1,0},{2,3},{3,2},{4,5},{5,4},{6,7},{7,6},{8,9},{9,8},{10,11... | collective-permute-start | bytes 688136 | tf_op jit(solution)/shard_map/ppermute | solution.py:274
  48.4 1.9 %collective-permute-start.16 = (bf16[8,16,896]{2,1,0:T(8,128)(2,1)S(1)}, bf16[8,16,896]{2,1,0:T(8,128)(2,1)S(1)}, u32[]{:S(2)}, u32[]{:S(2)}) collective-permute-start(bf16[8,16,896]{2,1,0:T(8,128)(2,1)S(1)} %collective-permute-done.7.refs_0_), channel_id=1, source_target_pairs={{0,1},{1,0},{2,3},{3,2},{4,5},{5,4},{6,7},{7,6},{8,9},{9,8},{10,11... | collective-permute-start | bytes 688136 | tf_op jit(solution)/shard_map/ppermute | solution.py:274
  50.2 2.2 %copy-start = (bf16[2048,1024]{1,0:T(8,128)(2,1)S(1)}, bf16[2048,1024]{1,0:T(8,128)(2,1)}, u32[]{:S(2)}) copy-start(bf16[2048,1024]{1,0:T(8,128)(2,1)} %queries_ref.1) | copy-start | bytes 12582916
  50.2 2.2 %copy-start.2 = (s32[64]{0:T(128)S(1)}, s32[64]{0:T(128)}, u32[]{:S(2)}) copy-start(s32[64]{0:T(128)} %plan.1.slots_ref) | copy-start | bytes 772

commit v4 on v3

--- a/solution.py
+++ b/solution.py
@@ -10,6 +10,7 @@
 GROUP = 64
 HEAD_DIM = 128
 MIB = 1024 * 1024
+PACE = 2 * 10**9
 LIGHT = pl.CostEstimate(flops=1, bytes_accessed=1, transcendentals=0)
 
 
@@ -46,18 +47,16 @@
     )(ids)
 
 
-def pick_kernel(plans, keep, *refs):
+def pick_kernel(plans, *refs):
     count = len(plans)
-    asked, stored_ref, pieces = refs[:count], refs[count], refs[count + 1 : -4]
-    here_ref = refs[-5] if keep else stored_ref
-    ids_at, table_ref, ids_sem, sem = refs[-4:]
+    asked, stored_ref, pieces = refs[:count], refs[count], refs[count + 1 : -5]
+    here_ref, ids_at, table_ref, ids_sem, sem = refs[-5:]
     tile_count, rows, _ = stored_ref.shape
     fetches = [pltpu.make_async_copy(ref, ids_at.at[i], ids_sem.at[i]) for i, ref in enumerate(asked)]
     for fetch in fetches:
         fetch.start()
-    if keep:
-        load = pltpu.make_async_copy(stored_ref, here_ref, sem)
-        load.start()
+    load = pltpu.make_async_copy(stored_ref, here_ref, sem)
+    load.start()
     lowest, mp_at = lax.axis_index("seq") * tile_count, lax.axis_index("mp")
     half = pl.multiple_of(mp_at // 2 * (rows // 2), rows // 2)
     for i in range(count):
@@ -68,8 +67,7 @@
                 local = ids_at[i, k, c] - lowest
                 table_ref[i, found] = local
                 found += ((local >= 0) & (local < tile_count)).astype(jnp.int32)
-    if keep:
-        load.wait()
+    load.wait()
     at = 0
     for i, (kind, sizes) in enumerate(plans):
         rank = (mp_at % 2) * sizes[0] if kind == "tiles" else 0
@@ -81,43 +79,45 @@
             at += 1
 
 
-def pick(asked, stored, plans, keep):
+def pick(asked, own, stored, plans):
     _, rows, width = stored.shape
-    vmem = pl.BlockSpec(memory_space=pltpu.VMEM)
+    vmem, anywhere = pl.BlockSpec(memory_space=pltpu.VMEM), pl.BlockSpec(memory_space=pl.ANY)
     shapes = [(size, rows // 2 if kind == "rows" else rows, width) for kind, sizes in plans for size in sizes]
-    shapes += [stored.shape] * keep
-    ids = asked[0]
-    return pl.pallas_call(
-        functools.partial(pick_kernel, plans, keep),
+    return pl.pallas_call(
+        functools.partial(pick_kernel, plans),
         out_shape=[pltpu.VMEM(shape, stored.dtype) for shape in shapes],
-        in_specs=[vmem] * len(asked) + [pl.BlockSpec(memory_space=pl.ANY) if keep else vmem],
+        in_specs=[vmem] * len(asked) + [anywhere, anywhere],
         out_specs=[vmem] * len(shapes),
         scratch_shapes=[
-            pltpu.SMEM((len(asked), *ids.shape), jnp.int32),
-            pltpu.SMEM((len(asked), ids.size + 1), jnp.int32),
-            pltpu.SemaphoreType.DMA((len(asked),)),
+            pltpu.VMEM(stored.shape, stored.dtype),
+            pltpu.SMEM((len(plans), *own.shape), jnp.int32),
+            pltpu.SMEM((len(plans), own.size + 1), jnp.int32),
+            pltpu.SemaphoreType.DMA((len(plans),)),
             pltpu.SemaphoreType.DMA,
         ],
-        compiler_params=pltpu.CompilerParams(vmem_limit_bytes=(52 if keep else 16) * MIB),
+        compiler_params=pltpu.CompilerParams(vmem_limit_bytes=52 * MIB),
         cost_estimate=LIGHT,
         name="pick",
-    )(*[in_vmem(a) for a in asked], stored)
-
-
-def pace_kernel(slots_ref, turn_ref):
-    turn_ref[0] = slots_ref[0]
-
-
-def pace(slots):
-    smem = pl.BlockSpec(memory_space=pltpu.SMEM)
-    return pl.pallas_call(
-        pace_kernel,
-        out_shape=jax.ShapeDtypeStruct((1,), jnp.int32),
-        in_specs=[smem],
-        out_specs=smem,
-        cost_estimate=pl.CostEstimate(flops=3 * 10**9, bytes_accessed=0, transcendentals=0),
-        name="pace",
-    )(slots)
+    )(*[in_vmem(a) for a in asked], own, stored)
+
+
+def turn_kernel(*refs):
+    pass
+
+
+def turn(values, others, flops):
+    vmem = pl.BlockSpec(memory_space=pltpu.VMEM)
+    count = len(values)
+    return pl.pallas_call(
+        turn_kernel,
+        out_shape=[pltpu.VMEM(v.shape, v.dtype) for v in values],
+        in_specs=[vmem] * count + [pl.BlockSpec(memory_space=pl.ANY)] * len(others),
+        out_specs=[vmem] * count,
+        input_output_aliases={i: i for i in range(count)},
+        compiler_params=pltpu.CompilerParams(vmem_limit_bytes=16 * MIB),
+        cost_estimate=pl.CostEstimate(flops=flops, bytes_accessed=1, transcendentals=0),
+        name="turn",
+    )(*[in_vmem(v) for v in values], *others)
 
 
 def project_kernel(places, *refs):
@@ -273,8 +273,6 @@
     def over_mp(value, flip):
         return lax.ppermute(value, "mp", [(m, m ^ flip) for m in range(mp_count)])
 
-    def after(value, *others):
-        return lax.optimization_barrier((value, *others))[0]
 
     ids = retrieved.T
     size = capacity // 2
@@ -288,49 +286,38 @@
             (first + capacity, rows // 2, over_mp(theirs, 1)),
         ]
 
-    asked = [across(ids, p) for p in (2, 1)]
-    picked2, *picked1, stored = pick(asked, encoded, [("rows", [capacity]), ("all", [size, size])], True)
-    got2, got1 = across(picked2, 2), across(picked1[0], 1)
-    ids, w_kv = after(ids, picked2), after(w_kv, picked2)
+    asked = [across(ids, p) for p in (2, 3, 1, 0)]
+    kinds = [("rows", [capacity]), ("rows", [capacity]), ("all", [size, size]), ("tiles", [size]), ("all", [capacity])]
+    picked2, picked3, *picked1, beside, own = pick(asked, ids, encoded, kinds)
+    got2, got1, beside = across(picked2, 2), across(picked1[0], 1), across(beside, 0)
     weights = in_vmem(w_kv.reshape(width, -1))
     slots = plan(ids, tile_count, capacity)
-    asked = lax.optimization_barrier((across(ids, 3), across(ids, 0), weights, slots))[:2]
-    picked3, beside, own = pick(
-        [*asked, ids], stored, [("rows", [capacity]), ("tiles", [size]), ("all", [capacity])], False
-    )
-    picked3, picked1[1], beside, got2, got1 = lax.optimization_barrier((picked3, picked1[1], beside, got2, got1))
-    got3 = across(picked3, 3)
-    rest1 = across(picked1[1], 1)
-    theirs2 = over_mp(got2, 2)
-    beside = across(beside, 0)
     shape = (ref_count, rows, weights.shape[1])
+
+    def add(held, pieces, weight):
+        return project(pieces, weights, held, shape, weight)
+
+    def core(value, tile, row, cuts):
+        step = value.shape[0] // cuts
+        return [(tile + at, row, over_mp(value[at : at + step], 1)) for at in range(0, value.shape[0], step)]
+
+    at1, at2, at3 = 2 * capacity, 4 * capacity, 6 * capacity
+    held = add(None, [(0, 0, own)], 1)
+    picked3 = turn([picked3], [got2, held, slots], PACE)[0]
+    next1, beside, got1, got2 = turn([picked1[1], beside, got1, got2], [picked3], 1)
+    got3, rest1, theirs2 = across(picked3, 3), across(next1, 1), over_mp(got2, 2)
+    held = add(held, [(capacity, 0, beside), *core(beside, capacity + size, 0, 2)], 1)
+    held = add(held, [(at2, 0, got2), *core(got2, at2 + capacity, 0, 2)], 1)
+    held = add(held, [(at1, 0, got1), *core(got1, at1 + capacity, 0, 2)], 1)
+    got3 = turn([got3], [held], PACE)[0]
     theirs3 = over_mp(got3, 2)
-    turn = pace(after(slots, got3))
-    got1, rest1, beside, got2, theirs2 = lax.optimization_barrier((got1, rest1, beside, got2, theirs2, turn))[:5]
-    first = 4 * capacity
-    part2 = [
-        (first, 0, got2),
-        (first, rows // 2, theirs2),
-        (first + capacity, 0, over_mp(got2, 1)),
-        (first + capacity, rows // 2, over_mp(theirs2, 1)),
-    ]
-    first = 2 * capacity
-    part1 = [
-        (first, 0, got1),
-        (first + size, 0, rest1),
-        (first + capacity, 0, over_mp(got1, 1)),
-        (first + capacity + size, 0, over_mp(rest1, 1)),
-    ]
-    part0 = [(0, 0, own), (capacity, 0, beside), (capacity + size, 0, over_mp(beside, 1))]
-    held = None
-    for pieces in (part0, part2, part1):
-        held = project(pieces, weights, held, shape, 1)
-    theirs3 = after(theirs3, held)
-    first = 6 * capacity
-    part3 = [(first, 0, got3), (first + capacity, 0, over_mp(got3, 1))]
-    rest3 = [(first, rows // 2, theirs3), (first + capacity, rows // 2, over_mp(theirs3, 1))]
-    held = project(part3, weights, held, shape, 64)
-    held = project(rest3, weights, held, shape, 8)
+    theirs2 = turn([theirs2], [got3], 1)[0]
+    rest1 = turn([rest1], [theirs2], 1)[0]
+    held = add(held, [(at2, rows // 2, theirs2), *core(theirs2, at2 + capacity, rows // 2, 2)], 1)
+    held = add(held, [(at1 + size, 0, rest1), *core(rest1, at1 + capacity + size, 0, 2)], 1)
+    theirs3 = turn([theirs3], [held], 1)[0]
+    held = add(held, [(at3, 0, got3), *core(got3, at3 + capacity, 0, 2)], 64)
+    held = add(held, [(at3, rows // 2, theirs3), *core(theirs3, at3 + capacity, rows // 2, 1)], 64)
     return attend(queries, held, slots, queries.shape[1] // HEAD_DIM)
 
 

time: 59.1 us -> 55.6 us (0.941)
  waiting for transfers between devices: 16.3 us -> 9.34 us
  starting transfers between devices: 17.6 us -> 20.8 us
  local copies, waits for them, and re-layouts: 4.17 us -> 4.89 us
  Pallas kernels: 20.7 us -> 20.1 us
    ppermute x2, waiting for transfers between devices: 4.73 us -> 0.01 us  [across(): return lax.ppermute(value, 'seq', [(s, s ^ 1) for s in range(seq_count)])]
    ppermute x9 -> x15, waiting for transfers between devices: 4.21 us -> 0.56 us  [over_mp(): return lax.ppermute(value, 'mp', [(m, m ^ flip) for m in range(mp_count)])]
    ppermute x9 -> x15, starting transfers between devices: 3.68 us -> 6.49 us  [over_mp(): return lax.ppermute(value, 'mp', [(m, m ^ flip) for m in range(mp_count)])]
    ppermute x7, waiting for transfers between devices: 7.4 us -> 8.77 us  [across(): lax.ppermute(value, both, joint(lambda s, m: (s ^ 2 * part ^ m % 2) * mp_...]
    pallas_call x2 -> x7, Pallas kernels: 2.95 us -> 1.98 us  [the longest x1 1.97 us: pick(): pl.pallas_call(functools.partial(pick_kernel, plans), out_shape=[pltpu.VM...]
    unnamed x7, local copies, waits for them, and re-layouts: 4.17 us -> 4.77 us
    pallas_call x5 -> x8, Pallas kernels: 9.57 us -> 10.1 us  [project(): pl.pallas_call(functools.partial(project_kernel, [(tile, row) for tile, r...]
  transfers between devices with their start and end apart: 18 -> 24, of which waited for: 7 -> 8; matrix products, arithmetic and copies ran while one was open for 6% -> 6% of each run, Pallas kernels for 19% -> 19%
where the time goes in v4:
time: 55.6 us; the launch traced here: 55.4 us
  starting transfers between devices  20.8 us (37%)
  Pallas kernels  20.1 us (36%)
  waiting for transfers between devices  9.34 us (17%)
  local copies, waits for them, and re-layouts  4.89 us (9%)
    ppermute x7, starting transfers between devices, across(): lax.ppermute(value, both, joint(lambda s, m: (s ^ 2 * part ^ m % 2) * mp_...  11.3 us
    pallas_call x8, Pallas kernels, project(): pl.pallas_call(functools.partial(project_kernel, [(tile, row) for tile, r...  10.1 us
    ppermute x7, waiting for transfers between devices, across(): lax.ppermute(value, both, joint(lambda s, m: (s ^ 2 * part ^ m % 2) * mp_...  8.77 us
    pallas_call x1, Pallas kernels, attend(): pl.pallas_call(functools.partial(attend_kernel, heads, many), out_shape=j...  6.52 us
    ppermute x15, starting transfers between devices, over_mp(): return lax.ppermute(value, 'mp', [(m, m ^ flip) for m in range(mp_count)])  6.49 us
    unnamed x7, local copies, waits for them, and re-layouts  4.77 us
    ppermute x2, starting transfers between devices, across(): return lax.ppermute(value, 'seq', [(s, s ^ 1) for s in range(seq_count)])  3.04 us
    pallas_call x1, Pallas kernels, pick(): pl.pallas_call(functools.partial(pick_kernel, plans), out_shape=[pltpu.VM...  1.97 us
  transfers between devices with their start and end apart: 24, of which 8 were waited for; matrix products, arithmetic and copies ran while one was open for 6% of the time, Pallas kernels for 19%

profile of v4, /device:TPU:0, one launch (start us, length us, event | category | flops | bytes accessed | tf_op | source)
XLA Modules:
  0.0 55.4 jit_solution(16633120891974523094)
XLA Ops:
  0.0 4.0 %collective-permute-start = (s32[2,32]{1,0:T(2,128)}, s32[2,32]{1,0:T(2,128)S(1)}, u32[]{:S(2)}, u32[]{:S(2)}) collective-permute-start(s32[2,32]{1,0:T(2,128)} %bitcast.11), channel_id=1, source_target_pairs={{0,16},{1,21},{2,18},{3,23},{4,20},{5,17},{6,22},{7,19},{8,24},{9,... | collective-permute-start | bytes 776 | tf_op jit(solution)/shard_map/ppermute | solution.py:271
  4.0 1.3 %collective-permute-start.1 = (s32[2,32]{1,0:T(2,128)}, s32[2,32]{1,0:T(2,128)S(1)}, u32[]{:S(2)}, u32[]{:S(2)}) collective-permute-start(s32[2,32]{1,0:T(2,128)} %bitcast.12), channel_id=1, source_target_pairs={{0,24},{1,29},{2,26},{3,31},{4,28},{5,25},{6,30},{7,27},{8,16},{9,... | collective-permute-start | bytes 776 | tf_op jit(solution)/shard_map/ppermute | solution.py:271
  5.6 1.5 %collective-permute-start.3 = (s32[2,32]{1,0:T(2,128)}, s32[2,32]{1,0:T(2,128)S(1)}, u32[]{:S(2)}, u32[]{:S(2)}) collective-permute-start(s32[2,32]{1,0:T(2,128)} %bitcast.14), channel_id=1, source_target_pairs={{0,4},{4,0},{8,12},{12,8},{16,20},{20,16},{24,28},{28,24},{1,5},{5... | collective-permute-start | bytes 776 | tf_op jit(solution)/shard_map/ppermute | solution.py:270
  7.1 2.5 %collective-permute-done.1.refs_1_ = s32[2,32]{1,0:T(2,128)S(1)} collective-permute-done((s32[2,32]{1,0:T(2,128)}, s32[2,32]{1,0:T(2,128)S(1)}, u32[]{:S(2)}, u32[]{:S(2)}) %collective-permute-start.1) | collective-permute-done | bytes 288 | tf_op jit(solution)/shard_map/ppermute | solution.py:271
  9.6 0.7 %copy-done.2 = s32[32,2]{0,1:T(2,128)S(1)} copy-done((s32[32,2]{0,1:T(2,128)S(1)}, s32[32,2]{0,1:T(2,128)}, u32[]{:S(2)}) %copy-start.2) | copy-done | bytes 280
  10.3 2.0 %pick.1 = (bf16[8,16,896]{2,1,0:T(8,128)(2,1)S(1)}, bf16[8,16,896]{2,1,0:T(8,128)(2,1)S(1)}, bf16[4,32,896]{2,1,0:T(8,128)(2,1)S(1)}, bf16[4,32,896]{2,1,0:T(8,1...) custom-call(s32[2,32]{1,0:T(2,128)S(1)} %collective-permute-done.refs_0_, ...), custom_call_target="tpu_custom_call" | custom-call | flops 1 | bytes 1 | tf_op jit(solution)/shard_map/pick/pallas_call | solution.py:86
  12.3 2.6 %collective-permute-start.4 = (bf16[8,16,896]{2,1,0:T(8,128)(2,1)S(1)}, bf16[8,16,896]{2,1,0:T(8,128)(2,1)S(1)}, u32[]{:S(2)}, u32[]{:S(2)}) collective-permute-start(bf16[8,16,896]{2,1,0:T(8,128)(2,1)S(1)} %get-tuple-element.16), channel_id=1, source_target_pairs={{0,16},{1,21},{2,18},{3,23},{4,20},{5,17},{6,22},{7,19},{8,24},{9,... | collective-permute-start | bytes 688136 | tf_op jit(solution)/shard_map/ppermute | solution.py:271
  14.9 1.5 %collective-permute-start.6 = (bf16[4,32,896]{2,1,0:T(8,128)(2,1)S(1)}, bf16[4,32,896]{2,1,0:T(8,128)(2,1)S(1)}, u32[]{:S(2)}, u32[]{:S(2)}) collective-permute-start(bf16[4,32,896]{2,1,0:T(8,128)(2,1)S(1)} %get-tuple-element.19), channel_id=1, source_target_pairs={{0,4},{4,0},{8,12},{12,8},{16,20},{20,16},{24,28},{28,24},{1,5},{5... | collective-permute-start | bytes 688136 | tf_op jit(solution)/shard_map/ppermute | solution.py:270
  16.5 0.7 %collective-permute-start.7 = (bf16[4,32,896]{2,1,0:T(8,128)(2,1)S(1)}, bf16[4,32,896]{2,1,0:T(8,128)(2,1)S(1)}, u32[]{:S(2)}, u32[]{:S(2)}) collective-permute-start(bf16[4,32,896]{2,1,0:T(8,128)(2,1)S(1)} %get-tuple-element.20), channel_id=1, source_target_pairs={{0,8},{1,13},{2,10},{3,15},{4,12},{5,9},{6,14},{7,11},{8,0},{9,5},... | collective-permute-start | bytes 688136 | tf_op jit(solution)/shard_map/ppermute | solution.py:271
  17.1 1.6 %plan.1.refs_3_.slots_ref = s32[64]{0:T(128)} custom-call(s32[2,32]{1,0:T(2,128)} %bitcast.15), custom_call_target="tpu_custom_call" | custom-call | flops 1 | bytes 1 | tf_op jit(solution)/shard_map/plan/pallas_call | solution.py:40
  18.7 3.3 %copy.21 = bf16[112,8,2,1024]{3,1,2,0:T(8,128)(2,1)S(1)} copy(bf16[112,8,2,1024]{3,2,1,0:T(2,128)(2,1)} %bitcast.17) | data formatting | bytes 7340032
  22.0 1.3 %project.8.refs_2_.refs_4_ = bf16[64,32,2048]{2,1,0:T(8,128)(2,1)S(1)} custom-call(bf16[8,32,896]{2,1,0:T(8,128)(2,1)S(1)} %get-tuple-element.17.refs_0_, bf16[896,2048]{1,0:T(8,128)(2,1)S(1)} %bitcast.3), custom_call_target="tpu_custom_call" | custom-call | flops 117440512 | tf_op jit(solution)/shard_map/project/pallas_call | solution.py:147
  23.3 3.1 %collective-permute-done.4.refs_1_.refs_3_ = bf16[8,16,896]{2,1,0:T(8,128)(2,1)S(1)} collective-permute-done((bf16[8,16,896]{2,1,0:T(8,128)(2,1)S(1)}, bf16[8,16,896]{2,1,0:T(8,128)(2,1)S(1)}, u32[]{:S(2)}, u32[]{:S(2)}) %collective-permute-start.4) | collective-permute-done | bytes 229408 | tf_op jit(solution)/shard_map/ppermute | solution.py:271
  26.4 2.3 %collective-permute-start.5 = (bf16[8,16,896]{2,1,0:T(8,128)(2,1)S(1)}, bf16[8,16,896]{2,1,0:T(8,128)(2,1)S(1)}, u32[]{:S(2)}, u32[]{:S(2)}) collective-permute-start(bf16[8,16,896]{2,1,0:T(8,128)(2,1)S(1)} %turn.6.refs_4_), channel_id=1, source_target_pairs={{0,24},{1,29},{2,26},{3,31},{4,28},{5,25},{6,30},{7,27},{8,16},{9,... | collective-permute-start | bytes 688136 | tf_op jit(solution)/shard_map/ppermute | solution.py:271
  28.9 0.4 collective-permute-start.13
  29.5 0.4 collective-permute-start.11
  30.7 1.5 %collective-permute-start.16 = (bf16[8,16,896]{2,1,0:T(8,128)(2,1)S(1)}, bf16[8,16,896]{2,1,0:T(8,128)(2,1)S(1)}, u32[]{:S(2)}, u32[]{:S(2)}) collective-permute-start(bf16[8,16,896]{2,1,0:T(8,128)(2,1)S(1)} %get-tuple-element.22.refs_0_), channel_id=1, source_target_pairs={{0,2},{1,3},{2,0},{3,1},{4,6},{5,7},{6,4},{7,5},{8,10},{9,11},{10,... | collective-permute-start | bytes 688136 | tf_op jit(solution)/shard_map/ppermute | solution.py:274
  32.2 1.3 %project.9.refs_4_ = bf16[64,32,2048]{2,1,0:T(8,128)(2,1)S(1)} custom-call(bf16[4,32,896]{2,1,0:T(8,128)(2,1)S(1)} %get-tuple-element.23.refs_0_, bf16[2,32,896]{2,1,0:T(8,128)(2,1)S(1)} %collective-permute-done.12.refs_1_, bf16[2,32,896]{2,1,0:T(8,128)(2,1)S(1)} %collective-permute-done.13.refs_2_, ...), custom_call_target="tpu_custom_call", output_to_operand_aliasing={{}: (4, {})} | custom-call | flops 117440512 | tf_op jit(solution)/shard_map/project/pallas_call | solution.py:147
  33.6 1.3 %project.10.refs_4_ = bf16[64,32,2048]{2,1,0:T(8,128)(2,1)S(1)} custom-call(bf16[8,16,896]{2,1,0:T(8,128)(2,1)S(1)} %get-tuple-element.22.refs_0_, bf16[4,16,896]{2,1,0:T(8,128)(2,1)S(1)} %collective-permute-done.10.refs_1_, bf16[4,16,896]{2,1,0:T(8,128)(2,1)S(1)} %collective-permute-done.11.refs_2_, ...), custom_call_target="tpu_custom_call", output_to_operand_aliasing={{}: (4, {})} | custom-call | flops 117440512 | tf_op jit(solution)/shard_map/project/pallas_call | solution.py:147
  34.9 1.3 %project.11.refs_1_.refs_4_ = bf16[64,32,2048]{2,1,0:T(8,128)(2,1)S(1)} custom-call(bf16[4,32,896]{2,1,0:T(8,128)(2,1)S(1)} %get-tuple-element.21.refs_0_, bf16[2,32,896]{2,1,0:T(8,128)(2,1)S(1)} %collective-permute-done.8.refs_1_, bf16[2,32,896]{2,1,0:T(8,128)(2,1)S(1)} %collective-permute-done.9.refs_2_, ...), custom_call_target="tpu_custom_call", output_to_operand_aliasing={{}: (4, {})} | custom-call | flops 117440512 | tf_op jit(solution)/shard_map/project/pallas_call | solution.py:147
  36.1 0.6 %collective-permute-done.5.refs_0_ = bf16[8,16,896]{2,1,0:T(8,128)(2,1)S(1)} collective-permute-done((bf16[8,16,896]{2,1,0:T(8,128)(2,1)S(1)}, bf16[8,16,896]{2,1,0:T(8,128)(2,1)S(1)}, u32[]{:S(2)}, u32[]{:S(2)}) %collective-permute-start.5) | collective-permute-done | bytes 229408 | tf_op jit(solution)/shard_map/ppermute | solution.py:271
  36.8 1.5 %collective-permute-start.14 = (bf16[8,16,896]{2,1,0:T(8,128)(2,1)S(1)}, bf16[8,16,896]{2,1,0:T(8,128)(2,1)S(1)}, u32[]{:S(2)}, u32[]{:S(2)}) collective-permute-start(bf16[8,16,896]{2,1,0:T(8,128)(2,1)S(1)} %turn.8.refs_1_.refs_0_), channel_id=1, source_target_pairs={{0,2},{1,3},{2,0},{3,1},{4,6},{5,7},{6,4},{7,5},{8,10},{9,11},{10,... | collective-permute-start | bytes 688136 | tf_op jit(solution)/shard_map/ppermute | solution.py:274
  38.5 0.5 collective-permute-start.20
  39.0 2.5 %collective-permute-done.15.refs_0_ = bf16[4,32,896]{2,1,0:T(8,128)(2,1)S(1)} collective-permute-done((bf16[4,32,896]{2,1,0:T(8,128)(2,1)S(1)}, bf16[4,32,896]{2,1,0:T(8,128)(2,1)S(1)}, u32[]{:S(2)}, u32[]{:S(2)}) %collective-permute-start.15) | collective-permute-done | bytes 229408 | tf_op jit(solution)/shard_map/ppermute | solution.py:271
  41.6 0.5 collective-permute-start.18
  42.3 0.4 collective-permute-start.23
  42.7 1.2 %project.12.refs_4_ = bf16[64,32,2048]{2,1,0:T(8,128)(2,1)S(1)} custom-call(bf16[8,16,896]{2,1,0:T(8,128)(2,1)S(1)} %turn.9.refs_1_.refs_0_, bf16[4,16,896]{2,1,0:T(8,128)(2,1)S(1)} %collective-permute-done.19.refs_1_, bf16[4,16,896]{2,1,0:T(8,128)(2,1)S(1)} %collective-permute-done.20.refs_2_, ...), custom_call_target="tpu_custom_call", output_to_operand_aliasing={{}: (4, {})} | custom-call | flops 117440512 | tf_op jit(solution)/shard_map/project/pallas_call | solution.py:147
  44.0 1.2 %project.13.refs_1_.refs_4_ = bf16[64,32,2048]{2,1,0:T(8,128)(2,1)S(1)} custom-call(bf16[4,32,896]{2,1,0:T(8,128)(2,1)S(1)} %turn.10.refs_0_, bf16[2,32,896]{2,1,0:T(8,128)(2,1)S(1)} %collective-permute-done.17.refs_1_, bf16[2,32,896]{2,1,0:T(8,128)(2,1)S(1)} %collective-permute-done.18.refs_2_, ...), custom_call_target="tpu_custom_call", output_to_operand_aliasing={{}: (4, {})} | custom-call | flops 117440512 | tf_op jit(solution)/shard_map/project/pallas_call | solution.py:147
  45.4 1.3 %project.14.refs_3_ = bf16[64,32,2048]{2,1,0:T(8,128)(2,1)S(1)} custom-call(bf16[8,16,896]{2,1,0:T(8,128)(2,1)S(1)} %turn.8.refs_1_.refs_0_, bf16[4,16,896]{2,1,0:T(8,128)(2,1)S(1)} %collective-permute-done.22.refs_1_, bf16[4,16,896]{2,1,0:T(8,128)(2,1)S(1)} %collective-permute-done.23.refs_2_, ...), custom_call_target="tpu_custom_call", output_to_operand_aliasing={{}: (4, {})} | custom-call | flops 7516192768 | tf_op jit(solution)/shard_map/project/pallas_call | solution.py:147
  46.8 1.2 %project.15.held_ref = bf16[64,32,2048]{2,1,0:T(8,128)(2,1)S(1)} custom-call(bf16[8,16,896]{2,1,0:T(8,128)(2,1)S(1)} %turn.11.refs_0_, bf16[8,16,896]{2,1,0:T(8,128)(2,1)S(1)} %collective-permute-done.21.refs_1_, bf16[896,2048]{1,0:T(8,128)(2,1)S(1)} %bitcast.10, bf16[64,32,2048]{2,1,0:T(8,128)(2,1)S(1)} %project.14.refs_3_), custom_call_target="tpu_custom_call", output_to_operand_aliasing={{}: (3, {})} | custom-call | flops 7516192768 | tf_op jit(solution)/shard_map/project/pallas_call | solution.py:147
  48.1 0.8 %copy-done = bf16[2048,1024]{1,0:T(8,128)(2,1)S(1)} copy-done((bf16[2048,1024]{1,0:T(8,128)(2,1)S(1)}, bf16[2048,1024]{1,0:T(8,128)(2,1)}, u32[]{:S(2)}) %copy-start) | copy-done | bytes 4194328
  48.9 6.5 %attend.1 = bf16[2048,1024]{1,0:T(8,128)(2,1)} custom-call(s32[64]{0:T(128)S(1)} %copy-done.1, bf16[2048,1024]{1,0:T(8,128)(2,1)S(1)} %copy-done, bf16[64,32,2048]{2,1,0:T(8,128)(2,1)S(1)} %project.15.held_ref), custom_call_target="tpu_custom_call" | custom-call | flops 1000000000 | bytes 16777216 | tf_op jit(solution)/shard_map/attend/pallas_call | solution.py:213
  (46 shorter events, 2.2 us)
Async XLA Ops:
  0.0 7.1 %collective-permute-start = (s32[2,32]{1,0:T(2,128)}, s32[2,32]{1,0:T(2,128)S(1)}, u32[]{:S(2)}, u32[]{:S(2)}) collective-permute-start(s32[2,32]{1,0:T(2,128)} %bitcast.11), channel_id=1, source_target_pairs={{0,16},{1,21},{2,18},{3,23},{4,20},{5,17},{6,22},{7,19},{8,24},{9,... | collective-permute-start | bytes 776 | tf_op jit(solution)/shard_map/ppermute | solution.py:271
  4.0 5.6 %collective-permute-start.1 = (s32[2,32]{1,0:T(2,128)}, s32[2,32]{1,0:T(2,128)S(1)}, u32[]{:S(2)}, u32[]{:S(2)}) collective-permute-start(s32[2,32]{1,0:T(2,128)} %bitcast.12), channel_id=1, source_target_pairs={{0,24},{1,29},{2,26},{3,31},{4,28},{5,25},{6,30},{7,27},{8,16},{9,... | collective-permute-start | bytes 776 | tf_op jit(solution)/shard_map/ppermute | solution.py:271
  5.4 4.2 %collective-permute-start.2 = (s32[2,32]{1,0:T(2,128)}, s32[2,32]{1,0:T(2,128)S(1)}, u32[]{:S(2)}, u32[]{:S(2)}) collective-permute-start(s32[2,32]{1,0:T(2,128)} %bitcast.13), channel_id=1, source_target_pairs={{0,8},{1,13},{2,10},{3,15},{4,12},{5,9},{6,14},{7,11},{8,0},{9,5},... | collective-permute-start | bytes 776 | tf_op jit(solution)/shard_map/ppermute | solution.py:271
  5.6 4.0 %collective-permute-start.3 = (s32[2,32]{1,0:T(2,128)}, s32[2,32]{1,0:T(2,128)S(1)}, u32[]{:S(2)}, u32[]{:S(2)}) collective-permute-start(s32[2,32]{1,0:T(2,128)} %bitcast.14), channel_id=1, source_target_pairs={{0,4},{4,0},{8,12},{12,8},{16,20},{20,16},{24,28},{28,24},{1,5},{5... | collective-permute-start | bytes 776 | tf_op jit(solution)/shard_map/ppermute | solution.py:270
  9.6 0.7 %copy-start.2 = (s32[32,2]{0,1:T(2,128)S(1)}, s32[32,2]{0,1:T(2,128)}, u32[]{:S(2)}) copy-start(s32[32,2]{0,1:T(2,128)} %param.7) | copy-start | bytes 772
  12.3 14.1 %collective-permute-start.4 = (bf16[8,16,896]{2,1,0:T(8,128)(2,1)S(1)}, bf16[8,16,896]{2,1,0:T(8,128)(2,1)S(1)}, u32[]{:S(2)}, u32[]{:S(2)}) collective-permute-start(bf16[8,16,896]{2,1,0:T(8,128)(2,1)S(1)} %get-tuple-element.16), channel_id=1, source_target_pairs={{0,16},{1,21},{2,18},{3,23},{4,20},{5,17},{6,22},{7,19},{8,24},{9,... | collective-permute-start | bytes 688136 | tf_op jit(solution)/shard_map/ppermute | solution.py:271
  14.9 13.8 %collective-permute-start.6 = (bf16[4,32,896]{2,1,0:T(8,128)(2,1)S(1)}, bf16[4,32,896]{2,1,0:T(8,128)(2,1)S(1)}, u32[]{:S(2)}, u32[]{:S(2)}) collective-permute-start(bf16[4,32,896]{2,1,0:T(8,128)(2,1)S(1)} %get-tuple-element.19), channel_id=1, source_target_pairs={{0,4},{4,0},{8,12},{12,8},{16,20},{20,16},{24,28},{28,24},{1,5},{5... | collective-permute-start | bytes 688136 | tf_op jit(solution)/shard_map/ppermute | solution.py:270
  16.5 12.2 %collective-permute-start.7 = (bf16[4,32,896]{2,1,0:T(8,128)(2,1)S(1)}, bf16[4,32,896]{2,1,0:T(8,128)(2,1)S(1)}, u32[]{:S(2)}, u32[]{:S(2)}) collective-permute-start(bf16[4,32,896]{2,1,0:T(8,128)(2,1)S(1)} %get-tuple-element.20), channel_id=1, source_target_pairs={{0,8},{1,13},{2,10},{3,15},{4,12},{5,9},{6,14},{7,11},{8,0},{9,5},... | collective-permute-start | bytes 688136 | tf_op jit(solution)/shard_map/ppermute | solution.py:271
  18.7 7.7 %copy-start.1 = (s32[64]{0:T(128)S(1)}, s32[64]{0:T(128)}, u32[]{:S(2)}) copy-start(s32[64]{0:T(128)} %plan.1.refs_3_.slots_ref) | copy-start | bytes 772
  26.4 10.3 %collective-permute-start.5 = (bf16[8,16,896]{2,1,0:T(8,128)(2,1)S(1)}, bf16[8,16,896]{2,1,0:T(8,128)(2,1)S(1)}, u32[]{:S(2)}, u32[]{:S(2)}) collective-permute-start(bf16[8,16,896]{2,1,0:T(8,128)(2,1)S(1)} %turn.6.refs_4_), channel_id=1, source_target_pairs={{0,24},{1,29},{2,26},{3,31},{4,28},{5,25},{6,30},{7,27},{8,16},{9,... | collective-permute-start | bytes 688136 | tf_op jit(solution)/shard_map/ppermute | solution.py:271
  28.7 1.4 %collective-permute-start.12 = (bf16[2,32,896]{2,1,0:T(8,128)(2,1)S(1)}, bf16[2,32,896]{2,1,0:T(8,128)(2,1)S(1)}, u32[]{:S(2)}, u32[]{:S(2)}) collective-permute-start(bf16[2,32,896]{2,1,0:T(8,128)(2,1)S(1)} %get-tuple-element.32), channel_id=1, source_target_pairs={{0,1},{1,0},{2,3},{3,2},{4,5},{5,4},{6,7},{7,6},{8,9},{9,8},{10,11... | collective-permute-start | bytes 344072 | tf_op jit(solution)/shard_map/ppermute | solution.py:274
  28.9 1.4 %collective-permute-start.13 = (bf16[2,32,896]{2,1,0:T(8,128)(2,1)S(1)}, bf16[2,32,896]{2,1,0:T(8,128)(2,1)S(1)}, u32[]{:S(2)}, u32[]{:S(2)}) collective-permute-start(bf16[2,32,896]{2,1,0:T(8,128)(2,1)S(1)} %get-tuple-element.31), channel_id=1, source_target_pairs={{0,1},{1,0},{2,3},{3,2},{4,5},{5,4},{6,7},{7,6},{8,9},{9,8},{10,11... | collective-permute-start | bytes 344072 | tf_op jit(solution)/shard_map/ppermute | solution.py:274
  29.3 1.4 %collective-permute-start.10 = (bf16[4,16,896]{2,1,0:T(8,128)(2,1)S(1)}, bf16[4,16,896]{2,1,0:T(8,128)(2,1)S(1)}, u32[]{:S(2)}, u32[]{:S(2)}) collective-permute-start(bf16[4,16,896]{2,1,0:T(8,128)(2,1)S(1)} %get-tuple-element.34), channel_id=1, source_target_pairs={{0,1},{1,0},{2,3},{3,2},{4,5},{5,4},{6,7},{7,6},{8,9},{9,8},{10,11... | collective-permute-start | bytes 344072 | tf_op jit(solution)/shard_map/ppermute | solution.py:274
  29.5 4.0 %collective-permute-start.11 = (bf16[4,16,896]{2,1,0:T(8,128)(2,1)S(1)}, bf16[4,16,896]{2,1,0:T(8,128)(2,1)S(1)}, u32[]{:S(2)}, u32[]{:S(2)}) collective-permute-start(bf16[4,16,896]{2,1,0:T(8,128)(2,1)S(1)} %get-tuple-element.33), channel_id=1, source_target_pairs={{0,1},{1,0},{2,3},{3,2},{4,5},{5,4},{6,7},{7,6},{8,9},{9,8},{10,11... | collective-permute-start | bytes 344072 | tf_op jit(solution)/shard_map/ppermute | solution.py:274
  30.1 4.7 %collective-permute-start.8 = (bf16[2,32,896]{2,1,0:T(8,128)(2,1)S(1)}, bf16[2,32,896]{2,1,0:T(8,128)(2,1)S(1)}, u32[]{:S(2)}, u32[]{:S(2)}) collective-permute-start(bf16[2,32,896]{2,1,0:T(8,128)(2,1)S(1)} %get-tuple-element.36), channel_id=1, source_target_pairs={{0,1},{1,0},{2,3},{3,2},{4,5},{5,4},{6,7},{7,6},{8,9},{9,8},{10,11... | collective-permute-start | bytes 344072 | tf_op jit(solution)/shard_map/ppermute | solution.py:274
  30.3 4.6 %collective-permute-start.9 = (bf16[2,32,896]{2,1,0:T(8,128)(2,1)S(1)}, bf16[2,32,896]{2,1,0:T(8,128)(2,1)S(1)}, u32[]{:S(2)}, u32[]{:S(2)}) collective-permute-start(bf16[2,32,896]{2,1,0:T(8,128)(2,1)S(1)} %get-tuple-element.35), channel_id=1, source_target_pairs={{0,1},{1,0},{2,3},{3,2},{4,5},{5,4},{6,7},{7,6},{8,9},{9,8},{10,11... | collective-permute-start | bytes 344072 | tf_op jit(solution)/shard_map/ppermute | solution.py:274
  30.7 7.7 %collective-permute-start.16 = (bf16[8,16,896]{2,1,0:T(8,128)(2,1)S(1)}, bf16[8,16,896]{2,1,0:T(8,128)(2,1)S(1)}, u32[]{:S(2)}, u32[]{:S(2)}) collective-permute-start(bf16[8,16,896]{2,1,0:T(8,128)(2,1)S(1)} %get-tuple-element.22.refs_0_), channel_id=1, source_target_pairs={{0,2},{1,3},{2,0},{3,1},{4,6},{5,7},{6,4},{7,5},{8,10},{9,11},{10,... | collective-permute-start | bytes 688136 | tf_op jit(solution)/shard_map/ppermute | solution.py:274
  33.5 8.0 %collective-permute-start.15 = (bf16[4,32,896]{2,1,0:T(8,128)(2,1)S(1)}, bf16[4,32,896]{2,1,0:T(8,128)(2,1)S(1)}, u32[]{:S(2)}, u32[]{:S(2)}) collective-permute-start(bf16[4,32,896]{2,1,0:T(8,128)(2,1)S(1)} %get-tuple-element.24), channel_id=1, source_target_pairs={{0,8},{1,13},{2,10},{3,15},{4,12},{5,9},{6,14},{7,11},{8,0},{9,5},... | collective-permute-start | bytes 688136 | tf_op jit(solution)/shard_map/ppermute | solution.py:271
  36.8 8.5 %collective-permute-start.14 = (bf16[8,16,896]{2,1,0:T(8,128)(2,1)S(1)}, bf16[8,16,896]{2,1,0:T(8,128)(2,1)S(1)}, u32[]{:S(2)}, u32[]{:S(2)}) collective-permute-start(bf16[8,16,896]{2,1,0:T(8,128)(2,1)S(1)} %turn.8.refs_1_.refs_0_), channel_id=1, source_target_pairs={{0,2},{1,3},{2,0},{3,1},{4,6},{5,7},{6,4},{7,5},{8,10},{9,11},{10,... | collective-permute-start | bytes 688136 | tf_op jit(solution)/shard_map/ppermute | solution.py:274
  38.4 3.7 %collective-permute-start.19 = (bf16[4,16,896]{2,1,0:T(8,128)(2,1)S(1)}, bf16[4,16,896]{2,1,0:T(8,128)(2,1)S(1)}, u32[]{:S(2)}, u32[]{:S(2)}) collective-permute-start(bf16[4,16,896]{2,1,0:T(8,128)(2,1)S(1)} %get-tuple-element.28), channel_id=1, source_target_pairs={{0,1},{1,0},{2,3},{3,2},{4,5},{5,4},{6,7},{7,6},{8,9},{9,8},{10,11... | collective-permute-start | bytes 344072 | tf_op jit(solution)/shard_map/ppermute | solution.py:274
  38.5 3.8 %collective-permute-start.20 = (bf16[4,16,896]{2,1,0:T(8,128)(2,1)S(1)}, bf16[4,16,896]{2,1,0:T(8,128)(2,1)S(1)}, u32[]{:S(2)}, u32[]{:S(2)}) collective-permute-start(bf16[4,16,896]{2,1,0:T(8,128)(2,1)S(1)} %get-tuple-element.27), channel_id=1, source_target_pairs={{0,1},{1,0},{2,3},{3,2},{4,5},{5,4},{6,7},{7,6},{8,9},{9,8},{10,11... | collective-permute-start | bytes 344072 | tf_op jit(solution)/shard_map/ppermute | solution.py:274
  41.5 2.4 %collective-permute-start.17 = (bf16[2,32,896]{2,1,0:T(8,128)(2,1)S(1)}, bf16[2,32,896]{2,1,0:T(8,128)(2,1)S(1)}, u32[]{:S(2)}, u32[]{:S(2)}) collective-permute-start(bf16[2,32,896]{2,1,0:T(8,128)(2,1)S(1)} %get-tuple-element.30), channel_id=1, source_target_pairs={{0,1},{1,0},{2,3},{3,2},{4,5},{5,4},{6,7},{7,6},{8,9},{9,8},{10,11... | collective-permute-start | bytes 344072 | tf_op jit(solution)/shard_map/ppermute | solution.py:274
  41.6 2.4 %collective-permute-start.18 = (bf16[2,32,896]{2,1,0:T(8,128)(2,1)S(1)}, bf16[2,32,896]{2,1,0:T(8,128)(2,1)S(1)}, u32[]{:S(2)}, u32[]{:S(2)}) collective-permute-start(bf16[2,32,896]{2,1,0:T(8,128)(2,1)S(1)} %get-tuple-element.29), channel_id=1, source_target_pairs={{0,1},{1,0},{2,3},{3,2},{4,5},{5,4},{6,7},{7,6},{8,9},{9,8},{10,11... | collective-permute-start | bytes 344072 | tf_op jit(solution)/shard_map/ppermute | solution.py:274
  42.1 3.3 %collective-permute-start.22 = (bf16[4,16,896]{2,1,0:T(8,128)(2,1)S(1)}, bf16[4,16,896]{2,1,0:T(8,128)(2,1)S(1)}, u32[]{:S(2)}, u32[]{:S(2)}) collective-permute-start(bf16[4,16,896]{2,1,0:T(8,128)(2,1)S(1)} %get-tuple-element.26), channel_id=1, source_target_pairs={{0,1},{1,0},{2,3},{3,2},{4,5},{5,4},{6,7},{7,6},{8,9},{9,8},{10,11... | collective-permute-start | bytes 344072 | tf_op jit(solution)/shard_map/ppermute | solution.py:274
  42.3 3.1 %collective-permute-start.23 = (bf16[4,16,896]{2,1,0:T(8,128)(2,1)S(1)}, bf16[4,16,896]{2,1,0:T(8,128)(2,1)S(1)}, u32[]{:S(2)}, u32[]{:S(2)}) collective-permute-start(bf16[4,16,896]{2,1,0:T(8,128)(2,1)S(1)} %get-tuple-element.25), channel_id=1, source_target_pairs={{0,1},{1,0},{2,3},{3,2},{4,5},{5,4},{6,7},{7,6},{8,9},{9,8},{10,11... | collective-permute-start | bytes 344072 | tf_op jit(solution)/shard_map/ppermute | solution.py:274
  45.3 1.6 %collective-permute-start.21 = (bf16[8,16,896]{2,1,0:T(8,128)(2,1)S(1)}, bf16[8,16,896]{2,1,0:T(8,128)(2,1)S(1)}, u32[]{:S(2)}, u32[]{:S(2)}) collective-permute-start(bf16[8,16,896]{2,1,0:T(8,128)(2,1)S(1)} %turn.11.refs_0_), channel_id=1, source_target_pairs={{0,1},{1,0},{2,3},{3,2},{4,5},{5,4},{6,7},{7,6},{8,9},{9,8},{10,11... | collective-permute-start | bytes 688136 | tf_op jit(solution)/shard_map/ppermute | solution.py:274
  46.7 2.2 %copy-start = (bf16[2048,1024]{1,0:T(8,128)(2,1)S(1)}, bf16[2048,1024]{1,0:T(8,128)(2,1)}, u32[]{:S(2)}) copy-start(bf16[2048,1024]{1,0:T(8,128)(2,1)} %queries_ref.1) | copy-start | bytes 12582916

commit v5 on v4

--- a/solution.py
+++ b/solution.py
@@ -18,33 +18,43 @@
     return pltpu.with_memory_space_constraint(value, pltpu.VMEM)
 
 
-def plan_kernel(capacity, tile_count, ids_ref, slots_ref):
+def plan_kernel(capacity, ids_ref, stored_ref, slots_ref, own_ref, table_ref):
     seq_at, core = lax.axis_index("seq"), lax.rem(lax.axis_index("mp"), 2)
+    tile_count = stored_ref.shape[0]
     bits = tile_count.bit_length() - 1
     half = capacity // 2
     counts = jnp.int32(0)
     for k in range(ids_ref.shape[0]):
         for c in range(ids_ref.shape[1]):
-            owner = lax.shift_right_logical(ids_ref[k, c], bits)
+            tile_id = ids_ref[k, c]
+            owner = lax.shift_right_logical(tile_id, bits)
             shift = owner * 4
             rank = lax.shift_right_logical(counts, shift) & (capacity - 1)
             counts += jnp.int32(1) << shift
             apart = owner ^ seq_at
+            table_ref[apart * capacity + rank] = tile_id & (tile_count - 1)
             near = ((apart & 1) * capacity) + (rank ^ ((apart & 1) * core * half))
             far = ((apart & -2) + ((apart & 1) ^ core)) * capacity + rank
             slots_ref[2 * c + k] = jnp.where(apart < 2, near, far)
-
-
-def plan(ids, tile_count, capacity):
-    smem = pl.BlockSpec(memory_space=pltpu.SMEM)
-    return pl.pallas_call(
-        functools.partial(plan_kernel, capacity, tile_count),
-        out_shape=jax.ShapeDtypeStruct((ids.size,), jnp.int32),
-        in_specs=[smem],
-        out_specs=smem,
+    for j in range(capacity):
+        own_ref[j] = stored_ref[table_ref[j]]
+
+
+def plan(ids, stored, capacity):
+    smem, vmem = pl.BlockSpec(memory_space=pltpu.SMEM), pl.BlockSpec(memory_space=pltpu.VMEM)
+    return pl.pallas_call(
+        functools.partial(plan_kernel, capacity),
+        out_shape=[
+            jax.ShapeDtypeStruct((ids.size,), jnp.int32),
+            pltpu.VMEM((capacity, *stored.shape[1:]), stored.dtype),
+        ],
+        in_specs=[smem, vmem],
+        out_specs=[smem, vmem],
+        scratch_shapes=[pltpu.SMEM((ids.size,), jnp.int32)],
+        compiler_params=pltpu.CompilerParams(vmem_limit_bytes=16 * MIB),
         cost_estimate=LIGHT,
         name="plan",
-    )(ids)
+    )(ids, stored)
 
 
 def pick_kernel(plans, *refs):
@@ -79,26 +89,25 @@
             at += 1
 
 
-def pick(asked, own, stored, plans):
+def pick(asked, stored, plans):
     _, rows, width = stored.shape
-    vmem, anywhere = pl.BlockSpec(memory_space=pltpu.VMEM), pl.BlockSpec(memory_space=pl.ANY)
+    vmem = pl.BlockSpec(memory_space=pltpu.VMEM)
     shapes = [(size, rows // 2 if kind == "rows" else rows, width) for kind, sizes in plans for size in sizes]
     return pl.pallas_call(
         functools.partial(pick_kernel, plans),
-        out_shape=[pltpu.VMEM(shape, stored.dtype) for shape in shapes],
-        in_specs=[vmem] * len(asked) + [anywhere, anywhere],
-        out_specs=[vmem] * len(shapes),
+        out_shape=[pltpu.VMEM(shape, stored.dtype) for shape in [*shapes, stored.shape]],
+        in_specs=[vmem] * len(asked) + [pl.BlockSpec(memory_space=pl.ANY)],
+        out_specs=[vmem] * (len(shapes) + 1),
         scratch_shapes=[
-            pltpu.VMEM(stored.shape, stored.dtype),
-            pltpu.SMEM((len(plans), *own.shape), jnp.int32),
-            pltpu.SMEM((len(plans), own.size + 1), jnp.int32),
+            pltpu.SMEM((len(plans), *asked[0].shape), jnp.int32),
+            pltpu.SMEM((len(plans), asked[0].size + 1), jnp.int32),
             pltpu.SemaphoreType.DMA((len(plans),)),
             pltpu.SemaphoreType.DMA,
         ],
         compiler_params=pltpu.CompilerParams(vmem_limit_bytes=52 * MIB),
         cost_estimate=LIGHT,
         name="pick",
-    )(*[in_vmem(a) for a in asked], own, stored)
+    )(*[in_vmem(a) for a in asked], stored)
 
 
 def turn_kernel(*refs):
@@ -181,17 +190,17 @@
     return both[:half, :HEAD_DIM], both[half:, HEAD_DIM:]
 
 
-def attend_kernel(heads, many, slots_ref, queries_ref, held_ref, out_ref):
+def attend_kernel(heads, per, slots_ref, queries_ref, held_ref, out_ref, made_ref, sem):
     apart = 6
-    first = pl.program_id(0) * many
-    items = [(g, h) for g in range(many) for h in range(0, heads, 2)]
+    groups = queries_ref.shape[0] // GROUP
+    items = [(g, h) for g in range(groups) for h in range(0, heads, 2)]
 
     def part_of(g, h):
-        one, two = slots_ref[2 * (first + g)], slots_ref[2 * (first + g) + 1]
+        one, two = slots_ref[2 * g], slots_ref[2 * g + 1]
         at = pl.ds(h * HEAD_DIM, HEAD_DIM)
         return jnp.concatenate([held_ref[one, :, at], held_ref[two, :, at]], axis=0)
 
-    scores, probs = {}, {}
+    scores, probs, copies = {}, {}, []
     for now in range(len(items) + 2 * apart):
         if now < len(items):
             g, h = items[now]
@@ -203,29 +212,29 @@
             g, h = items[now - 2 * apart]
             mixed = mix(probs.pop(now - 2 * apart), [part_of(g, heads + h + i) for i in range(2)])
             for i in range(2):
-                out_ref[pl.ds(g * GROUP, GROUP), pl.ds((h + i) * HEAD_DIM, HEAD_DIM)] = mixed[i].astype(jnp.bfloat16)
+                made_ref[pl.ds(g * GROUP, GROUP), pl.ds((h + i) * HEAD_DIM, HEAD_DIM)] = mixed[i].astype(jnp.bfloat16)
+            if h == heads - 2 and g % per == per - 1:
+                done = pl.ds((g + 1 - per) * GROUP, per * GROUP)
+                copies.append(pltpu.make_async_copy(made_ref.at[done], out_ref.at[done], sem.at[g // per]))
+                copies[-1].start()
+    for copy in copies:
+        copy.wait()
 
 
 def attend(queries, held, slots, heads):
     groups = queries.shape[0] // GROUP
-    many = 8 if groups % 8 == 0 else 1
-    block = (many * GROUP, queries.shape[1])
-    return pl.pallas_call(
-        functools.partial(attend_kernel, heads, many),
+    per = 2 if groups % 2 == 0 else 1
+    vmem = pl.BlockSpec(memory_space=pltpu.VMEM)
+    return pl.pallas_call(
+        functools.partial(attend_kernel, heads, per),
         out_shape=jax.ShapeDtypeStruct(queries.shape, jnp.bfloat16),
-        grid_spec=pltpu.PrefetchScalarGridSpec(
-            num_scalar_prefetch=1,
-            grid=(groups // many,),
-            in_specs=[
-                pl.BlockSpec(block, lambda c, s: (c, 0)),
-                pl.BlockSpec(memory_space=pltpu.VMEM),
-            ],
-            out_specs=pl.BlockSpec(block, lambda c, s: (c, 0)),
-        ),
+        in_specs=[pl.BlockSpec(memory_space=pltpu.SMEM), vmem, vmem],
+        out_specs=pl.BlockSpec(memory_space=pl.ANY),
+        scratch_shapes=[pltpu.VMEM(queries.shape, jnp.bfloat16), pltpu.SemaphoreType.DMA((groups // per,))],
         compiler_params=pltpu.CompilerParams(vmem_limit_bytes=24 * MIB),
         cost_estimate=pl.CostEstimate(flops=10**9, bytes_accessed=16 * MIB, transcendentals=10**6),
         name="attend",
-    )(slots, queries, in_vmem(held))
+    )(slots, in_vmem(queries), in_vmem(held))
 
 
 def ref_ranks(owners):
@@ -275,7 +284,7 @@
 
 
     ids = retrieved.T
-    size = capacity // 2
+    size, early = capacity // 2, capacity // 2
 
     def spread(mine, first):
         theirs = over_mp(mine, 2)
@@ -287,11 +296,11 @@
         ]
 
     asked = [across(ids, p) for p in (2, 3, 1, 0)]
-    kinds = [("rows", [capacity]), ("rows", [capacity]), ("all", [size, size]), ("tiles", [size]), ("all", [capacity])]
-    picked2, picked3, *picked1, beside, own = pick(asked, ids, encoded, kinds)
+    kinds = [("rows", [capacity]), ("rows", [capacity]), ("all", [early, capacity - early]), ("tiles", [size])]
+    picked2, picked3, *picked1, beside, stored = pick(asked, encoded, kinds)
     got2, got1, beside = across(picked2, 2), across(picked1[0], 1), across(beside, 0)
     weights = in_vmem(w_kv.reshape(width, -1))
-    slots = plan(ids, tile_count, capacity)
+    slots, own = plan(ids, stored, capacity)
     shape = (ref_count, rows, weights.shape[1])
 
     def add(held, pieces, weight):
@@ -308,15 +317,16 @@
     got3, rest1, theirs2 = across(picked3, 3), across(next1, 1), over_mp(got2, 2)
     held = add(held, [(capacity, 0, beside), *core(beside, capacity + size, 0, 2)], 1)
     held = add(held, [(at2, 0, got2), *core(got2, at2 + capacity, 0, 2)], 1)
-    held = add(held, [(at1, 0, got1), *core(got1, at1 + capacity, 0, 2)], 1)
+    held = add(held, [(at1, 0, got1), *core(got1, at1 + capacity, 0, 1 if early % 2 else 2)], 1)
     got3 = turn([got3], [held], PACE)[0]
     theirs3 = over_mp(got3, 2)
+    queries = in_vmem(queries)
     theirs2 = turn([theirs2], [got3], 1)[0]
-    rest1 = turn([rest1], [theirs2], 1)[0]
+    rest1 = turn([rest1], [theirs2, queries], 1)[0]
     held = add(held, [(at2, rows // 2, theirs2), *core(theirs2, at2 + capacity, rows // 2, 2)], 1)
-    held = add(held, [(at1 + size, 0, rest1), *core(rest1, at1 + capacity + size, 0, 2)], 1)
+    held = add(held, [(at1 + early, 0, rest1), *core(rest1, at1 + capacity + early, 0, 1 if early % 2 or early > size else 2)], 1)
     theirs3 = turn([theirs3], [held], 1)[0]
-    held = add(held, [(at3, 0, got3), *core(got3, at3 + capacity, 0, 2)], 64)
+    held = add(held, [(at3, 0, got3), *core(got3, at3 + capacity, 0, 1)], 64)
     held = add(held, [(at3, rows // 2, theirs3), *core(theirs3, at3 + capacity, rows // 2, 1)], 64)
     return attend(queries, held, slots, queries.shape[1] // HEAD_DIM)
 

time: 55.6 us -> 52.1 us (0.937)
  local copies, waits for them, and re-layouts: 4.89 us -> 3.38 us
  Pallas kernels: 20.1 us -> 18.7 us
  starting transfers between devices: 20.8 us -> 20.2 us
    unnamed x7 -> x5, local copies, waits for them, and re-layouts: 4.77 us -> 3.29 us
    pallas_call x2, Pallas kernels: 8.1 us -> 6.98 us  [the longest x1 5.3 us: attend(): pl.pallas_call(functools.partial(attend_kernel, heads, per), out_shape=ja...]
    ppermute x15 -> x14, starting transfers between devices: 6.49 us -> 5.95 us  [over_mp(): return lax.ppermute(value, 'mp', [(m, m ^ flip) for m in range(mp_count)])]
  transfers between devices with their start and end apart: 24 -> 23, of which waited for: 8 -> 8; matrix products, arithmetic and copies ran while one was open for 6% -> 6% of each run, Pallas kernels for 19% -> 20%
where the time goes in v5:
time: 52.1 us; the launch traced here: 52 us
  starting transfers between devices  20.2 us (39%)
  Pallas kernels  18.7 us (36%)
  waiting for transfers between devices  9.36 us (18%)
  local copies, waits for them, and re-layouts  3.38 us (6%)
    ppermute x7, starting transfers between devices, across(): lax.ppermute(value, both, joint(lambda s, m: (s ^ 2 * part ^ m % 2) * mp_...  11.2 us
    pallas_call x8, Pallas kernels, project(): pl.pallas_call(functools.partial(project_kernel, [(tile, row) for tile, r...  10 us
    ppermute x7, waiting for transfers between devices, across(): lax.ppermute(value, both, joint(lambda s, m: (s ^ 2 * part ^ m % 2) * mp_...  8.84 us
    ppermute x14, starting transfers between devices, over_mp(): return lax.ppermute(value, 'mp', [(m, m ^ flip) for m in range(mp_count)])  5.95 us
    pallas_call x1, Pallas kernels, attend(): pl.pallas_call(functools.partial(attend_kernel, heads, per), out_shape=ja...  5.3 us
    unnamed x5, local copies, waits for them, and re-layouts  3.29 us
    ppermute x2, starting transfers between devices, across(): return lax.ppermute(value, 'seq', [(s, s ^ 1) for s in range(seq_count)])  3.04 us
    pallas_call x1, Pallas kernels, plan(): pl.pallas_call(functools.partial(plan_kernel, capacity), out_shape=[jax.S...  1.69 us
  transfers between devices with their start and end apart: 23, of which 8 were waited for; matrix products, arithmetic and copies ran while one was open for 6% of the time, Pallas kernels for 20%

profile of v5, /device:TPU:0, one launch (start us, length us, event | category | flops | bytes accessed | tf_op | source)
XLA Modules:
  0.0 52.0 jit_solution(16725101376226433032)
XLA Ops:
  0.0 4.0 %collective-permute-start = (s32[2,32]{1,0:T(2,128)}, s32[2,32]{1,0:T(2,128)S(1)}, u32[]{:S(2)}, u32[]{:S(2)}) collective-permute-start(s32[2,32]{1,0:T(2,128)} %bitcast.11), channel_id=1, source_target_pairs={{0,16},{1,21},{2,18},{3,23},{4,20},{5,17},{6,22},{7,19},{8,24},{9,... | collective-permute-start | bytes 776 | tf_op jit(solution)/shard_map/ppermute | solution.py:280
  4.0 1.3 %collective-permute-start.1 = (s32[2,32]{1,0:T(2,128)}, s32[2,32]{1,0:T(2,128)S(1)}, u32[]{:S(2)}, u32[]{:S(2)}) collective-permute-start(s32[2,32]{1,0:T(2,128)} %bitcast.12), channel_id=1, source_target_pairs={{0,24},{1,29},{2,26},{3,31},{4,28},{5,25},{6,30},{7,27},{8,16},{9,... | collective-permute-start | bytes 776 | tf_op jit(solution)/shard_map/ppermute | solution.py:280
  5.4 0.2 collective-permute-start.2
  5.6 1.5 %collective-permute-start.3 = (s32[2,32]{1,0:T(2,128)}, s32[2,32]{1,0:T(2,128)S(1)}, u32[]{:S(2)}, u32[]{:S(2)}) collective-permute-start(s32[2,32]{1,0:T(2,128)} %bitcast.14), channel_id=1, source_target_pairs={{0,4},{4,0},{8,12},{12,8},{16,20},{20,16},{24,28},{28,24},{1,5},{5... | collective-permute-start | bytes 776 | tf_op jit(solution)/shard_map/ppermute | solution.py:279
  7.1 2.5 %collective-permute-done.1.refs_1_ = s32[2,32]{1,0:T(2,128)S(1)} collective-permute-done((s32[2,32]{1,0:T(2,128)}, s32[2,32]{1,0:T(2,128)S(1)}, u32[]{:S(2)}, u32[]{:S(2)}) %collective-permute-start.1) | collective-permute-done | bytes 288 | tf_op jit(solution)/shard_map/ppermute | solution.py:280
  9.6 1.7 %pick.1 = (bf16[8,16,896]{2,1,0:T(8,128)(2,1)S(1)}, bf16[8,16,896]{2,1,0:T(8,128)(2,1)S(1)}, bf16[4,32,896]{2,1,0:T(8,128)(2,1)S(1)}, bf16[4,32,896]{2,1,0:T(8,1...) custom-call(s32[2,32]{1,0:T(2,128)S(1)} %collective-permute-done.refs_0_, ...), custom_call_target="tpu_custom_call" | custom-call | flops 1 | bytes 1 | tf_op jit(solution)/shard_map/pick/pallas_call | solution.py:96
  11.3 2.6 %collective-permute-start.4 = (bf16[8,16,896]{2,1,0:T(8,128)(2,1)S(1)}, bf16[8,16,896]{2,1,0:T(8,128)(2,1)S(1)}, u32[]{:S(2)}, u32[]{:S(2)}) collective-permute-start(bf16[8,16,896]{2,1,0:T(8,128)(2,1)S(1)} %get-tuple-element.20), channel_id=1, source_target_pairs={{0,16},{1,21},{2,18},{3,23},{4,20},{5,17},{6,22},{7,19},{8,24},{9,... | collective-permute-start | bytes 688136 | tf_op jit(solution)/shard_map/ppermute | solution.py:280
  13.9 1.5 %collective-permute-start.6 = (bf16[4,32,896]{2,1,0:T(8,128)(2,1)S(1)}, bf16[4,32,896]{2,1,0:T(8,128)(2,1)S(1)}, u32[]{:S(2)}, u32[]{:S(2)}) collective-permute-start(bf16[4,32,896]{2,1,0:T(8,128)(2,1)S(1)} %get-tuple-element.23), channel_id=1, source_target_pairs={{0,4},{4,0},{8,12},{12,8},{16,20},{20,16},{24,28},{28,24},{1,5},{5... | collective-permute-start | bytes 688136 | tf_op jit(solution)/shard_map/ppermute | solution.py:279
  15.5 0.7 %collective-permute-start.7 = (bf16[4,32,896]{2,1,0:T(8,128)(2,1)S(1)}, bf16[4,32,896]{2,1,0:T(8,128)(2,1)S(1)}, u32[]{:S(2)}, u32[]{:S(2)}) collective-permute-start(bf16[4,32,896]{2,1,0:T(8,128)(2,1)S(1)} %get-tuple-element.24), channel_id=1, source_target_pairs={{0,8},{1,13},{2,10},{3,15},{4,12},{5,9},{6,14},{7,11},{8,0},{9,5},... | collective-permute-start | bytes 688136 | tf_op jit(solution)/shard_map/ppermute | solution.py:280
  16.1 3.3 %copy.21 = bf16[112,8,2,1024]{3,1,2,0:T(8,128)(2,1)S(1)} copy(bf16[112,8,2,1024]{3,2,1,0:T(2,128)(2,1)} %bitcast.16) | data formatting | bytes 7340032
  19.4 1.7 %plan.1 = (s32[64]{0:T(128)S(1)}, bf16[8,32,896]{2,1,0:T(8,128)(2,1)S(1)}) custom-call(s32[2,32]{1,0:T(2,128)S(1)} %bitcast.15, bf16[32,32,896]{2,1,0:T(8,128)(2,1)S(1)} %get-tuple-element.17.stored_ref), custom_call_target="tpu_custom_call" | custom-call | flops 1 | bytes 1 | tf_op jit(solution)/shard_map/plan/pallas_call | solution.py:45
  21.1 1.3 %project.8.refs_2_.refs_4_ = bf16[64,32,2048]{2,1,0:T(8,128)(2,1)S(1)} custom-call(bf16[8,32,896]{2,1,0:T(8,128)(2,1)S(1)} %get-tuple-element.21.refs_0_, bf16[896,2048]{1,0:T(8,128)(2,1)S(1)} %bitcast.3), custom_call_target="tpu_custom_call" | custom-call | flops 117440512 | tf_op jit(solution)/shard_map/project/pallas_call | solution.py:156
  22.4 3.1 %collective-permute-done.4.refs_1_.refs_3_ = bf16[8,16,896]{2,1,0:T(8,128)(2,1)S(1)} collective-permute-done((bf16[8,16,896]{2,1,0:T(8,128)(2,1)S(1)}, bf16[8,16,896]{2,1,0:T(8,128)(2,1)S(1)}, u32[]{:S(2)}, u32[]{:S(2)}) %collective-permute-start.4) | collective-permute-done | bytes 229408 | tf_op jit(solution)/shard_map/ppermute | solution.py:280
  25.5 2.2 %collective-permute-start.5 = (bf16[8,16,896]{2,1,0:T(8,128)(2,1)S(1)}, bf16[8,16,896]{2,1,0:T(8,128)(2,1)S(1)}, u32[]{:S(2)}, u32[]{:S(2)}) collective-permute-start(bf16[8,16,896]{2,1,0:T(8,128)(2,1)S(1)} %turn.6.refs_4_), channel_id=1, source_target_pairs={{0,24},{1,29},{2,26},{3,31},{4,28},{5,25},{6,30},{7,27},{8,16},{9,... | collective-permute-start | bytes 688136 | tf_op jit(solution)/shard_map/ppermute | solution.py:280
  27.9 0.4 collective-permute-start.13
  28.5 0.4 collective-permute-start.11
  28.9 0.2 collective-permute-done.12.refs_1_
  29.3 0.3 collective-permute-start.9
  29.7 1.5 %collective-permute-start.16 = (bf16[8,16,896]{2,1,0:T(8,128)(2,1)S(1)}, bf16[8,16,896]{2,1,0:T(8,128)(2,1)S(1)}, u32[]{:S(2)}, u32[]{:S(2)}) collective-permute-start(bf16[8,16,896]{2,1,0:T(8,128)(2,1)S(1)} %get-tuple-element.26.refs_0_), channel_id=1, source_target_pairs={{0,2},{1,3},{2,0},{3,1},{4,6},{5,7},{6,4},{7,5},{8,10},{9,11},{10,... | collective-permute-start | bytes 688136 | tf_op jit(solution)/shard_map/ppermute | solution.py:283
  31.2 1.2 %project.9.refs_4_ = bf16[64,32,2048]{2,1,0:T(8,128)(2,1)S(1)} custom-call(bf16[4,32,896]{2,1,0:T(8,128)(2,1)S(1)} %get-tuple-element.27.refs_0_, bf16[2,32,896]{2,1,0:T(8,128)(2,1)S(1)} %collective-permute-done.12.refs_1_, bf16[2,32,896]{2,1,0:T(8,128)(2,1)S(1)} %collective-permute-done.13.refs_2_, ...), custom_call_target="tpu_custom_call", output_to_operand_aliasing={{}: (4, {})} | custom-call | flops 117440512 | tf_op jit(solution)/shard_map/project/pallas_call | solution.py:156
  32.6 1.2 %project.10.refs_4_ = bf16[64,32,2048]{2,1,0:T(8,128)(2,1)S(1)} custom-call(bf16[8,16,896]{2,1,0:T(8,128)(2,1)S(1)} %get-tuple-element.26.refs_0_, bf16[4,16,896]{2,1,0:T(8,128)(2,1)S(1)} %collective-permute-done.10.refs_1_, bf16[4,16,896]{2,1,0:T(8,128)(2,1)S(1)} %collective-permute-done.11.refs_2_, ...), custom_call_target="tpu_custom_call", output_to_operand_aliasing={{}: (4, {})} | custom-call | flops 117440512 | tf_op jit(solution)/shard_map/project/pallas_call | solution.py:156
  33.8 1.2 %project.11.refs_1_.refs_4_ = bf16[64,32,2048]{2,1,0:T(8,128)(2,1)S(1)} custom-call(bf16[4,32,896]{2,1,0:T(8,128)(2,1)S(1)} %get-tuple-element.25.refs_0_, bf16[2,32,896]{2,1,0:T(8,128)(2,1)S(1)} %collective-permute-done.8.refs_1_, bf16[2,32,896]{2,1,0:T(8,128)(2,1)S(1)} %collective-permute-done.9.refs_2_, ...), custom_call_target="tpu_custom_call", output_to_operand_aliasing={{}: (4, {})} | custom-call | flops 117440512 | tf_op jit(solution)/shard_map/project/pallas_call | solution.py:156
  35.1 0.7 %collective-permute-done.5.refs_0_ = bf16[8,16,896]{2,1,0:T(8,128)(2,1)S(1)} collective-permute-done((bf16[8,16,896]{2,1,0:T(8,128)(2,1)S(1)}, bf16[8,16,896]{2,1,0:T(8,128)(2,1)S(1)}, u32[]{:S(2)}, u32[]{:S(2)}) %collective-permute-start.5) | collective-permute-done | bytes 229408 | tf_op jit(solution)/shard_map/ppermute | solution.py:280
  35.8 1.5 %collective-permute-start.14 = (bf16[8,16,896]{2,1,0:T(8,128)(2,1)S(1)}, bf16[8,16,896]{2,1,0:T(8,128)(2,1)S(1)}, u32[]{:S(2)}, u32[]{:S(2)}) collective-permute-start(bf16[8,16,896]{2,1,0:T(8,128)(2,1)S(1)} %turn.8.refs_1_.refs_0_), channel_id=1, source_target_pairs={{0,2},{1,3},{2,0},{3,1},{4,6},{5,7},{6,4},{7,5},{8,10},{9,11},{10,... | collective-permute-start | bytes 688136 | tf_op jit(solution)/shard_map/ppermute | solution.py:283
  37.4 0.5 collective-permute-start.19
  38.0 2.5 %collective-permute-done.15.refs_0_ = bf16[4,32,896]{2,1,0:T(8,128)(2,1)S(1)} collective-permute-done((bf16[4,32,896]{2,1,0:T(8,128)(2,1)S(1)}, bf16[4,32,896]{2,1,0:T(8,128)(2,1)S(1)}, u32[]{:S(2)}, u32[]{:S(2)}) %collective-permute-start.15) | collective-permute-done | bytes 229408 | tf_op jit(solution)/shard_map/ppermute | solution.py:280
  40.7 0.5 collective-permute-start.18
  41.1 1.2 %project.12.refs_4_ = bf16[64,32,2048]{2,1,0:T(8,128)(2,1)S(1)} custom-call(bf16[8,16,896]{2,1,0:T(8,128)(2,1)S(1)} %turn.9.refs_1_.refs_0_, bf16[4,16,896]{2,1,0:T(8,128)(2,1)S(1)} %collective-permute-done.19.refs_1_, bf16[4,16,896]{2,1,0:T(8,128)(2,1)S(1)} %collective-permute-done.20.refs_2_, ...), custom_call_target="tpu_custom_call", output_to_operand_aliasing={{}: (4, {})} | custom-call | flops 117440512 | tf_op jit(solution)/shard_map/project/pallas_call | solution.py:156
  42.4 1.2 %project.13.refs_1_.refs_3_ = bf16[64,32,2048]{2,1,0:T(8,128)(2,1)S(1)} custom-call(bf16[4,32,896]{2,1,0:T(8,128)(2,1)S(1)} %turn.10.refs_0_, bf16[2,32,896]{2,1,0:T(8,128)(2,1)S(1)} %collective-permute-done.17.refs_1_, bf16[2,32,896]{2,1,0:T(8,128)(2,1)S(1)} %collective-permute-done.18.refs_2_, ...), custom_call_target="tpu_custom_call", output_to_operand_aliasing={{}: (4, {})} | custom-call | flops 117440512 | tf_op jit(solution)/shard_map/project/pallas_call | solution.py:156
  43.9 1.2 %project.14.refs_3_ = bf16[64,32,2048]{2,1,0:T(8,128)(2,1)S(1)} custom-call(bf16[8,16,896]{2,1,0:T(8,128)(2,1)S(1)} %turn.8.refs_1_.refs_0_, bf16[8,16,896]{2,1,0:T(8,128)(2,1)S(1)} %collective-permute-done.22.refs_1_, bf16[896,2048]{1,0:T(8,128)(2,1)S(1)} %bitcast.9, bf16[64,32,2048]{2,1,0:T(8,128)(2,1)S(1)} %project.13.refs_1_.refs_3_), custom_call_target="tpu_custom_call", output_to_operand_aliasing={{}: (3, {})} | custom-call | flops 7516192768 | tf_op jit(solution)/shard_map/project/pallas_call | solution.py:156
  45.3 1.2 %project.15.held_ref = bf16[64,32,2048]{2,1,0:T(8,128)(2,1)S(1)} custom-call(bf16[8,16,896]{2,1,0:T(8,128)(2,1)S(1)} %turn.11.refs_0_, bf16[8,16,896]{2,1,0:T(8,128)(2,1)S(1)} %collective-permute-done.21.refs_1_, bf16[896,2048]{1,0:T(8,128)(2,1)S(1)} %bitcast.10, bf16[64,32,2048]{2,1,0:T(8,128)(2,1)S(1)} %project.14.refs_3_), custom_call_target="tpu_custom_call", output_to_operand_aliasing={{}: (3, {})} | custom-call | flops 7516192768 | tf_op jit(solution)/shard_map/project/pallas_call | solution.py:156
  46.5 5.3 %attend.1 = bf16[2048,1024]{1,0:T(8,128)(2,1)} custom-call(s32[64]{0:T(128)S(1)} %get-tuple-element.18.refs_3_.slots_ref, bf16[2048,1024]{1,0:T(8,128)(2,1)S(1)} %copy-done, bf16[64,32,2048]{2,1,0:T(8,128)(2,1)S(1)} %project.15.held_ref), custom_call_target="tpu_custom_call" | custom-call | flops 1000000000 | bytes 16777216 | tf_op jit(solution)/shard_map/attend/pallas_call | solution.py:228
  (41 shorter events, 1.2 us)
Async XLA Ops:
  0.0 19.4 %copy-start.1 = (s32[32,2]{0,1:T(2,128)S(1)}, s32[32,2]{0,1:T(2,128)}, u32[]{:S(2)}) copy-start(s32[32,2]{0,1:T(2,128)} %param.7) | copy-start | bytes 772
  0.0 7.1 %collective-permute-start = (s32[2,32]{1,0:T(2,128)}, s32[2,32]{1,0:T(2,128)S(1)}, u32[]{:S(2)}, u32[]{:S(2)}) collective-permute-start(s32[2,32]{1,0:T(2,128)} %bitcast.11), channel_id=1, source_target_pairs={{0,16},{1,21},{2,18},{3,23},{4,20},{5,17},{6,22},{7,19},{8,24},{9,... | collective-permute-start | bytes 776 | tf_op jit(solution)/shard_map/ppermute | solution.py:280
  4.0 5.6 %collective-permute-start.1 = (s32[2,32]{1,0:T(2,128)}, s32[2,32]{1,0:T(2,128)S(1)}, u32[]{:S(2)}, u32[]{:S(2)}) collective-permute-start(s32[2,32]{1,0:T(2,128)} %bitcast.12), channel_id=1, source_target_pairs={{0,24},{1,29},{2,26},{3,31},{4,28},{5,25},{6,30},{7,27},{8,16},{9,... | collective-permute-start | bytes 776 | tf_op jit(solution)/shard_map/ppermute | solution.py:280
  5.4 4.2 %collective-permute-start.2 = (s32[2,32]{1,0:T(2,128)}, s32[2,32]{1,0:T(2,128)S(1)}, u32[]{:S(2)}, u32[]{:S(2)}) collective-permute-start(s32[2,32]{1,0:T(2,128)} %bitcast.13), channel_id=1, source_target_pairs={{0,8},{1,13},{2,10},{3,15},{4,12},{5,9},{6,14},{7,11},{8,0},{9,5},... | collective-permute-start | bytes 776 | tf_op jit(solution)/shard_map/ppermute | solution.py:280
  5.6 4.0 %collective-permute-start.3 = (s32[2,32]{1,0:T(2,128)}, s32[2,32]{1,0:T(2,128)S(1)}, u32[]{:S(2)}, u32[]{:S(2)}) collective-permute-start(s32[2,32]{1,0:T(2,128)} %bitcast.14), channel_id=1, source_target_pairs={{0,4},{4,0},{8,12},{12,8},{16,20},{20,16},{24,28},{28,24},{1,5},{5... | collective-permute-start | bytes 776 | tf_op jit(solution)/shard_map/ppermute | solution.py:279
  11.3 14.2 %collective-permute-start.4 = (bf16[8,16,896]{2,1,0:T(8,128)(2,1)S(1)}, bf16[8,16,896]{2,1,0:T(8,128)(2,1)S(1)}, u32[]{:S(2)}, u32[]{:S(2)}) collective-permute-start(bf16[8,16,896]{2,1,0:T(8,128)(2,1)S(1)} %get-tuple-element.20), channel_id=1, source_target_pairs={{0,16},{1,21},{2,18},{3,23},{4,20},{5,17},{6,22},{7,19},{8,24},{9,... | collective-permute-start | bytes 688136 | tf_op jit(solution)/shard_map/ppermute | solution.py:280
  13.9 13.8 %collective-permute-start.6 = (bf16[4,32,896]{2,1,0:T(8,128)(2,1)S(1)}, bf16[4,32,896]{2,1,0:T(8,128)(2,1)S(1)}, u32[]{:S(2)}, u32[]{:S(2)}) collective-permute-start(bf16[4,32,896]{2,1,0:T(8,128)(2,1)S(1)} %get-tuple-element.23), channel_id=1, source_target_pairs={{0,4},{4,0},{8,12},{12,8},{16,20},{20,16},{24,28},{28,24},{1,5},{5... | collective-permute-start | bytes 688136 | tf_op jit(solution)/shard_map/ppermute | solution.py:279
  15.5 12.2 %collective-permute-start.7 = (bf16[4,32,896]{2,1,0:T(8,128)(2,1)S(1)}, bf16[4,32,896]{2,1,0:T(8,128)(2,1)S(1)}, u32[]{:S(2)}, u32[]{:S(2)}) collective-permute-start(bf16[4,32,896]{2,1,0:T(8,128)(2,1)S(1)} %get-tuple-element.24), channel_id=1, source_target_pairs={{0,8},{1,13},{2,10},{3,15},{4,12},{5,9},{6,14},{7,11},{8,0},{9,5},... | collective-permute-start | bytes 688136 | tf_op jit(solution)/shard_map/ppermute | solution.py:280
  25.5 10.3 %collective-permute-start.5 = (bf16[8,16,896]{2,1,0:T(8,128)(2,1)S(1)}, bf16[8,16,896]{2,1,0:T(8,128)(2,1)S(1)}, u32[]{:S(2)}, u32[]{:S(2)}) collective-permute-start(bf16[8,16,896]{2,1,0:T(8,128)(2,1)S(1)} %turn.6.refs_4_), channel_id=1, source_target_pairs={{0,24},{1,29},{2,26},{3,31},{4,28},{5,25},{6,30},{7,27},{8,16},{9,... | collective-permute-start | bytes 688136 | tf_op jit(solution)/shard_map/ppermute | solution.py:280
  27.7 1.4 %collective-permute-start.12 = (bf16[2,32,896]{2,1,0:T(8,128)(2,1)S(1)}, bf16[2,32,896]{2,1,0:T(8,128)(2,1)S(1)}, u32[]{:S(2)}, u32[]{:S(2)}) collective-permute-start(bf16[2,32,896]{2,1,0:T(8,128)(2,1)S(1)} %get-tuple-element.34), channel_id=1, source_target_pairs={{0,1},{1,0},{2,3},{3,2},{4,5},{5,4},{6,7},{7,6},{8,9},{9,8},{10,11... | collective-permute-start | bytes 344072 | tf_op jit(solution)/shard_map/ppermute | solution.py:283
  27.9 1.4 %collective-permute-start.13 = (bf16[2,32,896]{2,1,0:T(8,128)(2,1)S(1)}, bf16[2,32,896]{2,1,0:T(8,128)(2,1)S(1)}, u32[]{:S(2)}, u32[]{:S(2)}) collective-permute-start(bf16[2,32,896]{2,1,0:T(8,128)(2,1)S(1)} %get-tuple-element.33), channel_id=1, source_target_pairs={{0,1},{1,0},{2,3},{3,2},{4,5},{5,4},{6,7},{7,6},{8,9},{9,8},{10,11... | collective-permute-start | bytes 344072 | tf_op jit(solution)/shard_map/ppermute | solution.py:283
  28.3 1.4 %collective-permute-start.10 = (bf16[4,16,896]{2,1,0:T(8,128)(2,1)S(1)}, bf16[4,16,896]{2,1,0:T(8,128)(2,1)S(1)}, u32[]{:S(2)}, u32[]{:S(2)}) collective-permute-start(bf16[4,16,896]{2,1,0:T(8,128)(2,1)S(1)} %get-tuple-element.36), channel_id=1, source_target_pairs={{0,1},{1,0},{2,3},{3,2},{4,5},{5,4},{6,7},{7,6},{8,9},{9,8},{10,11... | collective-permute-start | bytes 344072 | tf_op jit(solution)/shard_map/ppermute | solution.py:283
  28.5 4.0 %collective-permute-start.11 = (bf16[4,16,896]{2,1,0:T(8,128)(2,1)S(1)}, bf16[4,16,896]{2,1,0:T(8,128)(2,1)S(1)}, u32[]{:S(2)}, u32[]{:S(2)}) collective-permute-start(bf16[4,16,896]{2,1,0:T(8,128)(2,1)S(1)} %get-tuple-element.35), channel_id=1, source_target_pairs={{0,1},{1,0},{2,3},{3,2},{4,5},{5,4},{6,7},{7,6},{8,9},{9,8},{10,11... | collective-permute-start | bytes 344072 | tf_op jit(solution)/shard_map/ppermute | solution.py:283
  29.1 4.7 %collective-permute-start.8 = (bf16[2,32,896]{2,1,0:T(8,128)(2,1)S(1)}, bf16[2,32,896]{2,1,0:T(8,128)(2,1)S(1)}, u32[]{:S(2)}, u32[]{:S(2)}) collective-permute-start(bf16[2,32,896]{2,1,0:T(8,128)(2,1)S(1)} %get-tuple-element.38), channel_id=1, source_target_pairs={{0,1},{1,0},{2,3},{3,2},{4,5},{5,4},{6,7},{7,6},{8,9},{9,8},{10,11... | collective-permute-start | bytes 344072 | tf_op jit(solution)/shard_map/ppermute | solution.py:283
  29.3 4.5 %collective-permute-start.9 = (bf16[2,32,896]{2,1,0:T(8,128)(2,1)S(1)}, bf16[2,32,896]{2,1,0:T(8,128)(2,1)S(1)}, u32[]{:S(2)}, u32[]{:S(2)}) collective-permute-start(bf16[2,32,896]{2,1,0:T(8,128)(2,1)S(1)} %get-tuple-element.37), channel_id=1, source_target_pairs={{0,1},{1,0},{2,3},{3,2},{4,5},{5,4},{6,7},{7,6},{8,9},{9,8},{10,11... | collective-permute-start | bytes 344072 | tf_op jit(solution)/shard_map/ppermute | solution.py:283
  29.7 7.7 %collective-permute-start.16 = (bf16[8,16,896]{2,1,0:T(8,128)(2,1)S(1)}, bf16[8,16,896]{2,1,0:T(8,128)(2,1)S(1)}, u32[]{:S(2)}, u32[]{:S(2)}) collective-permute-start(bf16[8,16,896]{2,1,0:T(8,128)(2,1)S(1)} %get-tuple-element.26.refs_0_), channel_id=1, source_target_pairs={{0,2},{1,3},{2,0},{3,1},{4,6},{5,7},{6,4},{7,5},{8,10},{9,11},{10,... | collective-permute-start | bytes 688136 | tf_op jit(solution)/shard_map/ppermute | solution.py:283
  32.5 8.1 %collective-permute-start.15 = (bf16[4,32,896]{2,1,0:T(8,128)(2,1)S(1)}, bf16[4,32,896]{2,1,0:T(8,128)(2,1)S(1)}, u32[]{:S(2)}, u32[]{:S(2)}) collective-permute-start(bf16[4,32,896]{2,1,0:T(8,128)(2,1)S(1)} %get-tuple-element.28), channel_id=1, source_target_pairs={{0,8},{1,13},{2,10},{3,15},{4,12},{5,9},{6,14},{7,11},{8,0},{9,5},... | collective-permute-start | bytes 688136 | tf_op jit(solution)/shard_map/ppermute | solution.py:280
  35.1 5.4 %copy-start = (bf16[2048,1024]{1,0:T(8,128)(2,1)S(1)}, bf16[2048,1024]{1,0:T(8,128)(2,1)}, u32[]{:S(2)}) copy-start(bf16[2048,1024]{1,0:T(8,128)(2,1)} %queries_ref.1) | copy-start | bytes 12582916
  35.8 7.8 %collective-permute-start.14 = (bf16[8,16,896]{2,1,0:T(8,128)(2,1)S(1)}, bf16[8,16,896]{2,1,0:T(8,128)(2,1)S(1)}, u32[]{:S(2)}, u32[]{:S(2)}) collective-permute-start(bf16[8,16,896]{2,1,0:T(8,128)(2,1)S(1)} %turn.8.refs_1_.refs_0_), channel_id=1, source_target_pairs={{0,2},{1,3},{2,0},{3,1},{4,6},{5,7},{6,4},{7,5},{8,10},{9,11},{10,... | collective-permute-start | bytes 688136 | tf_op jit(solution)/shard_map/ppermute | solution.py:283
  37.3 6.5 %collective-permute-start.22 = (bf16[8,16,896]{2,1,0:T(8,128)(2,1)S(1)}, bf16[8,16,896]{2,1,0:T(8,128)(2,1)S(1)}, u32[]{:S(2)}, u32[]{:S(2)}) collective-permute-start(bf16[8,16,896]{2,1,0:T(8,128)(2,1)S(1)} %turn.8.refs_1_.refs_0_), channel_id=1, source_target_pairs={{0,1},{1,0},{2,3},{3,2},{4,5},{5,4},{6,7},{7,6},{8,9},{9,8},{10,11... | collective-permute-start | bytes 688136 | tf_op jit(solution)/shard_map/ppermute | solution.py:283
  37.4 3.2 %collective-permute-start.19 = (bf16[4,16,896]{2,1,0:T(8,128)(2,1)S(1)}, bf16[4,16,896]{2,1,0:T(8,128)(2,1)S(1)}, u32[]{:S(2)}, u32[]{:S(2)}) collective-permute-start(bf16[4,16,896]{2,1,0:T(8,128)(2,1)S(1)} %get-tuple-element.30), channel_id=1, source_target_pairs={{0,1},{1,0},{2,3},{3,2},{4,5},{5,4},{6,7},{7,6},{8,9},{9,8},{10,11... | collective-permute-start | bytes 344072 | tf_op jit(solution)/shard_map/ppermute | solution.py:283
  37.9 3.2 %collective-permute-start.20 = (bf16[4,16,896]{2,1,0:T(8,128)(2,1)S(1)}, bf16[4,16,896]{2,1,0:T(8,128)(2,1)S(1)}, u32[]{:S(2)}, u32[]{:S(2)}) collective-permute-start(bf16[4,16,896]{2,1,0:T(8,128)(2,1)S(1)} %get-tuple-element.29), channel_id=1, source_target_pairs={{0,1},{1,0},{2,3},{3,2},{4,5},{5,4},{6,7},{7,6},{8,9},{9,8},{10,11... | collective-permute-start | bytes 344072 | tf_op jit(solution)/shard_map/ppermute | solution.py:283
  40.6 1.8 %collective-permute-start.17 = (bf16[2,32,896]{2,1,0:T(8,128)(2,1)S(1)}, bf16[2,32,896]{2,1,0:T(8,128)(2,1)S(1)}, u32[]{:S(2)}, u32[]{:S(2)}) collective-permute-start(bf16[2,32,896]{2,1,0:T(8,128)(2,1)S(1)} %get-tuple-element.32), channel_id=1, source_target_pairs={{0,1},{1,0},{2,3},{3,2},{4,5},{5,4},{6,7},{7,6},{8,9},{9,8},{10,11... | collective-permute-start | bytes 344072 | tf_op jit(solution)/shard_map/ppermute | solution.py:283
  40.7 1.8 %collective-permute-start.18 = (bf16[2,32,896]{2,1,0:T(8,128)(2,1)S(1)}, bf16[2,32,896]{2,1,0:T(8,128)(2,1)S(1)}, u32[]{:S(2)}, u32[]{:S(2)}) collective-permute-start(bf16[2,32,896]{2,1,0:T(8,128)(2,1)S(1)} %get-tuple-element.31), channel_id=1, source_target_pairs={{0,1},{1,0},{2,3},{3,2},{4,5},{5,4},{6,7},{7,6},{8,9},{9,8},{10,11... | collective-permute-start | bytes 344072 | tf_op jit(solution)/shard_map/ppermute | solution.py:283
  43.7 1.6 %collective-permute-start.21 = (bf16[8,16,896]{2,1,0:T(8,128)(2,1)S(1)}, bf16[8,16,896]{2,1,0:T(8,128)(2,1)S(1)}, u32[]{:S(2)}, u32[]{:S(2)}) collective-permute-start(bf16[8,16,896]{2,1,0:T(8,128)(2,1)S(1)} %turn.11.refs_0_), channel_id=1, source_target_pairs={{0,1},{1,0},{2,3},{3,2},{4,5},{5,4},{6,7},{7,6},{8,9},{9,8},{10,11... | collective-permute-start | bytes 688136 | tf_op jit(solution)/shard_map/ppermute | solution.py:283

commit v6 on v5

--- a/solution.py
+++ b/solution.py
@@ -57,16 +57,19 @@
     )(ids, stored)
 
 
-def pick_kernel(plans, *refs):
+def pick_kernel(plans, fetched, *refs):
     count = len(plans)
     asked, stored_ref, pieces = refs[:count], refs[count], refs[count + 1 : -5]
     here_ref, ids_at, table_ref, ids_sem, sem = refs[-5:]
+    if fetched:
+        here_ref, pieces = stored_ref, refs[count + 1 : -4]
     tile_count, rows, _ = stored_ref.shape
     fetches = [pltpu.make_async_copy(ref, ids_at.at[i], ids_sem.at[i]) for i, ref in enumerate(asked)]
     for fetch in fetches:
         fetch.start()
-    load = pltpu.make_async_copy(stored_ref, here_ref, sem)
-    load.start()
+    load = None if fetched else pltpu.make_async_copy(stored_ref, here_ref, sem)
+    if load is not None:
+        load.start()
     lowest, mp_at = lax.axis_index("seq") * tile_count, lax.axis_index("mp")
     half = pl.multiple_of(mp_at // 2 * (rows // 2), rows // 2)
     for i in range(count):
@@ -77,7 +80,8 @@
                 local = ids_at[i, k, c] - lowest
                 table_ref[i, found] = local
                 found += ((local >= 0) & (local < tile_count)).astype(jnp.int32)
-    load.wait()
+    if load is not None:
+        load.wait()
     at = 0
     for i, (kind, sizes) in enumerate(plans):
         rank = (mp_at % 2) * sizes[0] if kind == "tiles" else 0
@@ -89,22 +93,24 @@
             at += 1
 
 
-def pick(asked, stored, plans):
+def pick(asked, stored, plans, fetched):
     _, rows, width = stored.shape
     vmem = pl.BlockSpec(memory_space=pltpu.VMEM)
     shapes = [(size, rows // 2 if kind == "rows" else rows, width) for kind, sizes in plans for size in sizes]
-    return pl.pallas_call(
-        functools.partial(pick_kernel, plans),
-        out_shape=[pltpu.VMEM(shape, stored.dtype) for shape in [*shapes, stored.shape]],
-        in_specs=[vmem] * len(asked) + [pl.BlockSpec(memory_space=pl.ANY)],
-        out_specs=[vmem] * (len(shapes) + 1),
+    if not fetched:
+        shapes.append(stored.shape)
+    return pl.pallas_call(
+        functools.partial(pick_kernel, plans, fetched),
+        out_shape=[pltpu.VMEM(shape, stored.dtype) for shape in shapes],
+        in_specs=[vmem] * len(asked) + [vmem if fetched else pl.BlockSpec(memory_space=pl.ANY)],
+        out_specs=[vmem] * len(shapes),
         scratch_shapes=[
             pltpu.SMEM((len(plans), *asked[0].shape), jnp.int32),
             pltpu.SMEM((len(plans), asked[0].size + 1), jnp.int32),
             pltpu.SemaphoreType.DMA((len(plans),)),
             pltpu.SemaphoreType.DMA,
         ],
-        compiler_params=pltpu.CompilerParams(vmem_limit_bytes=52 * MIB),
+        compiler_params=pltpu.CompilerParams(vmem_limit_bytes=(16 if fetched else 52) * MIB),
         cost_estimate=LIGHT,
         name="pick",
     )(*[in_vmem(a) for a in asked], stored)
@@ -295,9 +301,12 @@
             (first + capacity, rows // 2, over_mp(theirs, 1)),
         ]
 
-    asked = [across(ids, p) for p in (2, 3, 1, 0)]
-    kinds = [("rows", [capacity]), ("rows", [capacity]), ("all", [early, capacity - early]), ("tiles", [size])]
-    picked2, picked3, *picked1, beside, stored = pick(asked, encoded, kinds)
+    asked = {p: across(ids, p) for p in (2, 3, 1, 0)}
+    kinds = [("rows", [capacity])]
+    picked2, stored = pick([asked[p] for p in (2,)], encoded, kinds, False)
+    kinds = [("rows", [capacity]), ("all", [early, capacity - early]), ("tiles", [size])]
+    picked3, *picked1, beside = pick([asked[p] for p in (3, 1, 0)], stored, kinds, True)
+    picked2 = turn([picked2], [asked[p] for p in (3, 1, 0)], 1)[0]
     got2, got1, beside = across(picked2, 2), across(picked1[0], 1), across(beside, 0)
     weights = in_vmem(w_kv.reshape(width, -1))
     slots, own = plan(ids, stored, capacity)

time: 52.1 us -> 50.9 us (0.977)
  waiting for transfers between devices: 9.36 us -> 6.94 us
  Pallas kernels: 18.7 us -> 19.9 us
    ppermute x7, waiting for transfers between devices: 8.84 us -> 5.69 us  [across(): lax.ppermute(value, both, joint(lambda s, m: (s ^ 2 * part ^ m % 2) * mp_...]
    pallas_call x1 -> x2, Pallas kernels: 1.67 us -> 2.9 us  [pick(): pl.pallas_call(functools.partial(pick_kernel, plans, fetched), out_shape=...]
    ppermute x14, waiting for transfers between devices: 0.51 us -> 1.24 us  [over_mp(): return lax.ppermute(value, 'mp', [(m, m ^ flip) for m in range(mp_count)])]
  transfers between devices with their start and end apart: 23 -> 23, of which waited for: 8 -> 8; matrix products, arithmetic and copies ran while one was open for 6% -> 7% of each run, Pallas kernels for 20% -> 26%
where the time goes in v6:
time: 50.9 us; the launch traced here: 50.7 us
  starting transfers between devices  20.1 us (39%)
  Pallas kernels  19.9 us (39%)
  waiting for transfers between devices  6.94 us (14%)
  local copies, waits for them, and re-layouts  3.38 us (7%)
    ppermute x7, starting transfers between devices, across(): lax.ppermute(value, both, joint(lambda s, m: (s ^ 2 * part ^ m % 2) * mp_...  11.1 us
    pallas_call x8, Pallas kernels, project(): pl.pallas_call(functools.partial(project_kernel, [(tile, row) for tile, r...  9.98 us
    ppermute x14, starting transfers between devices, over_mp(): return lax.ppermute(value, 'mp', [(m, m ^ flip) for m in range(mp_count)])  5.89 us
    ppermute x7, waiting for transfers between devices, across(): lax.ppermute(value, both, joint(lambda s, m: (s ^ 2 * part ^ m % 2) * mp_...  5.69 us
    pallas_call x1, Pallas kernels, attend(): pl.pallas_call(functools.partial(attend_kernel, heads, per), out_shape=ja...  5.31 us
    unnamed x5, local copies, waits for them, and re-layouts  3.28 us
    ppermute x2, starting transfers between devices, across(): return lax.ppermute(value, 'seq', [(s, s ^ 1) for s in range(seq_count)])  3.1 us
    pallas_call x2, Pallas kernels, pick(): pl.pallas_call(functools.partial(pick_kernel, plans, fetched), out_shape=...  2.9 us
  transfers between devices with their start and end apart: 23, of which 8 were waited for; matrix products, arithmetic and copies ran while one was open for 7% of the time, Pallas kernels for 26%

profile of v6, /device:TPU:0, one launch (start us, length us, event | category | flops | bytes accessed | tf_op | source)
XLA Modules:
  0.0 50.7 jit_solution(13943820931168310120)
XLA Ops:
  0.0 4.0 %collective-permute-start = (s32[2,32]{1,0:T(2,128)}, s32[2,32]{1,0:T(2,128)S(1)}, u32[]{:S(2)}, u32[]{:S(2)}) collective-permute-start(s32[2,32]{1,0:T(2,128)} %bitcast.11), channel_id=1, source_target_pairs={{0,16},{1,21},{2,18},{3,23},{4,20},{5,17},{6,22},{7,19},{8,24},{9,... | collective-permute-start | bytes 776 | tf_op jit(solution)/shard_map/ppermute | solution.py:286
  4.0 1.3 %collective-permute-start.1 = (s32[2,32]{1,0:T(2,128)}, s32[2,32]{1,0:T(2,128)S(1)}, u32[]{:S(2)}, u32[]{:S(2)}) collective-permute-start(s32[2,32]{1,0:T(2,128)} %bitcast.12), channel_id=1, source_target_pairs={{0,24},{1,29},{2,26},{3,31},{4,28},{5,25},{6,30},{7,27},{8,16},{9,... | collective-permute-start | bytes 776 | tf_op jit(solution)/shard_map/ppermute | solution.py:286
  5.6 1.5 %collective-permute-start.3 = (s32[2,32]{1,0:T(2,128)}, s32[2,32]{1,0:T(2,128)S(1)}, u32[]{:S(2)}, u32[]{:S(2)}) collective-permute-start(s32[2,32]{1,0:T(2,128)} %bitcast.14), channel_id=1, source_target_pairs={{0,4},{4,0},{8,12},{12,8},{16,20},{20,16},{24,28},{28,24},{1,5},{5... | collective-permute-start | bytes 776 | tf_op jit(solution)/shard_map/ppermute | solution.py:285
  7.1 1.5 %pick.2 = (bf16[8,16,896]{2,1,0:T(8,128)(2,1)S(1)}, bf16[32,32,896]{2,1,0:T(8,128)(2,1)S(1)}) custom-call(s32[2,32]{1,0:T(2,128)S(1)} %collective-permute-done.refs_0_, bf16[32,32,896]{2,1,0:T(8,128)(2,1)} %refs_1_.1), custom_call_target="tpu_custom_call" | custom-call | flops 1 | bytes 1 | tf_op jit(solution)/shard_map/pick/pallas_call | solution.py:102
  8.7 0.9 %collective-permute-done.1.refs_0_.refs_1_ = s32[2,32]{1,0:T(2,128)S(1)} collective-permute-done((s32[2,32]{1,0:T(2,128)}, s32[2,32]{1,0:T(2,128)S(1)}, u32[]{:S(2)}, u32[]{:S(2)}) %collective-permute-start.1) | collective-permute-done | bytes 288 | tf_op jit(solution)/shard_map/ppermute | solution.py:286
  9.6 2.6 %collective-permute-start.4 = (bf16[8,16,896]{2,1,0:T(8,128)(2,1)S(1)}, bf16[8,16,896]{2,1,0:T(8,128)(2,1)S(1)}, u32[]{:S(2)}, u32[]{:S(2)}) collective-permute-start(bf16[8,16,896]{2,1,0:T(8,128)(2,1)S(1)} %turn.7), channel_id=1, source_target_pairs={{0,16},{1,21},{2,18},{3,23},{4,20},{5,17},{6,22},{7,19},{8,24},{9,... | collective-permute-start | bytes 688136 | tf_op jit(solution)/shard_map/ppermute | solution.py:286
  12.2 1.4 %pick.3 = (bf16[8,16,896]{2,1,0:T(8,128)(2,1)S(1)}, bf16[4,32,896]{2,1,0:T(8,128)(2,1)S(1)}, bf16[4,32,896]{2,1,0:T(8,128)(2,1)S(1)}, bf16[4,32,896]{2,1,0:T(8,128)(2,1)S(1)}) custom-call(s32[2,32]{1,0:T(2,128)S(1)} %collective-permute-done.1.refs_0_.refs_1_, s32[2,32]{1,0:T(2,128)S(1)} %collective-permute-done.2.refs_1_.refs_2_, ...), custom_call_target="tpu_custom_call" | custom-call | flops 1 | bytes 1 | tf_op jit(solution)/shard_map/pick/pallas_call | solution.py:102
  13.6 1.6 %collective-permute-start.6 = (bf16[4,32,896]{2,1,0:T(8,128)(2,1)S(1)}, bf16[4,32,896]{2,1,0:T(8,128)(2,1)S(1)}, u32[]{:S(2)}, u32[]{:S(2)}) collective-permute-start(bf16[4,32,896]{2,1,0:T(8,128)(2,1)S(1)} %get-tuple-element.23), channel_id=1, source_target_pairs={{0,4},{4,0},{8,12},{12,8},{16,20},{20,16},{24,28},{28,24},{1,5},{5... | collective-permute-start | bytes 688136 | tf_op jit(solution)/shard_map/ppermute | solution.py:285
  15.2 0.7 %collective-permute-start.7 = (bf16[4,32,896]{2,1,0:T(8,128)(2,1)S(1)}, bf16[4,32,896]{2,1,0:T(8,128)(2,1)S(1)}, u32[]{:S(2)}, u32[]{:S(2)}) collective-permute-start(bf16[4,32,896]{2,1,0:T(8,128)(2,1)S(1)} %get-tuple-element.24), channel_id=1, source_target_pairs={{0,8},{1,13},{2,10},{3,15},{4,12},{5,9},{6,14},{7,11},{8,0},{9,5},... | collective-permute-start | bytes 688136 | tf_op jit(solution)/shard_map/ppermute | solution.py:286
  15.8 3.3 %copy.22 = bf16[112,8,2,1024]{3,1,2,0:T(8,128)(2,1)S(1)} copy(bf16[112,8,2,1024]{3,2,1,0:T(2,128)(2,1)} %bitcast.16) | data formatting | bytes 7340032
  19.1 1.7 %plan.1 = (s32[64]{0:T(128)S(1)}, bf16[8,32,896]{2,1,0:T(8,128)(2,1)S(1)}) custom-call(s32[2,32]{1,0:T(2,128)S(1)} %bitcast.15, bf16[32,32,896]{2,1,0:T(8,128)(2,1)S(1)} %get-tuple-element.17.stored_ref.refs_3_), custom_call_target="tpu_custom_call" | custom-call | flops 1 | bytes 1 | tf_op jit(solution)/shard_map/plan/pallas_call | solution.py:45
  20.8 1.2 %project.8.refs_2_.refs_4_ = bf16[64,32,2048]{2,1,0:T(8,128)(2,1)S(1)} custom-call(bf16[8,32,896]{2,1,0:T(8,128)(2,1)S(1)} %get-tuple-element.21.refs_0_, bf16[896,2048]{1,0:T(8,128)(2,1)S(1)} %bitcast.3), custom_call_target="tpu_custom_call" | custom-call | flops 117440512 | tf_op jit(solution)/shard_map/project/pallas_call | solution.py:162
  22.1 1.7 %collective-permute-done.4.refs_1_.refs_3_ = bf16[8,16,896]{2,1,0:T(8,128)(2,1)S(1)} collective-permute-done((bf16[8,16,896]{2,1,0:T(8,128)(2,1)S(1)}, bf16[8,16,896]{2,1,0:T(8,128)(2,1)S(1)}, u32[]{:S(2)}, u32[]{:S(2)}) %collective-permute-start.4) | collective-permute-done | bytes 229408 | tf_op jit(solution)/shard_map/ppermute | solution.py:286
  23.8 2.2 %collective-permute-start.5 = (bf16[8,16,896]{2,1,0:T(8,128)(2,1)S(1)}, bf16[8,16,896]{2,1,0:T(8,128)(2,1)S(1)}, u32[]{:S(2)}, u32[]{:S(2)}) collective-permute-start(bf16[8,16,896]{2,1,0:T(8,128)(2,1)S(1)} %turn.8.refs_4_), channel_id=1, source_target_pairs={{0,24},{1,29},{2,26},{3,31},{4,28},{5,25},{6,30},{7,27},{8,16},{9,... | collective-permute-start | bytes 688136 | tf_op jit(solution)/shard_map/ppermute | solution.py:286
  26.0 0.7 %collective-permute-done.7.refs_2_ = bf16[4,32,896]{2,1,0:T(8,128)(2,1)S(1)} collective-permute-done((bf16[4,32,896]{2,1,0:T(8,128)(2,1)S(1)}, bf16[4,32,896]{2,1,0:T(8,128)(2,1)S(1)}, u32[]{:S(2)}, u32[]{:S(2)}) %collective-permute-start.7) | collective-permute-done | bytes 229408 | tf_op jit(solution)/shard_map/ppermute | solution.py:286
  26.7 0.5 collective-permute-start.13
  27.4 0.4 collective-permute-start.11
  28.2 0.3 collective-permute-start.9
  28.6 1.5 %collective-permute-start.16 = (bf16[8,16,896]{2,1,0:T(8,128)(2,1)S(1)}, bf16[8,16,896]{2,1,0:T(8,128)(2,1)S(1)}, u32[]{:S(2)}, u32[]{:S(2)}) collective-permute-start(bf16[8,16,896]{2,1,0:T(8,128)(2,1)S(1)} %get-tuple-element.26.refs_0_), channel_id=1, source_target_pairs={{0,2},{1,3},{2,0},{3,1},{4,6},{5,7},{6,4},{7,5},{8,10},{9,11},{10,... | collective-permute-start | bytes 688136 | tf_op jit(solution)/shard_map/ppermute | solution.py:289
  30.1 1.2 %project.9.refs_4_ = bf16[64,32,2048]{2,1,0:T(8,128)(2,1)S(1)} custom-call(bf16[4,32,896]{2,1,0:T(8,128)(2,1)S(1)} %get-tuple-element.27.refs_0_, bf16[2,32,896]{2,1,0:T(8,128)(2,1)S(1)} %collective-permute-done.12.refs_1_, bf16[2,32,896]{2,1,0:T(8,128)(2,1)S(1)} %collective-permute-done.13.refs_2_, ...), custom_call_target="tpu_custom_call", output_to_operand_aliasing={{}: (4, {})} | custom-call | flops 117440512 | tf_op jit(solution)/shard_map/project/pallas_call | solution.py:162
  31.5 1.2 %project.10.refs_4_ = bf16[64,32,2048]{2,1,0:T(8,128)(2,1)S(1)} custom-call(bf16[8,16,896]{2,1,0:T(8,128)(2,1)S(1)} %get-tuple-element.26.refs_0_, bf16[4,16,896]{2,1,0:T(8,128)(2,1)S(1)} %collective-permute-done.10.refs_1_, bf16[4,16,896]{2,1,0:T(8,128)(2,1)S(1)} %collective-permute-done.11.refs_2_, ...), custom_call_target="tpu_custom_call", output_to_operand_aliasing={{}: (4, {})} | custom-call | flops 117440512 | tf_op jit(solution)/shard_map/project/pallas_call | solution.py:162
  32.8 1.2 %project.11.refs_1_.refs_4_ = bf16[64,32,2048]{2,1,0:T(8,128)(2,1)S(1)} custom-call(bf16[4,32,896]{2,1,0:T(8,128)(2,1)S(1)} %get-tuple-element.25.refs_0_, bf16[2,32,896]{2,1,0:T(8,128)(2,1)S(1)} %collective-permute-done.8.refs_1_, bf16[2,32,896]{2,1,0:T(8,128)(2,1)S(1)} %collective-permute-done.9.refs_2_, ...), custom_call_target="tpu_custom_call", output_to_operand_aliasing={{}: (4, {})} | custom-call | flops 117440512 | tf_op jit(solution)/shard_map/project/pallas_call | solution.py:162
  34.0 1.5 %collective-permute-start.14 = (bf16[8,16,896]{2,1,0:T(8,128)(2,1)S(1)}, bf16[8,16,896]{2,1,0:T(8,128)(2,1)S(1)}, u32[]{:S(2)}, u32[]{:S(2)}) collective-permute-start(bf16[8,16,896]{2,1,0:T(8,128)(2,1)S(1)} %turn.10.refs_1_.refs_0_), channel_id=1, source_target_pairs={{0,2},{1,3},{2,0},{3,1},{4,6},{5,7},{6,4},{7,5},{8,10},{9,11},{10,... | collective-permute-start | bytes 688136 | tf_op jit(solution)/shard_map/ppermute | solution.py:289
  35.5 0.8 %collective-permute-done.16.refs_0_ = bf16[8,16,896]{2,1,0:T(8,128)(2,1)S(1)} collective-permute-done((bf16[8,16,896]{2,1,0:T(8,128)(2,1)S(1)}, bf16[8,16,896]{2,1,0:T(8,128)(2,1)S(1)}, u32[]{:S(2)}, u32[]{:S(2)}) %collective-permute-start.16) | collective-permute-done | bytes 229408 | tf_op jit(solution)/shard_map/ppermute | solution.py:289
  36.4 0.5 collective-permute-start.20
  36.9 2.4 %collective-permute-done.15.refs_0_ = bf16[4,32,896]{2,1,0:T(8,128)(2,1)S(1)} collective-permute-done((bf16[4,32,896]{2,1,0:T(8,128)(2,1)S(1)}, bf16[4,32,896]{2,1,0:T(8,128)(2,1)S(1)}, u32[]{:S(2)}, u32[]{:S(2)}) %collective-permute-start.15) | collective-permute-done | bytes 229408 | tf_op jit(solution)/shard_map/ppermute | solution.py:286
  39.4 0.5 collective-permute-start.18
  39.9 1.2 %project.12.refs_4_ = bf16[64,32,2048]{2,1,0:T(8,128)(2,1)S(1)} custom-call(bf16[8,16,896]{2,1,0:T(8,128)(2,1)S(1)} %turn.11.refs_1_.refs_0_, bf16[4,16,896]{2,1,0:T(8,128)(2,1)S(1)} %collective-permute-done.19.refs_1_, bf16[4,16,896]{2,1,0:T(8,128)(2,1)S(1)} %collective-permute-done.20.refs_2_, ...), custom_call_target="tpu_custom_call", output_to_operand_aliasing={{}: (4, {})} | custom-call | flops 117440512 | tf_op jit(solution)/shard_map/project/pallas_call | solution.py:162
  41.2 1.2 %project.13.refs_1_.refs_3_ = bf16[64,32,2048]{2,1,0:T(8,128)(2,1)S(1)} custom-call(bf16[4,32,896]{2,1,0:T(8,128)(2,1)S(1)} %turn.12.refs_0_, bf16[2,32,896]{2,1,0:T(8,128)(2,1)S(1)} %collective-permute-done.17.refs_1_, bf16[2,32,896]{2,1,0:T(8,128)(2,1)S(1)} %collective-permute-done.18.refs_2_, ...), custom_call_target="tpu_custom_call", output_to_operand_aliasing={{}: (4, {})} | custom-call | flops 117440512 | tf_op jit(solution)/shard_map/project/pallas_call | solution.py:162
  42.6 1.2 %project.14.refs_3_ = bf16[64,32,2048]{2,1,0:T(8,128)(2,1)S(1)} custom-call(bf16[8,16,896]{2,1,0:T(8,128)(2,1)S(1)} %turn.10.refs_1_.refs_0_, bf16[8,16,896]{2,1,0:T(8,128)(2,1)S(1)} %collective-permute-done.22.refs_1_, bf16[896,2048]{1,0:T(8,128)(2,1)S(1)} %bitcast.9, bf16[64,32,2048]{2,1,0:T(8,128)(2,1)S(1)} %project.13.refs_1_.refs_3_), custom_call_target="tpu_custom_call", output_to_operand_aliasing={{}: (3, {})} | custom-call | flops 7516192768 | tf_op jit(solution)/shard_map/project/pallas_call | solution.py:162
  44.0 1.2 %project.15.held_ref = bf16[64,32,2048]{2,1,0:T(8,128)(2,1)S(1)} custom-call(bf16[8,16,896]{2,1,0:T(8,128)(2,1)S(1)} %turn.13.refs_0_, bf16[8,16,896]{2,1,0:T(8,128)(2,1)S(1)} %collective-permute-done.21.refs_1_, bf16[896,2048]{1,0:T(8,128)(2,1)S(1)} %bitcast.10, bf16[64,32,2048]{2,1,0:T(8,128)(2,1)S(1)} %project.14.refs_3_), custom_call_target="tpu_custom_call", output_to_operand_aliasing={{}: (3, {})} | custom-call | flops 7516192768 | tf_op jit(solution)/shard_map/project/pallas_call | solution.py:162
  45.3 5.3 %attend.1 = bf16[2048,1024]{1,0:T(8,128)(2,1)} custom-call(s32[64]{0:T(128)S(1)} %get-tuple-element.18.refs_3_.slots_ref, bf16[2048,1024]{1,0:T(8,128)(2,1)S(1)} %copy-done, bf16[64,32,2048]{2,1,0:T(8,128)(2,1)S(1)} %project.15.held_ref), custom_call_target="tpu_custom_call" | custom-call | flops 1000000000 | bytes 16777216 | tf_op jit(solution)/shard_map/attend/pallas_call | solution.py:234
  (43 shorter events, 1.5 us)
Async XLA Ops:
  0.0 19.1 %copy-start.1 = (s32[32,2]{0,1:T(2,128)S(1)}, s32[32,2]{0,1:T(2,128)}, u32[]{:S(2)}) copy-start(s32[32,2]{0,1:T(2,128)} %param.7) | copy-start | bytes 772
  0.0 7.1 %collective-permute-start = (s32[2,32]{1,0:T(2,128)}, s32[2,32]{1,0:T(2,128)S(1)}, u32[]{:S(2)}, u32[]{:S(2)}) collective-permute-start(s32[2,32]{1,0:T(2,128)} %bitcast.11), channel_id=1, source_target_pairs={{0,16},{1,21},{2,18},{3,23},{4,20},{5,17},{6,22},{7,19},{8,24},{9,... | collective-permute-start | bytes 776 | tf_op jit(solution)/shard_map/ppermute | solution.py:286
  4.0 5.6 %collective-permute-start.1 = (s32[2,32]{1,0:T(2,128)}, s32[2,32]{1,0:T(2,128)S(1)}, u32[]{:S(2)}, u32[]{:S(2)}) collective-permute-start(s32[2,32]{1,0:T(2,128)} %bitcast.12), channel_id=1, source_target_pairs={{0,24},{1,29},{2,26},{3,31},{4,28},{5,25},{6,30},{7,27},{8,16},{9,... | collective-permute-start | bytes 776 | tf_op jit(solution)/shard_map/ppermute | solution.py:286
  5.4 4.2 %collective-permute-start.2 = (s32[2,32]{1,0:T(2,128)}, s32[2,32]{1,0:T(2,128)S(1)}, u32[]{:S(2)}, u32[]{:S(2)}) collective-permute-start(s32[2,32]{1,0:T(2,128)} %bitcast.13), channel_id=1, source_target_pairs={{0,8},{1,13},{2,10},{3,15},{4,12},{5,9},{6,14},{7,11},{8,0},{9,5},... | collective-permute-start | bytes 776 | tf_op jit(solution)/shard_map/ppermute | solution.py:286
  5.6 4.0 %collective-permute-start.3 = (s32[2,32]{1,0:T(2,128)}, s32[2,32]{1,0:T(2,128)S(1)}, u32[]{:S(2)}, u32[]{:S(2)}) collective-permute-start(s32[2,32]{1,0:T(2,128)} %bitcast.14), channel_id=1, source_target_pairs={{0,4},{4,0},{8,12},{12,8},{16,20},{20,16},{24,28},{28,24},{1,5},{5... | collective-permute-start | bytes 776 | tf_op jit(solution)/shard_map/ppermute | solution.py:285
  9.6 14.1 %collective-permute-start.4 = (bf16[8,16,896]{2,1,0:T(8,128)(2,1)S(1)}, bf16[8,16,896]{2,1,0:T(8,128)(2,1)S(1)}, u32[]{:S(2)}, u32[]{:S(2)}) collective-permute-start(bf16[8,16,896]{2,1,0:T(8,128)(2,1)S(1)} %turn.7), channel_id=1, source_target_pairs={{0,16},{1,21},{2,18},{3,23},{4,20},{5,17},{6,22},{7,19},{8,24},{9,... | collective-permute-start | bytes 688136 | tf_op jit(solution)/shard_map/ppermute | solution.py:286
  13.6 12.4 %collective-permute-start.6 = (bf16[4,32,896]{2,1,0:T(8,128)(2,1)S(1)}, bf16[4,32,896]{2,1,0:T(8,128)(2,1)S(1)}, u32[]{:S(2)}, u32[]{:S(2)}) collective-permute-start(bf16[4,32,896]{2,1,0:T(8,128)(2,1)S(1)} %get-tuple-element.23), channel_id=1, source_target_pairs={{0,4},{4,0},{8,12},{12,8},{16,20},{20,16},{24,28},{28,24},{1,5},{5... | collective-permute-start | bytes 688136 | tf_op jit(solution)/shard_map/ppermute | solution.py:285
  15.2 11.5 %collective-permute-start.7 = (bf16[4,32,896]{2,1,0:T(8,128)(2,1)S(1)}, bf16[4,32,896]{2,1,0:T(8,128)(2,1)S(1)}, u32[]{:S(2)}, u32[]{:S(2)}) collective-permute-start(bf16[4,32,896]{2,1,0:T(8,128)(2,1)S(1)} %get-tuple-element.24), channel_id=1, source_target_pairs={{0,8},{1,13},{2,10},{3,15},{4,12},{5,9},{6,14},{7,11},{8,0},{9,5},... | collective-permute-start | bytes 688136 | tf_op jit(solution)/shard_map/ppermute | solution.py:286
  23.8 10.3 %collective-permute-start.5 = (bf16[8,16,896]{2,1,0:T(8,128)(2,1)S(1)}, bf16[8,16,896]{2,1,0:T(8,128)(2,1)S(1)}, u32[]{:S(2)}, u32[]{:S(2)}) collective-permute-start(bf16[8,16,896]{2,1,0:T(8,128)(2,1)S(1)} %turn.8.refs_4_), channel_id=1, source_target_pairs={{0,24},{1,29},{2,26},{3,31},{4,28},{5,25},{6,30},{7,27},{8,16},{9,... | collective-permute-start | bytes 688136 | tf_op jit(solution)/shard_map/ppermute | solution.py:286
  26.7 1.4 %collective-permute-start.12 = (bf16[2,32,896]{2,1,0:T(8,128)(2,1)S(1)}, bf16[2,32,896]{2,1,0:T(8,128)(2,1)S(1)}, u32[]{:S(2)}, u32[]{:S(2)}) collective-permute-start(bf16[2,32,896]{2,1,0:T(8,128)(2,1)S(1)} %get-tuple-element.34), channel_id=1, source_target_pairs={{0,1},{1,0},{2,3},{3,2},{4,5},{5,4},{6,7},{7,6},{8,9},{9,8},{10,11... | collective-permute-start | bytes 344072 | tf_op jit(solution)/shard_map/ppermute | solution.py:289
  26.7 1.5 %collective-permute-start.13 = (bf16[2,32,896]{2,1,0:T(8,128)(2,1)S(1)}, bf16[2,32,896]{2,1,0:T(8,128)(2,1)S(1)}, u32[]{:S(2)}, u32[]{:S(2)}) collective-permute-start(bf16[2,32,896]{2,1,0:T(8,128)(2,1)S(1)} %get-tuple-element.33), channel_id=1, source_target_pairs={{0,1},{1,0},{2,3},{3,2},{4,5},{5,4},{6,7},{7,6},{8,9},{9,8},{10,11... | collective-permute-start | bytes 344072 | tf_op jit(solution)/shard_map/ppermute | solution.py:289
  27.3 1.4 %collective-permute-start.10 = (bf16[4,16,896]{2,1,0:T(8,128)(2,1)S(1)}, bf16[4,16,896]{2,1,0:T(8,128)(2,1)S(1)}, u32[]{:S(2)}, u32[]{:S(2)}) collective-permute-start(bf16[4,16,896]{2,1,0:T(8,128)(2,1)S(1)} %get-tuple-element.36), channel_id=1, source_target_pairs={{0,1},{1,0},{2,3},{3,2},{4,5},{5,4},{6,7},{7,6},{8,9},{9,8},{10,11... | collective-permute-start | bytes 344072 | tf_op jit(solution)/shard_map/ppermute | solution.py:289
  27.4 4.0 %collective-permute-start.11 = (bf16[4,16,896]{2,1,0:T(8,128)(2,1)S(1)}, bf16[4,16,896]{2,1,0:T(8,128)(2,1)S(1)}, u32[]{:S(2)}, u32[]{:S(2)}) collective-permute-start(bf16[4,16,896]{2,1,0:T(8,128)(2,1)S(1)} %get-tuple-element.35), channel_id=1, source_target_pairs={{0,1},{1,0},{2,3},{3,2},{4,5},{5,4},{6,7},{7,6},{8,9},{9,8},{10,11... | collective-permute-start | bytes 344072 | tf_op jit(solution)/shard_map/ppermute | solution.py:289
  28.0 4.7 %collective-permute-start.8 = (bf16[2,32,896]{2,1,0:T(8,128)(2,1)S(1)}, bf16[2,32,896]{2,1,0:T(8,128)(2,1)S(1)}, u32[]{:S(2)}, u32[]{:S(2)}) collective-permute-start(bf16[2,32,896]{2,1,0:T(8,128)(2,1)S(1)} %get-tuple-element.38), channel_id=1, source_target_pairs={{0,1},{1,0},{2,3},{3,2},{4,5},{5,4},{6,7},{7,6},{8,9},{9,8},{10,11... | collective-permute-start | bytes 344072 | tf_op jit(solution)/shard_map/ppermute | solution.py:289
  28.2 4.5 %collective-permute-start.9 = (bf16[2,32,896]{2,1,0:T(8,128)(2,1)S(1)}, bf16[2,32,896]{2,1,0:T(8,128)(2,1)S(1)}, u32[]{:S(2)}, u32[]{:S(2)}) collective-permute-start(bf16[2,32,896]{2,1,0:T(8,128)(2,1)S(1)} %get-tuple-element.37), channel_id=1, source_target_pairs={{0,1},{1,0},{2,3},{3,2},{4,5},{5,4},{6,7},{7,6},{8,9},{9,8},{10,11... | collective-permute-start | bytes 344072 | tf_op jit(solution)/shard_map/ppermute | solution.py:289
  28.6 7.7 %collective-permute-start.16 = (bf16[8,16,896]{2,1,0:T(8,128)(2,1)S(1)}, bf16[8,16,896]{2,1,0:T(8,128)(2,1)S(1)}, u32[]{:S(2)}, u32[]{:S(2)}) collective-permute-start(bf16[8,16,896]{2,1,0:T(8,128)(2,1)S(1)} %get-tuple-element.26.refs_0_), channel_id=1, source_target_pairs={{0,2},{1,3},{2,0},{3,1},{4,6},{5,7},{6,4},{7,5},{8,10},{9,11},{10,... | collective-permute-start | bytes 688136 | tf_op jit(solution)/shard_map/ppermute | solution.py:289
  31.4 7.9 %collective-permute-start.15 = (bf16[4,32,896]{2,1,0:T(8,128)(2,1)S(1)}, bf16[4,32,896]{2,1,0:T(8,128)(2,1)S(1)}, u32[]{:S(2)}, u32[]{:S(2)}) collective-permute-start(bf16[4,32,896]{2,1,0:T(8,128)(2,1)S(1)} %get-tuple-element.28), channel_id=1, source_target_pairs={{0,8},{1,13},{2,10},{3,15},{4,12},{5,9},{6,14},{7,11},{8,0},{9,5},... | collective-permute-start | bytes 688136 | tf_op jit(solution)/shard_map/ppermute | solution.py:286
  34.0 5.3 %copy-start = (bf16[2048,1024]{1,0:T(8,128)(2,1)S(1)}, bf16[2048,1024]{1,0:T(8,128)(2,1)}, u32[]{:S(2)}) copy-start(bf16[2048,1024]{1,0:T(8,128)(2,1)} %queries_ref.1) | copy-start | bytes 12582916
  34.0 8.4 %collective-permute-start.14 = (bf16[8,16,896]{2,1,0:T(8,128)(2,1)S(1)}, bf16[8,16,896]{2,1,0:T(8,128)(2,1)S(1)}, u32[]{:S(2)}, u32[]{:S(2)}) collective-permute-start(bf16[8,16,896]{2,1,0:T(8,128)(2,1)S(1)} %turn.10.refs_1_.refs_0_), channel_id=1, source_target_pairs={{0,2},{1,3},{2,0},{3,1},{4,6},{5,7},{6,4},{7,5},{8,10},{9,11},{10,... | collective-permute-start | bytes 688136 | tf_op jit(solution)/shard_map/ppermute | solution.py:289
  35.5 7.1 %collective-permute-start.22 = (bf16[8,16,896]{2,1,0:T(8,128)(2,1)S(1)}, bf16[8,16,896]{2,1,0:T(8,128)(2,1)S(1)}, u32[]{:S(2)}, u32[]{:S(2)}) collective-permute-start(bf16[8,16,896]{2,1,0:T(8,128)(2,1)S(1)} %turn.10.refs_1_.refs_0_), channel_id=1, source_target_pairs={{0,1},{1,0},{2,3},{3,2},{4,5},{5,4},{6,7},{7,6},{8,9},{9,8},{10,11... | collective-permute-start | bytes 688136 | tf_op jit(solution)/shard_map/ppermute | solution.py:289
  36.3 3.1 %collective-permute-start.19 = (bf16[4,16,896]{2,1,0:T(8,128)(2,1)S(1)}, bf16[4,16,896]{2,1,0:T(8,128)(2,1)S(1)}, u32[]{:S(2)}, u32[]{:S(2)}) collective-permute-start(bf16[4,16,896]{2,1,0:T(8,128)(2,1)S(1)} %get-tuple-element.30), channel_id=1, source_target_pairs={{0,1},{1,0},{2,3},{3,2},{4,5},{5,4},{6,7},{7,6},{8,9},{9,8},{10,11... | collective-permute-start | bytes 344072 | tf_op jit(solution)/shard_map/ppermute | solution.py:289
  36.4 3.5 %collective-permute-start.20 = (bf16[4,16,896]{2,1,0:T(8,128)(2,1)S(1)}, bf16[4,16,896]{2,1,0:T(8,128)(2,1)S(1)}, u32[]{:S(2)}, u32[]{:S(2)}) collective-permute-start(bf16[4,16,896]{2,1,0:T(8,128)(2,1)S(1)} %get-tuple-element.29), channel_id=1, source_target_pairs={{0,1},{1,0},{2,3},{3,2},{4,5},{5,4},{6,7},{7,6},{8,9},{9,8},{10,11... | collective-permute-start | bytes 344072 | tf_op jit(solution)/shard_map/ppermute | solution.py:289
  39.3 1.8 %collective-permute-start.17 = (bf16[2,32,896]{2,1,0:T(8,128)(2,1)S(1)}, bf16[2,32,896]{2,1,0:T(8,128)(2,1)S(1)}, u32[]{:S(2)}, u32[]{:S(2)}) collective-permute-start(bf16[2,32,896]{2,1,0:T(8,128)(2,1)S(1)} %get-tuple-element.32), channel_id=1, source_target_pairs={{0,1},{1,0},{2,3},{3,2},{4,5},{5,4},{6,7},{7,6},{8,9},{9,8},{10,11... | collective-permute-start | bytes 344072 | tf_op jit(solution)/shard_map/ppermute | solution.py:289
  39.4 1.8 %collective-permute-start.18 = (bf16[2,32,896]{2,1,0:T(8,128)(2,1)S(1)}, bf16[2,32,896]{2,1,0:T(8,128)(2,1)S(1)}, u32[]{:S(2)}, u32[]{:S(2)}) collective-permute-start(bf16[2,32,896]{2,1,0:T(8,128)(2,1)S(1)} %get-tuple-element.31), channel_id=1, source_target_pairs={{0,1},{1,0},{2,3},{3,2},{4,5},{5,4},{6,7},{7,6},{8,9},{9,8},{10,11... | collective-permute-start | bytes 344072 | tf_op jit(solution)/shard_map/ppermute | solution.py:289
  42.5 1.6 %collective-permute-start.21 = (bf16[8,16,896]{2,1,0:T(8,128)(2,1)S(1)}, bf16[8,16,896]{2,1,0:T(8,128)(2,1)S(1)}, u32[]{:S(2)}, u32[]{:S(2)}) collective-permute-start(bf16[8,16,896]{2,1,0:T(8,128)(2,1)S(1)} %turn.13.refs_0_), channel_id=1, source_target_pairs={{0,1},{1,0},{2,3},{3,2},{4,5},{5,4},{6,7},{7,6},{8,9},{9,8},{10,11... | collective-permute-start | bytes 688136 | tf_op jit(solution)/shard_map/ppermute | solution.py:289

commit v7 on v6

--- a/solution.py
+++ b/solution.py
@@ -138,7 +138,7 @@
 def project_kernel(places, *refs):
     pieces, weights_ref, out_ref = refs[: len(places)], refs[len(places)], refs[-1]
     flat = jnp.concatenate([piece[...].reshape(-1, piece.shape[2]) for piece in pieces], axis=0)
-    step = min(512, weights_ref.shape[1])
+    step = min(2048, weights_ref.shape[1])
     for at in range(0, weights_ref.shape[1], step):
         columns = pl.ds(at, step)
         made = jnp.dot(flat, weights_ref[:, columns], preferred_element_type=jnp.float32).astype(jnp.bfloat16)

time: 50.9 us -> 50.9 us (level)
  no operation moved by 1% of the time
where the time goes in v7:
time: 50.9 us; the launch traced here: 50.7 us
  starting transfers between devices  20.1 us (39%)
  Pallas kernels  19.9 us (39%)
  waiting for transfers between devices  6.94 us (14%)
  local copies, waits for them, and re-layouts  3.38 us (7%)
    ppermute x7, starting transfers between devices, across(): lax.ppermute(value, both, joint(lambda s, m: (s ^ 2 * part ^ m % 2) * mp_...  11.1 us
    pallas_call x8, Pallas kernels, project(): pl.pallas_call(functools.partial(project_kernel, [(tile, row) for tile, r...  9.98 us
    ppermute x14, starting transfers between devices, over_mp(): return lax.ppermute(value, 'mp', [(m, m ^ flip) for m in range(mp_count)])  5.89 us
    ppermute x7, waiting for transfers between devices, across(): lax.ppermute(value, both, joint(lambda s, m: (s ^ 2 * part ^ m % 2) * mp_...  5.69 us
    pallas_call x1, Pallas kernels, attend(): pl.pallas_call(functools.partial(attend_kernel, heads, per), out_shape=ja...  5.31 us
    unnamed x5, local copies, waits for them, and re-layouts  3.28 us
    ppermute x2, starting transfers between devices, across(): return lax.ppermute(value, 'seq', [(s, s ^ 1) for s in range(seq_count)])  3.1 us
    pallas_call x2, Pallas kernels, pick(): pl.pallas_call(functools.partial(pick_kernel, plans, fetched), out_shape=...  2.9 us
  transfers between devices with their start and end apart: 23, of which 8 were waited for; matrix products, arithmetic and copies ran while one was open for 7% of the time, Pallas kernels for 26%

profile of v7, /device:TPU:0, one launch (start us, length us, event | category | flops | bytes accessed | tf_op | source)
XLA Modules:
  0.0 50.7 jit_solution(13943820931168310120)
XLA Ops:
  0.0 4.0 %collective-permute-start = (s32[2,32]{1,0:T(2,128)}, s32[2,32]{1,0:T(2,128)S(1)}, u32[]{:S(2)}, u32[]{:S(2)}) collective-permute-start(s32[2,32]{1,0:T(2,128)} %bitcast.11), channel_id=1, source_target_pairs={{0,16},{1,21},{2,18},{3,23},{4,20},{5,17},{6,22},{7,19},{8,24},{9,... | collective-permute-start | bytes 776 | tf_op jit(solution)/shard_map/ppermute | solution.py:286
  4.0 1.3 %collective-permute-start.1 = (s32[2,32]{1,0:T(2,128)}, s32[2,32]{1,0:T(2,128)S(1)}, u32[]{:S(2)}, u32[]{:S(2)}) collective-permute-start(s32[2,32]{1,0:T(2,128)} %bitcast.12), channel_id=1, source_target_pairs={{0,24},{1,29},{2,26},{3,31},{4,28},{5,25},{6,30},{7,27},{8,16},{9,... | collective-permute-start | bytes 776 | tf_op jit(solution)/shard_map/ppermute | solution.py:286
  5.6 1.5 %collective-permute-start.3 = (s32[2,32]{1,0:T(2,128)}, s32[2,32]{1,0:T(2,128)S(1)}, u32[]{:S(2)}, u32[]{:S(2)}) collective-permute-start(s32[2,32]{1,0:T(2,128)} %bitcast.14), channel_id=1, source_target_pairs={{0,4},{4,0},{8,12},{12,8},{16,20},{20,16},{24,28},{28,24},{1,5},{5... | collective-permute-start | bytes 776 | tf_op jit(solution)/shard_map/ppermute | solution.py:285
  7.1 1.5 %pick.2 = (bf16[8,16,896]{2,1,0:T(8,128)(2,1)S(1)}, bf16[32,32,896]{2,1,0:T(8,128)(2,1)S(1)}) custom-call(s32[2,32]{1,0:T(2,128)S(1)} %collective-permute-done.refs_0_, bf16[32,32,896]{2,1,0:T(8,128)(2,1)} %refs_1_.1), custom_call_target="tpu_custom_call" | custom-call | flops 1 | bytes 1 | tf_op jit(solution)/shard_map/pick/pallas_call | solution.py:102
  8.7 0.9 %collective-permute-done.1.refs_0_.refs_1_ = s32[2,32]{1,0:T(2,128)S(1)} collective-permute-done((s32[2,32]{1,0:T(2,128)}, s32[2,32]{1,0:T(2,128)S(1)}, u32[]{:S(2)}, u32[]{:S(2)}) %collective-permute-start.1) | collective-permute-done | bytes 288 | tf_op jit(solution)/shard_map/ppermute | solution.py:286
  9.6 2.6 %collective-permute-start.4 = (bf16[8,16,896]{2,1,0:T(8,128)(2,1)S(1)}, bf16[8,16,896]{2,1,0:T(8,128)(2,1)S(1)}, u32[]{:S(2)}, u32[]{:S(2)}) collective-permute-start(bf16[8,16,896]{2,1,0:T(8,128)(2,1)S(1)} %turn.7), channel_id=1, source_target_pairs={{0,16},{1,21},{2,18},{3,23},{4,20},{5,17},{6,22},{7,19},{8,24},{9,... | collective-permute-start | bytes 688136 | tf_op jit(solution)/shard_map/ppermute | solution.py:286
  12.2 1.4 %pick.3 = (bf16[8,16,896]{2,1,0:T(8,128)(2,1)S(1)}, bf16[4,32,896]{2,1,0:T(8,128)(2,1)S(1)}, bf16[4,32,896]{2,1,0:T(8,128)(2,1)S(1)}, bf16[4,32,896]{2,1,0:T(8,128)(2,1)S(1)}) custom-call(s32[2,32]{1,0:T(2,128)S(1)} %collective-permute-done.1.refs_0_.refs_1_, s32[2,32]{1,0:T(2,128)S(1)} %collective-permute-done.2.refs_1_.refs_2_, ...), custom_call_target="tpu_custom_call" | custom-call | flops 1 | bytes 1 | tf_op jit(solution)/shard_map/pick/pallas_call | solution.py:102
  13.6 1.6 %collective-permute-start.6 = (bf16[4,32,896]{2,1,0:T(8,128)(2,1)S(1)}, bf16[4,32,896]{2,1,0:T(8,128)(2,1)S(1)}, u32[]{:S(2)}, u32[]{:S(2)}) collective-permute-start(bf16[4,32,896]{2,1,0:T(8,128)(2,1)S(1)} %get-tuple-element.23), channel_id=1, source_target_pairs={{0,4},{4,0},{8,12},{12,8},{16,20},{20,16},{24,28},{28,24},{1,5},{5... | collective-permute-start | bytes 688136 | tf_op jit(solution)/shard_map/ppermute | solution.py:285
  15.2 0.7 %collective-permute-start.7 = (bf16[4,32,896]{2,1,0:T(8,128)(2,1)S(1)}, bf16[4,32,896]{2,1,0:T(8,128)(2,1)S(1)}, u32[]{:S(2)}, u32[]{:S(2)}) collective-permute-start(bf16[4,32,896]{2,1,0:T(8,128)(2,1)S(1)} %get-tuple-element.24), channel_id=1, source_target_pairs={{0,8},{1,13},{2,10},{3,15},{4,12},{5,9},{6,14},{7,11},{8,0},{9,5},... | collective-permute-start | bytes 688136 | tf_op jit(solution)/shard_map/ppermute | solution.py:286
  15.8 3.3 %copy.22 = bf16[112,8,2,1024]{3,1,2,0:T(8,128)(2,1)S(1)} copy(bf16[112,8,2,1024]{3,2,1,0:T(2,128)(2,1)} %bitcast.16) | data formatting | bytes 7340032
  19.1 1.7 %plan.1 = (s32[64]{0:T(128)S(1)}, bf16[8,32,896]{2,1,0:T(8,128)(2,1)S(1)}) custom-call(s32[2,32]{1,0:T(2,128)S(1)} %bitcast.15, bf16[32,32,896]{2,1,0:T(8,128)(2,1)S(1)} %get-tuple-element.17.stored_ref.refs_3_), custom_call_target="tpu_custom_call" | custom-call | flops 1 | bytes 1 | tf_op jit(solution)/shard_map/plan/pallas_call | solution.py:45
  20.8 1.2 %project.8.refs_2_.refs_4_ = bf16[64,32,2048]{2,1,0:T(8,128)(2,1)S(1)} custom-call(bf16[8,32,896]{2,1,0:T(8,128)(2,1)S(1)} %get-tuple-element.21.refs_0_, bf16[896,2048]{1,0:T(8,128)(2,1)S(1)} %bitcast.3), custom_call_target="tpu_custom_call" | custom-call | flops 117440512 | tf_op jit(solution)/shard_map/project/pallas_call | solution.py:162
  22.1 1.7 %collective-permute-done.4.refs_1_.refs_3_ = bf16[8,16,896]{2,1,0:T(8,128)(2,1)S(1)} collective-permute-done((bf16[8,16,896]{2,1,0:T(8,128)(2,1)S(1)}, bf16[8,16,896]{2,1,0:T(8,128)(2,1)S(1)}, u32[]{:S(2)}, u32[]{:S(2)}) %collective-permute-start.4) | collective-permute-done | bytes 229408 | tf_op jit(solution)/shard_map/ppermute | solution.py:286
  23.8 2.2 %collective-permute-start.5 = (bf16[8,16,896]{2,1,0:T(8,128)(2,1)S(1)}, bf16[8,16,896]{2,1,0:T(8,128)(2,1)S(1)}, u32[]{:S(2)}, u32[]{:S(2)}) collective-permute-start(bf16[8,16,896]{2,1,0:T(8,128)(2,1)S(1)} %turn.8.refs_4_), channel_id=1, source_target_pairs={{0,24},{1,29},{2,26},{3,31},{4,28},{5,25},{6,30},{7,27},{8,16},{9,... | collective-permute-start | bytes 688136 | tf_op jit(solution)/shard_map/ppermute | solution.py:286
  26.0 0.7 %collective-permute-done.7.refs_2_ = bf16[4,32,896]{2,1,0:T(8,128)(2,1)S(1)} collective-permute-done((bf16[4,32,896]{2,1,0:T(8,128)(2,1)S(1)}, bf16[4,32,896]{2,1,0:T(8,128)(2,1)S(1)}, u32[]{:S(2)}, u32[]{:S(2)}) %collective-permute-start.7) | collective-permute-done | bytes 229408 | tf_op jit(solution)/shard_map/ppermute | solution.py:286
  26.7 0.5 collective-permute-start.13
  27.4 0.4 collective-permute-start.11
  28.2 0.3 collective-permute-start.9
  28.6 1.5 %collective-permute-start.16 = (bf16[8,16,896]{2,1,0:T(8,128)(2,1)S(1)}, bf16[8,16,896]{2,1,0:T(8,128)(2,1)S(1)}, u32[]{:S(2)}, u32[]{:S(2)}) collective-permute-start(bf16[8,16,896]{2,1,0:T(8,128)(2,1)S(1)} %get-tuple-element.26.refs_0_), channel_id=1, source_target_pairs={{0,2},{1,3},{2,0},{3,1},{4,6},{5,7},{6,4},{7,5},{8,10},{9,11},{10,... | collective-permute-start | bytes 688136 | tf_op jit(solution)/shard_map/ppermute | solution.py:289
  30.1 1.2 %project.9.refs_4_ = bf16[64,32,2048]{2,1,0:T(8,128)(2,1)S(1)} custom-call(bf16[4,32,896]{2,1,0:T(8,128)(2,1)S(1)} %get-tuple-element.27.refs_0_, bf16[2,32,896]{2,1,0:T(8,128)(2,1)S(1)} %collective-permute-done.12.refs_1_, bf16[2,32,896]{2,1,0:T(8,128)(2,1)S(1)} %collective-permute-done.13.refs_2_, ...), custom_call_target="tpu_custom_call", output_to_operand_aliasing={{}: (4, {})} | custom-call | flops 117440512 | tf_op jit(solution)/shard_map/project/pallas_call | solution.py:162
  31.5 1.2 %project.10.refs_4_ = bf16[64,32,2048]{2,1,0:T(8,128)(2,1)S(1)} custom-call(bf16[8,16,896]{2,1,0:T(8,128)(2,1)S(1)} %get-tuple-element.26.refs_0_, bf16[4,16,896]{2,1,0:T(8,128)(2,1)S(1)} %collective-permute-done.10.refs_1_, bf16[4,16,896]{2,1,0:T(8,128)(2,1)S(1)} %collective-permute-done.11.refs_2_, ...), custom_call_target="tpu_custom_call", output_to_operand_aliasing={{}: (4, {})} | custom-call | flops 117440512 | tf_op jit(solution)/shard_map/project/pallas_call | solution.py:162
  32.8 1.2 %project.11.refs_1_.refs_4_ = bf16[64,32,2048]{2,1,0:T(8,128)(2,1)S(1)} custom-call(bf16[4,32,896]{2,1,0:T(8,128)(2,1)S(1)} %get-tuple-element.25.refs_0_, bf16[2,32,896]{2,1,0:T(8,128)(2,1)S(1)} %collective-permute-done.8.refs_1_, bf16[2,32,896]{2,1,0:T(8,128)(2,1)S(1)} %collective-permute-done.9.refs_2_, ...), custom_call_target="tpu_custom_call", output_to_operand_aliasing={{}: (4, {})} | custom-call | flops 117440512 | tf_op jit(solution)/shard_map/project/pallas_call | solution.py:162
  34.0 1.5 %collective-permute-start.14 = (bf16[8,16,896]{2,1,0:T(8,128)(2,1)S(1)}, bf16[8,16,896]{2,1,0:T(8,128)(2,1)S(1)}, u32[]{:S(2)}, u32[]{:S(2)}) collective-permute-start(bf16[8,16,896]{2,1,0:T(8,128)(2,1)S(1)} %turn.10.refs_1_.refs_0_), channel_id=1, source_target_pairs={{0,2},{1,3},{2,0},{3,1},{4,6},{5,7},{6,4},{7,5},{8,10},{9,11},{10,... | collective-permute-start | bytes 688136 | tf_op jit(solution)/shard_map/ppermute | solution.py:289
  35.5 0.8 %collective-permute-done.16.refs_0_ = bf16[8,16,896]{2,1,0:T(8,128)(2,1)S(1)} collective-permute-done((bf16[8,16,896]{2,1,0:T(8,128)(2,1)S(1)}, bf16[8,16,896]{2,1,0:T(8,128)(2,1)S(1)}, u32[]{:S(2)}, u32[]{:S(2)}) %collective-permute-start.16) | collective-permute-done | bytes 229408 | tf_op jit(solution)/shard_map/ppermute | solution.py:289
  36.4 0.5 collective-permute-start.20
  36.9 2.4 %collective-permute-done.15.refs_0_ = bf16[4,32,896]{2,1,0:T(8,128)(2,1)S(1)} collective-permute-done((bf16[4,32,896]{2,1,0:T(8,128)(2,1)S(1)}, bf16[4,32,896]{2,1,0:T(8,128)(2,1)S(1)}, u32[]{:S(2)}, u32[]{:S(2)}) %collective-permute-start.15) | collective-permute-done | bytes 229408 | tf_op jit(solution)/shard_map/ppermute | solution.py:286
  39.4 0.5 collective-permute-start.18
  39.9 1.2 %project.12.refs_4_ = bf16[64,32,2048]{2,1,0:T(8,128)(2,1)S(1)} custom-call(bf16[8,16,896]{2,1,0:T(8,128)(2,1)S(1)} %turn.11.refs_1_.refs_0_, bf16[4,16,896]{2,1,0:T(8,128)(2,1)S(1)} %collective-permute-done.19.refs_1_, bf16[4,16,896]{2,1,0:T(8,128)(2,1)S(1)} %collective-permute-done.20.refs_2_, ...), custom_call_target="tpu_custom_call", output_to_operand_aliasing={{}: (4, {})} | custom-call | flops 117440512 | tf_op jit(solution)/shard_map/project/pallas_call | solution.py:162
  41.2 1.2 %project.13.refs_1_.refs_3_ = bf16[64,32,2048]{2,1,0:T(8,128)(2,1)S(1)} custom-call(bf16[4,32,896]{2,1,0:T(8,128)(2,1)S(1)} %turn.12.refs_0_, bf16[2,32,896]{2,1,0:T(8,128)(2,1)S(1)} %collective-permute-done.17.refs_1_, bf16[2,32,896]{2,1,0:T(8,128)(2,1)S(1)} %collective-permute-done.18.refs_2_, ...), custom_call_target="tpu_custom_call", output_to_operand_aliasing={{}: (4, {})} | custom-call | flops 117440512 | tf_op jit(solution)/shard_map/project/pallas_call | solution.py:162
  42.6 1.2 %project.14.refs_3_ = bf16[64,32,2048]{2,1,0:T(8,128)(2,1)S(1)} custom-call(bf16[8,16,896]{2,1,0:T(8,128)(2,1)S(1)} %turn.10.refs_1_.refs_0_, bf16[8,16,896]{2,1,0:T(8,128)(2,1)S(1)} %collective-permute-done.22.refs_1_, bf16[896,2048]{1,0:T(8,128)(2,1)S(1)} %bitcast.9, bf16[64,32,2048]{2,1,0:T(8,128)(2,1)S(1)} %project.13.refs_1_.refs_3_), custom_call_target="tpu_custom_call", output_to_operand_aliasing={{}: (3, {})} | custom-call | flops 7516192768 | tf_op jit(solution)/shard_map/project/pallas_call | solution.py:162
  44.0 1.2 %project.15.held_ref = bf16[64,32,2048]{2,1,0:T(8,128)(2,1)S(1)} custom-call(bf16[8,16,896]{2,1,0:T(8,128)(2,1)S(1)} %turn.13.refs_0_, bf16[8,16,896]{2,1,0:T(8,128)(2,1)S(1)} %collective-permute-done.21.refs_1_, bf16[896,2048]{1,0:T(8,128)(2,1)S(1)} %bitcast.10, bf16[64,32,2048]{2,1,0:T(8,128)(2,1)S(1)} %project.14.refs_3_), custom_call_target="tpu_custom_call", output_to_operand_aliasing={{}: (3, {})} | custom-call | flops 7516192768 | tf_op jit(solution)/shard_map/project/pallas_call | solution.py:162
  45.3 5.3 %attend.1 = bf16[2048,1024]{1,0:T(8,128)(2,1)} custom-call(s32[64]{0:T(128)S(1)} %get-tuple-element.18.refs_3_.slots_ref, bf16[2048,1024]{1,0:T(8,128)(2,1)S(1)} %copy-done, bf16[64,32,2048]{2,1,0:T(8,128)(2,1)S(1)} %project.15.held_ref), custom_call_target="tpu_custom_call" | custom-call | flops 1000000000 | bytes 16777216 | tf_op jit(solution)/shard_map/attend/pallas_call | solution.py:234
  (43 shorter events, 1.5 us)
Async XLA Ops:
  0.0 19.1 %copy-start.1 = (s32[32,2]{0,1:T(2,128)S(1)}, s32[32,2]{0,1:T(2,128)}, u32[]{:S(2)}) copy-start(s32[32,2]{0,1:T(2,128)} %param.7) | copy-start | bytes 772
  0.0 7.1 %collective-permute-start = (s32[2,32]{1,0:T(2,128)}, s32[2,32]{1,0:T(2,128)S(1)}, u32[]{:S(2)}, u32[]{:S(2)}) collective-permute-start(s32[2,32]{1,0:T(2,128)} %bitcast.11), channel_id=1, source_target_pairs={{0,16},{1,21},{2,18},{3,23},{4,20},{5,17},{6,22},{7,19},{8,24},{9,... | collective-permute-start | bytes 776 | tf_op jit(solution)/shard_map/ppermute | solution.py:286
  4.0 5.6 %collective-permute-start.1 = (s32[2,32]{1,0:T(2,128)}, s32[2,32]{1,0:T(2,128)S(1)}, u32[]{:S(2)}, u32[]{:S(2)}) collective-permute-start(s32[2,32]{1,0:T(2,128)} %bitcast.12), channel_id=1, source_target_pairs={{0,24},{1,29},{2,26},{3,31},{4,28},{5,25},{6,30},{7,27},{8,16},{9,... | collective-permute-start | bytes 776 | tf_op jit(solution)/shard_map/ppermute | solution.py:286
  5.4 4.2 %collective-permute-start.2 = (s32[2,32]{1,0:T(2,128)}, s32[2,32]{1,0:T(2,128)S(1)}, u32[]{:S(2)}, u32[]{:S(2)}) collective-permute-start(s32[2,32]{1,0:T(2,128)} %bitcast.13), channel_id=1, source_target_pairs={{0,8},{1,13},{2,10},{3,15},{4,12},{5,9},{6,14},{7,11},{8,0},{9,5},... | collective-permute-start | bytes 776 | tf_op jit(solution)/shard_map/ppermute | solution.py:286
  5.6 4.0 %collective-permute-start.3 = (s32[2,32]{1,0:T(2,128)}, s32[2,32]{1,0:T(2,128)S(1)}, u32[]{:S(2)}, u32[]{:S(2)}) collective-permute-start(s32[2,32]{1,0:T(2,128)} %bitcast.14), channel_id=1, source_target_pairs={{0,4},{4,0},{8,12},{12,8},{16,20},{20,16},{24,28},{28,24},{1,5},{5... | collective-permute-start | bytes 776 | tf_op jit(solution)/shard_map/ppermute | solution.py:285
  9.6 14.1 %collective-permute-start.4 = (bf16[8,16,896]{2,1,0:T(8,128)(2,1)S(1)}, bf16[8,16,896]{2,1,0:T(8,128)(2,1)S(1)}, u32[]{:S(2)}, u32[]{:S(2)}) collective-permute-start(bf16[8,16,896]{2,1,0:T(8,128)(2,1)S(1)} %turn.7), channel_id=1, source_target_pairs={{0,16},{1,21},{2,18},{3,23},{4,20},{5,17},{6,22},{7,19},{8,24},{9,... | collective-permute-start | bytes 688136 | tf_op jit(solution)/shard_map/ppermute | solution.py:286
  13.6 12.4 %collective-permute-start.6 = (bf16[4,32,896]{2,1,0:T(8,128)(2,1)S(1)}, bf16[4,32,896]{2,1,0:T(8,128)(2,1)S(1)}, u32[]{:S(2)}, u32[]{:S(2)}) collective-permute-start(bf16[4,32,896]{2,1,0:T(8,128)(2,1)S(1)} %get-tuple-element.23), channel_id=1, source_target_pairs={{0,4},{4,0},{8,12},{12,8},{16,20},{20,16},{24,28},{28,24},{1,5},{5... | collective-permute-start | bytes 688136 | tf_op jit(solution)/shard_map/ppermute | solution.py:285
  15.2 11.5 %collective-permute-start.7 = (bf16[4,32,896]{2,1,0:T(8,128)(2,1)S(1)}, bf16[4,32,896]{2,1,0:T(8,128)(2,1)S(1)}, u32[]{:S(2)}, u32[]{:S(2)}) collective-permute-start(bf16[4,32,896]{2,1,0:T(8,128)(2,1)S(1)} %get-tuple-element.24), channel_id=1, source_target_pairs={{0,8},{1,13},{2,10},{3,15},{4,12},{5,9},{6,14},{7,11},{8,0},{9,5},... | collective-permute-start | bytes 688136 | tf_op jit(solution)/shard_map/ppermute | solution.py:286
  23.8 10.3 %collective-permute-start.5 = (bf16[8,16,896]{2,1,0:T(8,128)(2,1)S(1)}, bf16[8,16,896]{2,1,0:T(8,128)(2,1)S(1)}, u32[]{:S(2)}, u32[]{:S(2)}) collective-permute-start(bf16[8,16,896]{2,1,0:T(8,128)(2,1)S(1)} %turn.8.refs_4_), channel_id=1, source_target_pairs={{0,24},{1,29},{2,26},{3,31},{4,28},{5,25},{6,30},{7,27},{8,16},{9,... | collective-permute-start | bytes 688136 | tf_op jit(solution)/shard_map/ppermute | solution.py:286
  26.7 1.4 %collective-permute-start.12 = (bf16[2,32,896]{2,1,0:T(8,128)(2,1)S(1)}, bf16[2,32,896]{2,1,0:T(8,128)(2,1)S(1)}, u32[]{:S(2)}, u32[]{:S(2)}) collective-permute-start(bf16[2,32,896]{2,1,0:T(8,128)(2,1)S(1)} %get-tuple-element.34), channel_id=1, source_target_pairs={{0,1},{1,0},{2,3},{3,2},{4,5},{5,4},{6,7},{7,6},{8,9},{9,8},{10,11... | collective-permute-start | bytes 344072 | tf_op jit(solution)/shard_map/ppermute | solution.py:289
  26.7 1.5 %collective-permute-start.13 = (bf16[2,32,896]{2,1,0:T(8,128)(2,1)S(1)}, bf16[2,32,896]{2,1,0:T(8,128)(2,1)S(1)}, u32[]{:S(2)}, u32[]{:S(2)}) collective-permute-start(bf16[2,32,896]{2,1,0:T(8,128)(2,1)S(1)} %get-tuple-element.33), channel_id=1, source_target_pairs={{0,1},{1,0},{2,3},{3,2},{4,5},{5,4},{6,7},{7,6},{8,9},{9,8},{10,11... | collective-permute-start | bytes 344072 | tf_op jit(solution)/shard_map/ppermute | solution.py:289
  27.3 1.4 %collective-permute-start.10 = (bf16[4,16,896]{2,1,0:T(8,128)(2,1)S(1)}, bf16[4,16,896]{2,1,0:T(8,128)(2,1)S(1)}, u32[]{:S(2)}, u32[]{:S(2)}) collective-permute-start(bf16[4,16,896]{2,1,0:T(8,128)(2,1)S(1)} %get-tuple-element.36), channel_id=1, source_target_pairs={{0,1},{1,0},{2,3},{3,2},{4,5},{5,4},{6,7},{7,6},{8,9},{9,8},{10,11... | collective-permute-start | bytes 344072 | tf_op jit(solution)/shard_map/ppermute | solution.py:289
  27.4 4.0 %collective-permute-start.11 = (bf16[4,16,896]{2,1,0:T(8,128)(2,1)S(1)}, bf16[4,16,896]{2,1,0:T(8,128)(2,1)S(1)}, u32[]{:S(2)}, u32[]{:S(2)}) collective-permute-start(bf16[4,16,896]{2,1,0:T(8,128)(2,1)S(1)} %get-tuple-element.35), channel_id=1, source_target_pairs={{0,1},{1,0},{2,3},{3,2},{4,5},{5,4},{6,7},{7,6},{8,9},{9,8},{10,11... | collective-permute-start | bytes 344072 | tf_op jit(solution)/shard_map/ppermute | solution.py:289
  28.1 4.7 %collective-permute-start.8 = (bf16[2,32,896]{2,1,0:T(8,128)(2,1)S(1)}, bf16[2,32,896]{2,1,0:T(8,128)(2,1)S(1)}, u32[]{:S(2)}, u32[]{:S(2)}) collective-permute-start(bf16[2,32,896]{2,1,0:T(8,128)(2,1)S(1)} %get-tuple-element.38), channel_id=1, source_target_pairs={{0,1},{1,0},{2,3},{3,2},{4,5},{5,4},{6,7},{7,6},{8,9},{9,8},{10,11... | collective-permute-start | bytes 344072 | tf_op jit(solution)/shard_map/ppermute | solution.py:289
  28.2 4.5 %collective-permute-start.9 = (bf16[2,32,896]{2,1,0:T(8,128)(2,1)S(1)}, bf16[2,32,896]{2,1,0:T(8,128)(2,1)S(1)}, u32[]{:S(2)}, u32[]{:S(2)}) collective-permute-start(bf16[2,32,896]{2,1,0:T(8,128)(2,1)S(1)} %get-tuple-element.37), channel_id=1, source_target_pairs={{0,1},{1,0},{2,3},{3,2},{4,5},{5,4},{6,7},{7,6},{8,9},{9,8},{10,11... | collective-permute-start | bytes 344072 | tf_op jit(solution)/shard_map/ppermute | solution.py:289
  28.6 7.7 %collective-permute-start.16 = (bf16[8,16,896]{2,1,0:T(8,128)(2,1)S(1)}, bf16[8,16,896]{2,1,0:T(8,128)(2,1)S(1)}, u32[]{:S(2)}, u32[]{:S(2)}) collective-permute-start(bf16[8,16,896]{2,1,0:T(8,128)(2,1)S(1)} %get-tuple-element.26.refs_0_), channel_id=1, source_target_pairs={{0,2},{1,3},{2,0},{3,1},{4,6},{5,7},{6,4},{7,5},{8,10},{9,11},{10,... | collective-permute-start | bytes 688136 | tf_op jit(solution)/shard_map/ppermute | solution.py:289
  31.4 7.9 %collective-permute-start.15 = (bf16[4,32,896]{2,1,0:T(8,128)(2,1)S(1)}, bf16[4,32,896]{2,1,0:T(8,128)(2,1)S(1)}, u32[]{:S(2)}, u32[]{:S(2)}) collective-permute-start(bf16[4,32,896]{2,1,0:T(8,128)(2,1)S(1)} %get-tuple-element.28), channel_id=1, source_target_pairs={{0,8},{1,13},{2,10},{3,15},{4,12},{5,9},{6,14},{7,11},{8,0},{9,5},... | collective-permute-start | bytes 688136 | tf_op jit(solution)/shard_map/ppermute | solution.py:286
  34.0 5.3 %copy-start = (bf16[2048,1024]{1,0:T(8,128)(2,1)S(1)}, bf16[2048,1024]{1,0:T(8,128)(2,1)}, u32[]{:S(2)}) copy-start(bf16[2048,1024]{1,0:T(8,128)(2,1)} %queries_ref.1) | copy-start | bytes 12582916
  34.0 8.4 %collective-permute-start.14 = (bf16[8,16,896]{2,1,0:T(8,128)(2,1)S(1)}, bf16[8,16,896]{2,1,0:T(8,128)(2,1)S(1)}, u32[]{:S(2)}, u32[]{:S(2)}) collective-permute-start(bf16[8,16,896]{2,1,0:T(8,128)(2,1)S(1)} %turn.10.refs_1_.refs_0_), channel_id=1, source_target_pairs={{0,2},{1,3},{2,0},{3,1},{4,6},{5,7},{6,4},{7,5},{8,10},{9,11},{10,... | collective-permute-start | bytes 688136 | tf_op jit(solution)/shard_map/ppermute | solution.py:289
  35.5 7.1 %collective-permute-start.22 = (bf16[8,16,896]{2,1,0:T(8,128)(2,1)S(1)}, bf16[8,16,896]{2,1,0:T(8,128)(2,1)S(1)}, u32[]{:S(2)}, u32[]{:S(2)}) collective-permute-start(bf16[8,16,896]{2,1,0:T(8,128)(2,1)S(1)} %turn.10.refs_1_.refs_0_), channel_id=1, source_target_pairs={{0,1},{1,0},{2,3},{3,2},{4,5},{5,4},{6,7},{7,6},{8,9},{9,8},{10,11... | collective-permute-start | bytes 688136 | tf_op jit(solution)/shard_map/ppermute | solution.py:289
  36.3 3.1 %collective-permute-start.19 = (bf16[4,16,896]{2,1,0:T(8,128)(2,1)S(1)}, bf16[4,16,896]{2,1,0:T(8,128)(2,1)S(1)}, u32[]{:S(2)}, u32[]{:S(2)}) collective-permute-start(bf16[4,16,896]{2,1,0:T(8,128)(2,1)S(1)} %get-tuple-element.30), channel_id=1, source_target_pairs={{0,1},{1,0},{2,3},{3,2},{4,5},{5,4},{6,7},{7,6},{8,9},{9,8},{10,11... | collective-permute-start | bytes 344072 | tf_op jit(solution)/shard_map/ppermute | solution.py:289
  36.4 3.5 %collective-permute-start.20 = (bf16[4,16,896]{2,1,0:T(8,128)(2,1)S(1)}, bf16[4,16,896]{2,1,0:T(8,128)(2,1)S(1)}, u32[]{:S(2)}, u32[]{:S(2)}) collective-permute-start(bf16[4,16,896]{2,1,0:T(8,128)(2,1)S(1)} %get-tuple-element.29), channel_id=1, source_target_pairs={{0,1},{1,0},{2,3},{3,2},{4,5},{5,4},{6,7},{7,6},{8,9},{9,8},{10,11... | collective-permute-start | bytes 344072 | tf_op jit(solution)/shard_map/ppermute | solution.py:289
  39.3 1.8 %collective-permute-start.17 = (bf16[2,32,896]{2,1,0:T(8,128)(2,1)S(1)}, bf16[2,32,896]{2,1,0:T(8,128)(2,1)S(1)}, u32[]{:S(2)}, u32[]{:S(2)}) collective-permute-start(bf16[2,32,896]{2,1,0:T(8,128)(2,1)S(1)} %get-tuple-element.32), channel_id=1, source_target_pairs={{0,1},{1,0},{2,3},{3,2},{4,5},{5,4},{6,7},{7,6},{8,9},{9,8},{10,11... | collective-permute-start | bytes 344072 | tf_op jit(solution)/shard_map/ppermute | solution.py:289
  39.4 1.8 %collective-permute-start.18 = (bf16[2,32,896]{2,1,0:T(8,128)(2,1)S(1)}, bf16[2,32,896]{2,1,0:T(8,128)(2,1)S(1)}, u32[]{:S(2)}, u32[]{:S(2)}) collective-permute-start(bf16[2,32,896]{2,1,0:T(8,128)(2,1)S(1)} %get-tuple-element.31), channel_id=1, source_target_pairs={{0,1},{1,0},{2,3},{3,2},{4,5},{5,4},{6,7},{7,6},{8,9},{9,8},{10,11... | collective-permute-start | bytes 344072 | tf_op jit(solution)/shard_map/ppermute | solution.py:289
  42.5 1.6 %collective-permute-start.21 = (bf16[8,16,896]{2,1,0:T(8,128)(2,1)S(1)}, bf16[8,16,896]{2,1,0:T(8,128)(2,1)S(1)}, u32[]{:S(2)}, u32[]{:S(2)}) collective-permute-start(bf16[8,16,896]{2,1,0:T(8,128)(2,1)S(1)} %turn.13.refs_0_), channel_id=1, source_target_pairs={{0,1},{1,0},{2,3},{3,2},{4,5},{5,4},{6,7},{7,6},{8,9},{9,8},{10,11... | collective-permute-start | bytes 688136 | tf_op jit(solution)/shard_map/ppermute | solution.py:289
